TPU v7x, 256 devices: a whole 4x4x8 slice. The times are simulated.
256 devices in a mesh: row: 16 (over z, core), col: 16 (over y, x).
Axes of the slice: x: 4, y: 4, z: 8, core: 2. Of those that a mesh axis runs over, the one named last changes fastest.
Arguments:
- gen_points: bfloat16 [8192, 512], P(('row', 'col')), may hold values from -8 to 8
- data_points: bfloat16 [16384, 512], P('col', 'row'), may hold values from -8 to 8
- data_potential: float32 [16384], P('col'), may hold values from -3 to 3
Outputs:
- gen_potential: float32 [8192], P('row')
- data_potential_out: float32 [16384], P('col')
- transport_target: float32 [512, 8192], P('col', 'row')
All inputs are finite; a program needn't handle non-finite values.
Results may differ from a plain program's by a relative error of at most 0.0003.
Values may be sent and summed in bfloat16 or wider, within the bound.
No kernel may reach another device: no remote copies, remote signals or barrier semaphores. Data moves between devices by JAX's collectives and lax.ppermute only.
A program may use at most 64 MiB of HBM per device.

v0:
```python
import math

import jax
import jax.numpy as jnp
from jax import lax
from jax.sharding import PartitionSpec as P

ITERS = 2


EPS = 0.05


def merged(shard, axis, combine):
    everything = jax.tree.map(lambda part: lax.all_gather(part, axis), shard)
    first = jax.tree.map(lambda part: part[0], everything)

    def step(k, so_far):
        return combine(so_far, jax.tree.map(lambda part: part[k], everything))

    return lax.fori_loop(1, lax.axis_size(axis), step, first)


def pair_combine(first, second):
    top = jnp.maximum(first[0], second[0])
    return (top, first[1] * jnp.exp(first[0] - top) + second[1] * jnp.exp(second[0] - top))


def row_scores(tile, potential):
    return (potential[None, :] - tile) / EPS


def row_pass(cost, potential, block):
    gen_rows, data_cols = cost.shape
    tiles = cost.reshape(gen_rows // block, block, data_cols)

    def one_block(tile):
        scores = row_scores(tile, potential)
        largest = jnp.max(scores, axis=1)
        return (largest, jnp.sum(jnp.exp(scores - largest[:, None]), axis=1))

    largest, total = lax.map(one_block, tiles)
    return (largest.reshape(gen_rows), total.reshape(gen_rows))


def col_pass(cost, potential, block):
    gen_rows, data_cols = cost.shape
    tiles = cost.reshape(gen_rows // block, block, data_cols)
    pot_blocks = potential.reshape(gen_rows // block, block)

    def step(carry, pieces):
        largest, total = carry
        tile, pot_block = pieces
        scores = (pot_block[:, None] - tile) / EPS
        fresh = jnp.maximum(largest, jnp.max(scores, axis=0))
        total = total * jnp.exp(largest - fresh) + jnp.sum(jnp.exp(scores - fresh[None, :]), axis=0)
        return ((fresh, total), None)

    start = (jnp.full((data_cols,), -jnp.inf, jnp.float32), jnp.zeros((data_cols,), jnp.float32))
    (largest, total), _ = lax.scan(step, start, (tiles, pot_blocks))
    return (largest, total)


def row_statistics(cost, potential, block):
    largest, total = row_pass(cost, potential, block)
    largest, total = merged((largest, total), "col", pair_combine)
    return (largest, total)


def col_statistics(cost, potential, block):
    largest, total = col_pass(cost, potential, block)
    largest, total = merged((largest, total), "row", pair_combine)
    return (largest, total)


def local(gen_points, data_points, data_potential):
    features = gen_points.shape[1]
    data_cols = data_points.shape[0]
    gen_rows = gen_points.shape[0] * lax.axis_size("col")
    gen_count = gen_rows * lax.axis_size("row")
    data_count = data_cols * lax.axis_size("col")
    block = min(512, gen_rows)
    data_full = lax.all_gather(data_points, "row", axis=1, tiled=True)
    data_f32 = data_full.astype(jnp.float32)
    data_sq = jnp.sum(data_f32 * data_f32, axis=1)
    piece = lax.all_gather(gen_points, "col", axis=0, tiled=True)
    piece_f32 = piece.astype(jnp.float32)
    gen_sq = jnp.sum(piece_f32 * piece_f32, axis=1)
    cross = lax.dot_general(
        piece, data_full, (((1,), (1,)), ((), ())), preferred_element_type=jnp.float32
    )
    cost = (gen_sq[:, None] + data_sq[None, :] - 2.0 * cross) / features
    potential = data_potential
    for step in range(ITERS):
        largest, total = row_statistics(cost, potential, block)
        gen_pot = -EPS * (largest + jnp.log(total)) + EPS * math.log(data_count)
        col_top, col_total = col_statistics(cost, gen_pot, block)
        potential = -EPS * (col_top + jnp.log(col_total)) + EPS * math.log(gen_count)
    largest, total = row_statistics(cost, potential, block)
    gen_pot = -EPS * (largest + jnp.log(total)) + EPS * math.log(data_count)

    def weight_block(pieces):
        tile, top_block, total_block = pieces
        scores = row_scores(tile, potential)
        return jnp.exp(scores - top_block[:, None]) / total_block[:, None]

    weights = lax.map(
        weight_block,
        (
            cost.reshape(gen_rows // block, block, data_cols),
            largest.reshape(gen_rows // block, block),
            total.reshape(gen_rows // block, block),
        ),
    )
    weights = weights.reshape(gen_rows, data_cols)
    target = lax.psum_scatter(
        lax.dot_general(
            data_f32,
            weights,
            (((0,), (1,)), ((), ())),
            precision=lax.Precision.HIGHEST,
            preferred_element_type=jnp.float32,
        ),
        "col",
        scatter_dimension=0,
        tiled=True,
    )
    return (gen_pot, potential, target)


def solution(mesh):
    placed = (P(("row", "col"), None), P("col", "row"), P("col"))
    return jax.shard_map(
        local,
        mesh=mesh,
        in_specs=placed,
        out_specs=(P("row"), P("col"), P("col", "row")),
        check_vma=False,
    )
```

profile of v0, /device:TPU:1, one launch (start us, length us, event | category | flops | bytes accessed | tf_op | source)
XLA Modules:
  0.0 345.4 jit_solution(7788803930866131647)
XLA Ops:
  7.2 0.0 copy-start.2
  7.2 0.0 all-gather.18.cloned.1.call-start
  7.2 0.7 all-gather.18.cloned.1.call-update
  7.9 0.0 reduce-scatter.4.cloned.1.call-start
  8.0 20.0 %all_gather.44 = bf16[512,512]{1,0:T(8,128)(2,1)S(1)} all-gather(bf16[32,512]{1,0:T(8,128)(2,1)} %param.13), channel_id=1, replica_groups=mesh['row'=16,'col'=16] {'col'}, dimensions={0}, use_global_device_ids=true | all-gather | bytes 557056 | tf_op jit(solution)/shard_map/all_gather | solution.py:86
  28.0 0.2 multiply_reduce_fusion.1
  28.2 24.4 %all-gather.18.cloned.1.call-done = bf16[1024,512]{0,1:T(8,128)(2,1)} async-done(((bf16[1024,32]{0,1:T(8,128)(2,1)}), bf16[1024,512]{0,1:T(8,128)(2,1)}) %all-gather.18.cloned.1.call-update) | async-done | bytes 1048592 | tf_op jit(solution)/shard_map/all_gather | solution.py:83
  52.6 1.5 multiply_reduce_fusion
  54.0 0.0 copy-done.2
  54.1 2.2 fusion.4
  56.3 0.6 exponential_reduce_fusion.4
  56.8 17.9 %all-gather.9 = f32[16,1,512]{2,1,0:T(1,128)S(1)} all-gather(f32[1,1,512]{2,1,0:T(1,128)S(1)} %bitcast.108), channel_id=3, replica_groups=mesh['row'=16,'col'=16] {'col'}, dimensions={0}, use_global_device_ids=true | all-gather | bytes 34816 | tf_op jit(solution)/shard_map/all_gather | solution.py:15
  74.7 17.1 %all-gather.8 = f32[16,1,512]{2,1,0:T(1,128)S(1)} all-gather(f32[1,1,512]{2,1,0:T(1,128)S(1)} %bitcast.106), channel_id=2, replica_groups=mesh['row'=16,'col'=16] {'col'}, dimensions={0}, use_global_device_ids=true | all-gather | bytes 34816 | tf_op jit(solution)/shard_map/all_gather | solution.py:15
  91.8 0.9 while.55
  92.7 0.3 fusion.5
  93.0 0.5 exponential_reduce_fusion.3
  93.5 26.8 %all-gather.10 = f32[16,1,1024]{2,1,0:T(1,128)S(1)} all-gather(f32[1,1,1024]{2,1,0:T(1,128)S(1)} %bitcast.104), channel_id=1, replica_groups=mesh['row'=16,'col'=16] {'row'}, dimensions={0}, use_global_device_ids=true | all-gather | bytes 69632 | tf_op jit(solution)/shard_map/all_gather | solution.py:15
  120.4 14.9 %all-gather.2 = f32[16384]{0:T(1024)S(1)} all-gather(f32[1024]{0:T(1024)S(1)} %fusion.5), channel_id=4, replica_groups=mesh['row'=16,'col'=16] {'row'}, dimensions={0}, use_global_device_ids=true | all-gather | bytes 69632 | tf_op jit(solution)/shard_map/all_gather | solution.py:15
  135.3 0.9 while.56
  136.2 0.3 fusion.6
  136.5 0.6 exponential_reduce_fusion.2
  137.0 15.5 %all-gather.11 = f32[16,1,512]{2,1,0:T(1,128)S(1)} all-gather(f32[1,1,512]{2,1,0:T(1,128)S(1)} %bitcast.103), channel_id=5, replica_groups=mesh['row'=16,'col'=16] {'col'}, dimensions={0}, use_global_device_ids=true | all-gather | bytes 34816 | tf_op jit(solution)/shard_map/all_gather | solution.py:15
  152.6 17.2 %all-gather.12 = f32[16,1,512]{2,1,0:T(1,128)S(1)} all-gather(f32[1,1,512]{2,1,0:T(1,128)S(1)} %bitcast.107), channel_id=6, replica_groups=mesh['row'=16,'col'=16] {'col'}, dimensions={0}, use_global_device_ids=true | all-gather | bytes 34816 | tf_op jit(solution)/shard_map/all_gather | solution.py:15
  169.8 0.9 while.57
  170.7 0.3 fusion.7
  171.0 0.5 exponential_reduce_fusion.1
  171.5 27.4 %all-gather.13 = f32[16,1,1024]{2,1,0:T(1,128)S(1)} all-gather(f32[1,1,1024]{2,1,0:T(1,128)S(1)} %bitcast.105), channel_id=1, replica_groups=mesh['row'=16,'col'=16] {'row'}, dimensions={0}, use_global_device_ids=true | all-gather | bytes 69632 | tf_op jit(solution)/shard_map/all_gather | solution.py:15
  198.9 14.6 %all-gather.5 = f32[16384]{0:T(1024)S(1)} all-gather(f32[1024]{0:T(1024)S(1)} %fusion.7), channel_id=7, replica_groups=mesh['row'=16,'col'=16] {'row'}, dimensions={0}, use_global_device_ids=true | all-gather | bytes 69632 | tf_op jit(solution)/shard_map/all_gather | solution.py:15
  213.5 0.9 while.58
  214.5 0.0 copy-start.1
  214.5 0.0 copy-start
  214.5 0.3 fusion.8
  214.8 0.6 exponential_reduce_fusion
  215.3 15.6 %all-gather.15 = f32[16,1,512]{2,1,0:T(1,128)S(1)} all-gather(f32[1,1,512]{2,1,0:T(1,128)S(1)} %bitcast.109), channel_id=9, replica_groups=mesh['row'=16,'col'=16] {'col'}, dimensions={0}, use_global_device_ids=true | all-gather | bytes 34816 | tf_op jit(solution)/shard_map/all_gather | solution.py:15
  230.9 17.1 %all-gather.14 = f32[16,1,512]{2,1,0:T(1,128)S(1)} all-gather(f32[1,1,512]{2,1,0:T(1,128)S(1)} %bitcast.102), channel_id=8, replica_groups=mesh['row'=16,'col'=16] {'col'}, dimensions={0}, use_global_device_ids=true | all-gather | bytes 34816 | tf_op jit(solution)/shard_map/all_gather | solution.py:15
  248.1 0.9 while.118
  249.0 0.0 copy-done.1
  249.0 0.0 copy-done
  249.0 3.2 fusion.9
  252.2 2.6 copy.8
  254.8 0.0 reduce-scatter.4.cloned.1.call-update
  254.8 0.6 multiply_add_fusion.9
  255.4 83.2 %reduce-scatter.4.cloned.1.call-done = f32[32,512]{1,0:T(8,128)} async-done(((f32[512,512]{1,0:T(8,128)}), f32[32,512]{1,0:T(8,128)}) %reduce-scatter.4.cloned.1.call-update) | async-done | bytes 65552
  (176 shorter events, 2.4 us)
Async XLA Ops:
  7.2 46.9 %copy-start.2 = (f32[1024]{0:T(1024)S(1)}, f32[1024]{0:T(1024)}, u32[]{:S(2)}) copy-start(f32[1024]{0:T(1024)} %param.15) | copy-start | bytes 12292
  7.2 45.4 %all-gather.18.cloned.1.call-start = ((), (), s32[]{:S(2)}) async-start(), calls=%async_computation.1 | async-start | bytes 1114112 | tf_op jit(solution)/shard_map/all_gather | solution.py:83
  7.9 330.7 %reduce-scatter.4.cloned.1.call-start = ((), (), s32[]{:S(2)}) async-start(), calls=%async_computation.2 | async-start | bytes 1114112
  214.5 34.5 %copy-start.1 = (f32[1024]{0:T(1024)}, f32[1024]{0:T(1024)S(1)}, u32[]{:S(2)}) copy-start(f32[1024]{0:T(1024)S(1)} %multiply_add_fusion.7) | copy-start | bytes 12292
  214.5 34.5 %copy-start = (bf16[1024,512]{0,1:T(8,128)(2,1)S(1)}, bf16[1024,512]{0,1:T(8,128)(2,1)}, u32[]{:S(2)}) copy-start(bf16[1024,512]{0,1:T(8,128)(2,1)} %all-gather.18.cloned.1.call-done) | copy-start | bytes 3145732
Sparse Core Ops, SparseCore 0:
  9.8 42.6 all-gather.17
  254.9 83.6 reduce-scatter.3
where the time goes:
time: 346 us; the launch traced here: 345 us
  blocking collectives  204 us (59%)
  waiting for transfers between devices  108 us (31%)
  between operations  14.3 us (4%)
  other arithmetic  7.39 us (2%)
  matrix products  5.4 us (2%)
  local copies, waits for them, and re-layouts  3.7 us (1%)
    all_gather x10, blocking collectives, merged(): everything = jax.tree.map(lambda part: lax.all_gather(part, axis), shard)  184 us
    unnamed x3, waiting for transfers between devices  83.9 us
    all_gather x1, waiting for transfers between devices, local(): data_full = lax.all_gather(data_points, 'row', axis=1, tiled=True)  24.4 us
    all_gather x1, blocking collectives, local(): piece = lax.all_gather(gen_points, 'col', axis=0, tiled=True)  20 us
  transfers between devices with their start and end apart: 2, of which 2 were waited for; matrix products, arithmetic and copies ran while one was open for 0% of the time, Pallas kernels for 0%

commit v1 on v0

v1 whole, which is shorter than its diff:
```python
import math

import jax
import jax.numpy as jnp
from jax import lax
from jax.experimental import pallas as pl
from jax.experimental.pallas import tpu as pltpu
from jax.sharding import PartitionSpec as P

ITERS = 2
EPS = 0.05
LN2 = math.log(2.0)
SCALE = 1.0 / (EPS * LN2)
LANES = 128


def vmem():
    return pl.BlockSpec(memory_space=pltpu.VMEM)


def params():
    return pltpu.CompilerParams(vmem_limit_bytes=40 * 1024 * 1024)


def in_vmem(array):
    return pltpu.with_memory_space_constraint(array, pltpu.VMEM)


def kernel_call(body, out_shape, args, scratch=()):
    return pl.pallas_call(
        body,
        out_shape=out_shape,
        in_specs=[vmem() for _ in args],
        out_specs=jax.tree.map(lambda _: vmem(), out_shape),
        scratch_shapes=list(scratch),
        compiler_params=params(),
    )(*args)


def log_sum(parts):
    top = jnp.max(parts, axis=0)
    return top + jnp.log2(jnp.sum(jnp.exp2(parts - top[None]), axis=0))


def lanes_to_rows(chunk):
    return jnp.broadcast_to(chunk, (LANES, LANES)).T


def rows_to_lanes(column):
    return jnp.broadcast_to(column, (LANES, LANES)).T[0:1, :]


def row_lse_into(out_ref, affinity_ref, potential, gen_rows):
    for n in range(gen_rows // LANES):
        tile = affinity_ref[n * LANES : (n + 1) * LANES, :] + potential
        top = jnp.max(tile, axis=1, keepdims=True)
        total = jnp.sum(jnp.exp2(tile - top), axis=1, keepdims=True)
        line = rows_to_lanes(top + jnp.log2(total))
        out_ref[:, n : n + 1, :] = jnp.broadcast_to(line[None], (out_ref.shape[0], 1, LANES))


def chunks_to_line(chunks):
    return jnp.concatenate([chunks[n : n + 1, :] for n in range(chunks.shape[0])], axis=1)


def build_kernel(gen_ref, own_ref, other_ref, pot_ref, affinity_ref, out_ref):
    gen_rows, features = gen_ref.shape
    half = own_ref.shape[1]
    gen = gen_ref[...]
    gen_f32 = gen.astype(jnp.float32)
    gen_sq = jnp.sum(gen_f32 * gen_f32, axis=1, keepdims=True)
    for part, data_ref in enumerate((own_ref, other_ref)):
        data = data_ref[...]
        data_f32 = data.astype(jnp.float32)
        data_sq = jnp.sum(data_f32 * data_f32, axis=0, keepdims=True)
        cross = jnp.dot(gen, data, preferred_element_type=jnp.float32)
        affinity_ref[:, part * half : (part + 1) * half] = (2.0 * cross - (gen_sq + data_sq)) * (SCALE / features)
    potential = chunks_to_line(pot_ref[...])
    row_lse_into(out_ref, affinity_ref, potential, gen_rows)


def col_kernel(log_data, affinity_ref, got_ref, swap_ref, out_ref):
    gen_rows, data_cols = affinity_ref.shape
    row_log = log_sum(got_ref[...])
    top = jnp.full((8, data_cols), -jnp.inf, jnp.float32)
    for n in range(gen_rows // LANES):
        pot = log_data - lanes_to_rows(row_log[n : n + 1, :])
        pot = jnp.concatenate([pot] * (data_cols // LANES), axis=1)
        tile = affinity_ref[n * LANES : (n + 1) * LANES, :] + pot
        top = jnp.maximum(top, jnp.max(tile.reshape(LANES // 8, 8, data_cols), axis=0))
    top = jnp.max(top, axis=0, keepdims=True)
    total = jnp.zeros((8, data_cols), jnp.float32)
    for n in range(gen_rows // LANES):
        pot = log_data - lanes_to_rows(row_log[n : n + 1, :])
        pot = jnp.concatenate([pot] * (data_cols // LANES), axis=1)
        tile = affinity_ref[n * LANES : (n + 1) * LANES, :] + pot
        total = total + jnp.sum(jnp.exp2(tile - top).reshape(LANES // 8, 8, data_cols), axis=0)
    line = top + jnp.log2(jnp.sum(total, axis=0, keepdims=True))
    chunks = jnp.concatenate([line[:, n * LANES : (n + 1) * LANES] for n in range(data_cols // LANES)], axis=0)
    half = chunks.shape[0] // 2
    swapped = jnp.concatenate([chunks[half:], chunks[:half]], axis=0)
    chunks = jnp.where(swap_ref[...] > 0.0, swapped, chunks)
    out_ref[...] = jnp.broadcast_to(chunks[None], out_ref.shape)


def col_potential(got_ref, swap_ref, log_gen):
    chunks = log_gen - log_sum(got_ref[...])
    half = chunks.shape[0] // 2
    swapped = jnp.concatenate([chunks[half:], chunks[:half]], axis=0)
    return chunks, jnp.where(swap_ref[...] > 0.0, swapped, chunks)


def row_kernel(log_gen, affinity_ref, got_ref, swap_ref, out_ref):
    _, pot = col_potential(got_ref, swap_ref, log_gen)
    row_lse_into(out_ref, affinity_ref, chunks_to_line(pot), affinity_ref.shape[0])


def target_kernel(log_gen, affinity_ref, got_ref, swap_ref, own_ref, other_ref, pot_ref, out_ref, high, low):
    gen_rows, data_cols = affinity_ref.shape
    half = own_ref.shape[1]
    receivers = out_ref.shape[0]
    chunks = gen_rows // LANES
    feats = own_ref.shape[0] // receivers
    canonical, pot = col_potential(got_ref, swap_ref, log_gen)
    pot_ref[...] = canonical * (1.0 / SCALE)
    potential = chunks_to_line(pot)
    for n in range(chunks):
        rows = slice(n * LANES, (n + 1) * LANES)
        tile = affinity_ref[rows, :] + potential
        top = jnp.max(tile, axis=1, keepdims=True)
        weights = jnp.exp2(tile - top)
        total = jnp.sum(weights, axis=1, keepdims=True)
        upper = weights.astype(jnp.bfloat16)
        high[rows, :] = upper
        low[rows, :] = (weights - upper.astype(jnp.float32)).astype(jnp.bfloat16)
        base = chunks * feats
        for place, column in ((base + n, top), (base + chunks + n, total)):
            out_ref[:, place : place + 1, :] = jnp.broadcast_to(rows_to_lanes(column)[None], (receivers, 1, LANES))
    dims = (((1,), (1,)), ((), ()))
    for n in range(chunks):
        rows = slice(n * LANES, (n + 1) * LANES)
        sums = jnp.zeros((own_ref.shape[0], LANES), jnp.float32)
        for part, data_ref in enumerate((own_ref, other_ref)):
            cols = slice(part * half, (part + 1) * half)
            for piece in (high, low):
                sums = sums + lax.dot_general(data_ref[...], piece[rows, cols], dims, preferred_element_type=jnp.float32)
        out_ref[:, n * feats : (n + 1) * feats, :] = sums.reshape(receivers, feats, LANES)


def merge_kernel(log_data, got_ref, gen_pot_ref, target_ref):
    feats = target_ref.shape[0]
    chunks = target_ref.shape[1] // LANES
    base = chunks * feats
    tops = got_ref[:, base : base + chunks, :]
    totals = got_ref[:, base + chunks : base + 2 * chunks, :]
    top = jnp.max(tops, axis=0)
    factors = jnp.exp2(tops - top[None])
    total = jnp.sum(factors * totals, axis=0)
    gen_pot_ref[...] = (log_data - (top + jnp.log2(total))) * (1.0 / SCALE)
    factors = factors / total[None]
    for n in range(chunks):
        piece = got_ref[:, n * feats : (n + 1) * feats, :]
        target_ref[:, n * LANES : (n + 1) * LANES] = jnp.sum(piece * factors[:, n : n + 1, :], axis=0)


def local(gen_points, data_points, data_potential):
    f32 = jnp.float32
    rows_n, cols_n = lax.axis_size("row"), lax.axis_size("col")
    gen_rows = gen_points.shape[0] * cols_n
    data_cols = data_points.shape[0]
    features = gen_points.shape[1]
    log_data = math.log2(data_cols * cols_n)
    log_gen = math.log2(gen_rows * rows_n)
    half = data_cols // 2
    gen_chunks, data_chunks = gen_rows // LANES, data_cols // LANES

    core = lax.axis_index("row") % 2
    pieces = data_points.T.reshape(data_points.shape[1], 2, half).transpose(1, 0, 2)
    outgoing = jnp.broadcast_to(pieces[None], (rows_n // 2,) + pieces.shape).reshape((rows_n,) + pieces.shape[1:])
    own = lax.all_to_all(outgoing, "row", 0, 0).reshape(features, half)
    gen = lax.all_to_all(jnp.broadcast_to(gen_points[None], (cols_n,) + gen_points.shape), "col", 0, 0)
    gen = gen.reshape(gen_rows, features)
    other = lax.ppermute(own, "row", [(i, i ^ 1) for i in range(rows_n)])

    swap = jnp.broadcast_to(core.astype(f32), (data_chunks, LANES))
    start = (data_potential * SCALE).reshape(2, data_chunks // 2, LANES)
    start = jnp.where(core == 1, start[::-1], start).reshape(data_chunks, LANES)

    row_out = jax.ShapeDtypeStruct((cols_n, gen_chunks, LANES), f32)
    col_out = jax.ShapeDtypeStruct((rows_n, data_chunks, LANES), f32)

    def at(body, number):
        return lambda *refs: body(number, *refs)

    affinity, lines = kernel_call(
        build_kernel,
        (pltpu.VMEM((gen_rows, data_cols), f32), row_out),
        (gen, own, other, start),
    )
    affinity = in_vmem(affinity)
    for step in range(ITERS):
        got = lax.all_to_all(lines, "col", 0, 0)
        lines = kernel_call(at(col_kernel, log_data), col_out, (affinity, got, swap))
        got = lax.all_to_all(lines, "row", 0, 0)
        if step < ITERS - 1:
            lines = kernel_call(at(row_kernel, log_gen), row_out, (affinity, got, swap))
    feats = features // cols_n
    potential, lines = kernel_call(
        at(target_kernel, log_gen),
        (
            jax.ShapeDtypeStruct((data_chunks, LANES), f32),
            jax.ShapeDtypeStruct((cols_n, gen_chunks * (feats + 2), LANES), f32),
        ),
        (affinity, got, swap, own, other),
        scratch=[pltpu.VMEM((gen_rows, data_cols), jnp.bfloat16)] * 2,
    )
    got = lax.all_to_all(lines, "col", 0, 0)
    gen_pot, target = kernel_call(
        at(merge_kernel, log_data),
        (
            jax.ShapeDtypeStruct((gen_chunks, LANES), f32),
            jax.ShapeDtypeStruct((feats, gen_rows), f32),
        ),
        (got,),
    )
    return (gen_pot.reshape(gen_rows), potential.reshape(data_cols), target)


def solution(mesh):
    placed = (P(("row", "col"), None), P("col", "row"), P("col"))
    return jax.shard_map(
        local,
        mesh=mesh,
        in_specs=placed,
        out_specs=(P("row"), P("col"), P("col", "row")),
        check_vma=False,
    )
```

time: 346 us -> 121 us (0.35)
  blocking collectives: 204 us -> 81.7 us
  waiting for transfers between devices: 108 us -> 17 us
  between operations: 14.3 us -> 0.75 us
  starting transfers between devices: 0.08 us -> 10.3 us
  Pallas kernels: 0 us -> 7.6 us
  other arithmetic: 7.39 us -> 0.01 us
  matrix products: 5.4 us -> 0 us
    all_gather x11 -> x0, blocking collectives: 204 us -> none  [the longest x10 184 us: merged(): everything = jax.tree.map(lambda part: lax.all_gather(part, axis), shard)]
    unnamed x3 -> x0, waiting for transfers between devices: 83.9 us -> none
    all_to_all x0 -> x5, blocking collectives: none -> 81.7 us  [the longest x2 29.3 us: local(): got = lax.all_to_all(lines, 'col', 0, 0)]
    all_gather x1 -> x0, waiting for transfers between devices: 24.4 us -> none  [local(): data_full = lax.all_gather(data_points, 'row', axis=1, tiled=True)]
    all_to_all x0 -> x2, waiting for transfers between devices: none -> 17 us  [the longest x1 10.5 us: local(): lax.all_to_all(jnp.broadcast_to(gen_points[None], (cols_n,) + gen_points....]
    all_to_all x0 -> x2, starting transfers between devices: none -> 10.3 us  [the longest x1 6.75 us: local(): lax.all_to_all(jnp.broadcast_to(gen_points[None], (cols_n,) + gen_points....]
    pallas_call x0 -> x6, Pallas kernels: none -> 7.6 us  [kernel_call(): pl.pallas_call(body, out_shape=out_shape, in_specs=[vmem() for _ in args]...]
    dot_general x2 -> x0, matrix products: 5.4 us -> none  [the longest x1 3.19 us: local(): lax.dot_general(data_f32, weights, (((0,), (1,)), ((), ())), precision=la...]
  transfers between devices with their start and end apart: 2 -> 3, of which waited for: 2 -> 2; matrix products, arithmetic and copies ran while one was open for 0% -> 1% of each run, Pallas kernels for 0% -> 0%
where the time goes in v1:
time: 121 us
  blocking collectives  81.7 us (68%)
  waiting for transfers between devices  17 us (14%)
  starting transfers between devices  10.3 us (9%)
  Pallas kernels  7.6 us (6%)
  local copies, waits for them, and re-layouts  3.61 us (3%)
    all_to_all x2, blocking collectives, local(): got = lax.all_to_all(lines, 'col', 0, 0)  29.3 us
    all_to_all x1, blocking collectives, local(): own = lax.all_to_all(outgoing, 'row', 0, 0).reshape(features, half)  27.1 us
    all_to_all x2, blocking collectives, local(): got = lax.all_to_all(lines, 'row', 0, 0)  25.3 us
    all_to_all x1, waiting for transfers between devices, local(): lax.all_to_all(jnp.broadcast_to(gen_points[None], (cols_n,) + gen_points....  10.5 us
    pallas_call x6, Pallas kernels, kernel_call(): pl.pallas_call(body, out_shape=out_shape, in_specs=[vmem() for _ in args]...  7.6 us
    all_to_all x1, starting transfers between devices, local(): lax.all_to_all(jnp.broadcast_to(gen_points[None], (cols_n,) + gen_points....  6.75 us
    all_to_all x1, waiting for transfers between devices, local(): got = lax.all_to_all(lines, 'col', 0, 0)  6.44 us
    all_to_all x1, starting transfers between devices, local(): got = lax.all_to_all(lines, 'col', 0, 0)  3.51 us
  transfers between devices with their start and end apart: 3, of which 2 were waited for; matrix products, arithmetic and copies ran while one was open for 1% of the time, Pallas kernels for 0%

profile of v1, /device:TPU:1, one launch (start us, length us, event | category | flops | bytes accessed | tf_op | source)
XLA Modules:
  0.0 120.9 jit_solution(518514863288291978)
XLA Ops:
  0.6 0.0 copy-start.2
  0.6 0.9 reshape.33
  1.6 0.0 copy-start.3
  1.6 27.1 %all_to_all.35 = bf16[16,32,512]{2,1,0:T(8,128)(2,1)S(1)} all-to-all(bf16[16,32,512]{2,1,0:T(8,128)(2,1)S(1)} %bitcast.14), channel_id=1, replica_groups=mesh['row'=16,'col'=16] {'row'}, dimensions={0} | all-to-all | bytes 1048576 | tf_op jit(solution)/shard_map/all_to_all | solution.py:180
  28.7 0.0 collective-permute-start
  28.7 0.0 copy-done.2
  28.7 0.8 broadcast_in_dim.6
  29.5 6.8 %all-to-all-start = ((bf16[16,32,512]{2,1,0:T(8,128)(2,1)}), bf16[16,32,512]{2,1,0:T(8,128)(2,1)S(1)}, u32[]{:S(2)}, u32[]{:S(2)}) async-start(bf16[16,32,512]{2,1,0:T(8,128)(2,1)} %broadcast_in_dim.6), calls=%async_computation | async-start | bytes 1048576 | tf_op jit(solution)/shard_map/all_to_all | solution.py:181
  36.3 0.0 copy-done.3
  36.4 10.5 %all-to-all-done = bf16[16,32,512]{2,1,0:T(8,128)(2,1)S(1)} async-done(((bf16[16,32,512]{2,1,0:T(8,128)(2,1)}), bf16[16,32,512]{2,1,0:T(8,128)(2,1)S(1)}, u32[]{:S(2)}, u32[]{:S(2)}) %all-to-all-start) | async-done | bytes 524320 | tf_op jit(solution)/shard_map/all_to_all | solution.py:181
  46.9 0.0 copy-start
  46.9 0.8 copy-done
  47.7 0.0 collective-permute-done.other_ref.refs_4_
  47.7 0.0 copy-start.1
  47.7 1.0 copy-done.1
  48.7 1.9 %shard_map.58 = (f32[512,1024]{1,0:T(8,128)S(1)}, f32[16,4,128]{2,1,0:T(4,128)}) custom-call(bf16[512,512]{1,0:T(8,128)(2,1)S(1)} %bitcast.12, bf16[512,512]{1,0:T(8,128)(2,1)S(1)} %bitcast.10, bf16[512,512]{1,0:T(8,128)(2,1)S(1)} %collective-permute-done.other_ref.refs_4_, f32[8,128]{1,0:T(8,128)S(1)} %bitcast.13), custom_call_target="tpu_custom_call" | custom-call | tf_op jit(solution)/shard_map/pallas_call | solution.py:30
  50.6 3.5 %all-to-all-start.2 = ((f32[16,4,128]{2,1,0:T(4,128)}), f32[16,4,128]{2,1,0:T(4,128)S(1)}, u32[]{:S(2)}, u32[]{:S(2)}) async-start(f32[16,4,128]{2,1,0:T(4,128)} %get-tuple-element.10), calls=%async_computation.2 | async-start | bytes 65536 | tf_op jit(solution)/shard_map/all_to_all | solution.py:202
  54.1 6.4 %all-to-all-done.2.refs_1_ = f32[16,4,128]{2,1,0:T(4,128)S(1)} async-done(((f32[16,4,128]{2,1,0:T(4,128)}), f32[16,4,128]{2,1,0:T(4,128)S(1)}, u32[]{:S(2)}, u32[]{:S(2)}) %all-to-all-start.2) | async-done | bytes 32800 | tf_op jit(solution)/shard_map/all_to_all | solution.py:202
  60.6 0.6 shard_map.59
  61.1 13.5 %all_to_all.36.refs_1_ = f32[16,8,128]{2,1,0:T(8,128)S(1)} all-to-all(f32[16,8,128]{2,1,0:T(8,128)S(1)} %shard_map.59), channel_id=1, replica_groups=mesh['row'=16,'col'=16] {'row'}, dimensions={0} | all-to-all | bytes 131072 | tf_op jit(solution)/shard_map/all_to_all | solution.py:204
  74.6 0.6 shard_map.60
  75.3 9.3 %all_to_all.37.refs_1_ = f32[16,4,128]{2,1,0:T(4,128)S(1)} all-to-all(f32[16,4,128]{2,1,0:T(4,128)S(1)} %shard_map.60), channel_id=1, replica_groups=mesh['row'=16,'col'=16] {'col'}, dimensions={0} | all-to-all | bytes 65536 | tf_op jit(solution)/shard_map/all_to_all | solution.py:202
  84.5 0.6 shard_map.61
  85.1 11.8 %all_to_all.38.refs_1_ = f32[16,8,128]{2,1,0:T(8,128)S(1)} all-to-all(f32[16,8,128]{2,1,0:T(8,128)S(1)} %shard_map.61), channel_id=1, replica_groups=mesh['row'=16,'col'=16] {'row'}, dimensions={0} | all-to-all | bytes 131072 | tf_op jit(solution)/shard_map/all_to_all | solution.py:204
  96.9 3.2 %shard_map.62 = (f32[8,128]{1,0:T(8,128)}, f32[16,136,128]{2,1,0:T(8,128)S(1)}) custom-call(f32[512,1024]{1,0:T(8,128)S(1)} %get-tuple-element.9.refs_0_, f32[16,8,128]{2,1,0:T(8,128)S(1)} %all_to_all.38.refs_1_, f32[8,128]{1,0:T(8,128)S(1)} %broadcast_in_dim.8.refs_2_, bf16[512,512]{1,0:T(8,128)(2,1)S(1)} %bitcast.11, ...), custom_call_target="tpu_custom_call" | custom-call | tf_op jit(solution)/shard_map/pallas_call | solution.py:30
  100.1 20.0 %all_to_all.39.refs_0_ = f32[16,136,128]{2,1,0:T(8,128)S(1)} all-to-all(f32[16,136,128]{2,1,0:T(8,128)S(1)} %get-tuple-element.11), channel_id=1, replica_groups=mesh['row'=16,'col'=16] {'col'}, dimensions={0} | all-to-all | bytes 2228224 | tf_op jit(solution)/shard_map/all_to_all | solution.py:217
  120.2 0.8 shard_map.63
  (5 shorter events, 0.1 us)
Async XLA Ops:
  0.6 28.1 %copy-start.2 = (bf16[32,512]{1,0:T(8,128)(2,1)S(1)}, bf16[32,512]{1,0:T(8,128)(2,1)}, u32[]{:S(2)}) copy-start(bf16[32,512]{1,0:T(8,128)(2,1)} %param.3) | copy-start | bytes 98308
  1.6 34.7 %copy-start.3 = (f32[1024]{0:T(1024)S(1)}, f32[1024]{0:T(1024)}, u32[]{:S(2)}) copy-start(f32[1024]{0:T(1024)} %param.5) | copy-start | bytes 12292
  28.7 19.0 %collective-permute-start = (bf16[512,512]{1,0:T(8,128)(2,1)S(1)}, bf16[512,512]{1,0:T(8,128)(2,1)S(1)}, u32[]{:S(2)}, u32[]{:S(2)}) collective-permute-start(bf16[512,512]{1,0:T(8,128)(2,1)S(1)} %bitcast.9), channel_id=1, source_target_pairs={{0,16},{16,0},{32,48},{48,32},{64,80},{80,64},{96,112},{112,96},{1... | collective-permute-start | bytes 1572872 | tf_op jit(solution)/shard_map/ppermute | solution.py:183
  29.5 17.3 %all-to-all-start = ((bf16[16,32,512]{2,1,0:T(8,128)(2,1)}), bf16[16,32,512]{2,1,0:T(8,128)(2,1)S(1)}, u32[]{:S(2)}, u32[]{:S(2)}) async-start(bf16[16,32,512]{2,1,0:T(8,128)(2,1)} %broadcast_in_dim.6), calls=%async_computation | async-start | bytes 1048576 | tf_op jit(solution)/shard_map/all_to_all | solution.py:181
  46.9 0.8 copy-start
  47.7 1.0 copy-start.1
  50.6 10.0 %all-to-all-start.2 = ((f32[16,4,128]{2,1,0:T(4,128)}), f32[16,4,128]{2,1,0:T(4,128)S(1)}, u32[]{:S(2)}, u32[]{:S(2)}) async-start(f32[16,4,128]{2,1,0:T(4,128)} %get-tuple-element.10), calls=%async_computation.2 | async-start | bytes 65536 | tf_op jit(solution)/shard_map/all_to_all | solution.py:202

commit v2 on v1

v2 whole, which is shorter than its diff:
```python
import functools
import math

import jax
import jax.numpy as jnp
from jax import lax
from jax.experimental import pallas as pl
from jax.experimental.pallas import tpu as pltpu
from jax.sharding import PartitionSpec as P

ITERS = 2
EPS = 0.05
LN2 = math.log(2.0)
SCALE = 1.0 / (EPS * LN2)
LANES = 128


def in_vmem(array):
    return pltpu.with_memory_space_constraint(array, pltpu.VMEM)


def kernel_call(body, out_shape, args, scratch=(), scalars=0, flops=None, aliases=(), space=pltpu.VMEM):
    whole = pl.BlockSpec(memory_space=space)
    smem = pl.BlockSpec(memory_space=pltpu.SMEM)
    return pl.pallas_call(
        body,
        out_shape=out_shape,
        in_specs=[smem] * scalars + [whole] * (len(args) - scalars),
        out_specs=jax.tree.map(lambda _: whole, out_shape),
        scratch_shapes=list(scratch),
        input_output_aliases=dict(aliases),
        cost_estimate=flops and pl.CostEstimate(flops=flops, bytes_accessed=0, transcendentals=0),
        compiler_params=pltpu.CompilerParams(vmem_limit_bytes=16 * 1024 * 1024),
    )(*args)


def log_sum(parts):
    top = jnp.max(parts, axis=0)
    return top + jnp.log2(jnp.sum(jnp.exp2(parts - top[None]), axis=0))


def lanes_to_rows(chunk):
    return jnp.broadcast_to(chunk, (LANES, LANES)).T


def rows_to_lanes(column):
    return jnp.broadcast_to(column, (LANES, LANES)).T[0:1, :]


def chunks_to_line(chunks):
    return jnp.concatenate([chunks[n : n + 1, :] for n in range(chunks.shape[0])], axis=1)


def line_to_chunks(line):
    return jnp.concatenate([line[:, n : n + LANES] for n in range(0, line.shape[1], LANES)], axis=0)


def chunk(n):
    return slice(n * LANES, (n + 1) * LANES)


def halves(chunks):
    half = chunks.shape[0] // 2
    return [chunks_to_line(chunks[:half]), chunks_to_line(chunks[half:])]


def send_row_log_sums(refs, lines, out_ref):
    for n in range(refs[0].shape[0] // LANES):
        tiles = [ref[chunk(n), :] + line for ref, line in zip(refs, lines)]
        top = jnp.max(functools.reduce(jnp.maximum, tiles), axis=1, keepdims=True)
        total = jnp.sum(sum(jnp.exp2(tile - top) for tile in tiles), axis=1, keepdims=True)
        line = rows_to_lanes(top + jnp.log2(total))
        out_ref[:, n : n + 1, :] = jnp.broadcast_to(line[None], (out_ref.shape[0], 1, LANES))


def layout_kernel(data_ref, out_ref, sems):
    half = out_ref.shape[2]
    copies = [
        pltpu.make_async_copy(data_ref.at[:, pl.ds(n % 2 * half, half)], out_ref.at[n], sems.at[n])
        for n in range(out_ref.shape[0])
    ]
    for copy in copies:
        copy.start()
    for copy in copies:
        copy.wait()


def stack_kernel(*refs):
    for n, ref in enumerate(refs[:-1]):
        refs[-1][n, :, :] = ref[...]


def ordered_kernel(*_):
    pass


def affinity_of(gen, data):
    gen_f32, data_f32 = gen.astype(jnp.float32), data.astype(jnp.float32)
    gen_sq = jnp.sum(gen_f32 * gen_f32, axis=1, keepdims=True)
    data_sq = jnp.sum(data_f32 * data_f32, axis=0, keepdims=True)
    cross = jnp.dot(gen, data, preferred_element_type=jnp.float32)
    return (2.0 * cross - (gen_sq + data_sq)) * (SCALE / gen.shape[1])


def own_kernel(place_ref, g0, g1, g2, g3, data_ref, gen_ref, affinity_ref):
    rows = g0.shape[1]
    for a, ref in enumerate((g0, g1, g2, g3)):
        for b in range(ref.shape[0]):
            start = pl.multiple_of(place_ref[a * ref.shape[0] + b] * rows, rows)
            gen_ref[pl.ds(start, rows), :] = ref[b, :, :]
    affinity_ref[...] = affinity_of(gen_ref[...], data_ref[...])


def other_kernel(gen_ref, data_ref, own_ref, pot_ref, affinity_ref, out_ref):
    affinity_ref[...] = affinity_of(gen_ref[...], data_ref[...])
    send_row_log_sums([own_ref, affinity_ref], halves(pot_ref[...]), out_ref)


def swap_halves(chunks, swap_ref):
    half = chunks.shape[0] // 2
    swapped = jnp.concatenate([chunks[half:], chunks[:half]], axis=0)
    return jnp.where(swap_ref[...] > 0.0, swapped, chunks)


def col_kernel(log_data, own_ref, other_ref, got_ref, swap_ref, out_ref, pot_ref):
    gen_rows, half = own_ref.shape
    row_pot = log_data - log_sum(got_ref[...])
    for n in range(gen_rows // LANES):
        pot_ref[chunk(n), :] = lanes_to_rows(row_pot[n : n + 1, :])
    lines = []
    for ref in (own_ref, other_ref):

        def tile(n):
            return ref[chunk(n), :] + jnp.concatenate([pot_ref[chunk(n), :]] * (half // LANES), axis=1)

        def folded(values):
            return values.reshape(LANES // 8, 8, half)

        top = jnp.full((8, half), -jnp.inf, jnp.float32)
        for n in range(gen_rows // LANES):
            top = jnp.maximum(top, jnp.max(folded(tile(n)), axis=0))
        top = jnp.max(top, axis=0, keepdims=True)
        total = jnp.zeros((8, half), jnp.float32)
        for n in range(gen_rows // LANES):
            total = total + jnp.sum(folded(jnp.exp2(tile(n) - top)), axis=0)
        lines.append(line_to_chunks(top + jnp.log2(jnp.sum(total, axis=0, keepdims=True))))
    chunks = swap_halves(jnp.concatenate(lines, axis=0), swap_ref)
    out_ref[...] = jnp.broadcast_to(chunks[None], out_ref.shape)


def row_kernel(log_gen, own_ref, other_ref, got_ref, swap_ref, out_ref):
    pot = swap_halves(log_gen - log_sum(got_ref[...]), swap_ref)
    send_row_log_sums([own_ref, other_ref], halves(pot), out_ref)


def target_kernel(log_gen, own_ref, other_ref, got_ref, swap_ref, data_ref, more_ref, pot_ref, out_ref, high, low):
    gen_rows, half = own_ref.shape
    receivers = out_ref.shape[0]
    chunks = gen_rows // LANES
    features = data_ref.shape[0]
    feats = features // receivers
    base = chunks * feats
    pot = log_gen - log_sum(got_ref[...])
    pot_ref[...] = pot * (1.0 / SCALE)
    lines = halves(swap_halves(pot, swap_ref))
    dims = (((1,), (1,)), ((), ()))
    group = 2
    for first in range(0, chunks, group):
        for n in range(first, first + group):
            tiles = [ref[chunk(n), :] + line for ref, line in zip((own_ref, other_ref), lines)]
            top = jnp.max(jnp.maximum(*tiles), axis=1, keepdims=True)
            total = 0.0
            for part, tile in enumerate(tiles):
                weights = jnp.exp2(tile - top)
                total = total + weights
                upper = weights.astype(jnp.bfloat16)
                cols = slice(part * half, (part + 1) * half)
                high[chunk(n), cols] = upper
                low[chunk(n), cols] = (weights - upper.astype(jnp.float32)).astype(jnp.bfloat16)
            total = jnp.sum(total, axis=1, keepdims=True)
            for place, column in ((base + n, top), (base + chunks + n, total)):
                out_ref[:, place : place + 1, :] = jnp.broadcast_to(rows_to_lanes(column)[None], (receivers, 1, LANES))
        rows = slice(first * LANES, (first + group) * LANES)
        sums = jnp.zeros((features, group * LANES), jnp.float32)
        for part, ref in enumerate((data_ref, more_ref)):
            cols = slice(part * half, (part + 1) * half)
            for piece in (high, low):
                sums = sums + lax.dot_general(ref[...], piece[rows, cols], dims, preferred_element_type=jnp.float32)
        for n in range(group):
            out_ref[:, (first + n) * feats : (first + n + 1) * feats, :] = sums[:, chunk(n)].reshape(receivers, feats, LANES)


def merge_kernel(log_data, got_ref, gen_pot_ref, target_ref):
    feats = target_ref.shape[0]
    chunks = target_ref.shape[1] // LANES
    base = chunks * feats
    tops = got_ref[:, base : base + chunks, :]
    totals = got_ref[:, base + chunks : base + 2 * chunks, :]
    top = jnp.max(tops, axis=0)
    factors = jnp.exp2(tops - top[None])
    total = jnp.sum(factors * totals, axis=0)
    gen_pot_ref[...] = (log_data - (top + jnp.log2(total))) * (1.0 / SCALE)
    factors = factors / total[None]
    for n in range(chunks):
        piece = got_ref[:, n * feats : (n + 1) * feats, :]
        target_ref[:, chunk(n)] = jnp.sum(piece * factors[:, n : n + 1, :], axis=0)


def local(gen_points, data_points, data_potential):
    f32 = jnp.float32
    rows_n, cols_n = lax.axis_size("row"), lax.axis_size("col")
    gen_rows = gen_points.shape[0] * cols_n
    data_cols = data_points.shape[0]
    features = gen_points.shape[1]
    log_data = math.log2(data_cols * cols_n)
    log_gen = math.log2(gen_rows * rows_n)
    half = data_cols // 2
    gen_chunks, data_chunks = gen_rows // LANES, data_cols // LANES
    feats = features // cols_n
    dtype = gen_points.dtype
    shaped = jax.ShapeDtypeStruct

    side = math.isqrt(cols_n)
    offsets = (0, 1, side - 1, 2)

    def from_x(array, back):
        return lax.ppermute(array, "col", [(i, i - i % side + (i + back) % side) for i in range(cols_n)])

    def from_y(array, back):
        return lax.ppermute(array, "col", [(i, (i + back * side) % cols_n) for i in range(cols_n)])

    along_x = [from_x(gen_points, back) for back in offsets[1:]]
    outgoing = kernel_call(
        layout_kernel,
        shaped((rows_n, data_points.shape[1], half), dtype),
        (data_points.T,),
        scratch=[pltpu.SemaphoreType.DMA((rows_n,))],
        space=pl.ANY,
    )
    own = lax.all_to_all(outgoing, "row", 0, 0).reshape(features, half)
    stack = kernel_call(stack_kernel, shaped((side,) + gen_points.shape, dtype), (gen_points, *along_x))
    stacks = (stack,) + tuple(from_y(stack, back) for back in offsets[1:])

    core = lax.axis_index("row") % 2
    place = lax.axis_index("col")
    back = jnp.array(offsets, jnp.int32)
    places = (((place // side - back) % side)[:, None] * side + ((place % side - back) % side)[None, :]).reshape(-1)
    swap = jnp.broadcast_to(core.astype(f32), (data_chunks, LANES))
    start = (data_potential * SCALE).reshape(2, data_chunks // 2, LANES)
    start = jnp.where(core == 1, start[::-1], start).reshape(data_chunks, LANES)

    own = kernel_call(ordered_kernel, pltpu.VMEM(own.shape, dtype), (own, *stacks[1:]), aliases={0: 0})
    other = in_vmem(lax.ppermute(own, "row", [(i, i ^ 1) for i in range(rows_n)]))
    own = in_vmem(own)
    row_out = pltpu.VMEM((cols_n, gen_chunks, LANES), f32)
    col_out = pltpu.VMEM((rows_n, data_chunks, LANES), f32)
    block = pltpu.VMEM((gen_rows, half), f32)

    def at(body, number):
        return lambda *refs: body(number, *refs)

    gen, own_affinity = kernel_call(
        own_kernel,
        (pltpu.VMEM((gen_rows, features), dtype), block),
        (places, *stacks, own),
        scalars=1,
        flops=2 * gen_rows * half * features,
    )
    own_affinity = in_vmem(own_affinity)
    other_affinity, lines = kernel_call(other_kernel, (block, row_out), (gen, other, own_affinity, start))
    affinity = (own_affinity, in_vmem(other_affinity))
    for step in range(ITERS):
        got = lax.all_to_all(lines, "col", 0, 0)
        lines = kernel_call(
            at(col_kernel, log_data),
            col_out,
            (*affinity, got, swap),
            scratch=[pltpu.VMEM((gen_rows, LANES), f32)],
        )
        got = lax.all_to_all(lines, "row", 0, 0)
        if step < ITERS - 1:
            lines = kernel_call(at(row_kernel, log_gen), row_out, (*affinity, got, swap))
    potential, lines = kernel_call(
        at(target_kernel, log_gen),
        (shaped((data_chunks, LANES), f32), shaped((cols_n, gen_chunks * (feats + 2), LANES), f32)),
        (*affinity, got, swap, own, other),
        scratch=[pltpu.VMEM((gen_rows, data_cols), dtype)] * 2,
    )
    got = lax.all_to_all(lines, "col", 0, 0)
    gen_pot, target = kernel_call(
        at(merge_kernel, log_data),
        (shaped((gen_chunks, LANES), f32), shaped((feats, gen_rows), f32)),
        (got,),
    )
    return (gen_pot.reshape(gen_rows), potential.reshape(data_cols), target)


def solution(mesh):
    placed = (P(("row", "col"), None), P("col", "row"), P("col"))
    return jax.shard_map(
        local,
        mesh=mesh,
        in_specs=placed,
        out_specs=(P("row"), P("col"), P("col", "row")),
        check_vma=False,
    )
```

time: 121 us -> 109 us (0.901)
  blocking collectives: 81.7 us -> 57.1 us
  starting transfers between devices: 10.3 us -> 25.9 us
  local copies, waits for them, and re-layouts: 3.61 us -> 0.94 us
  waiting for transfers between devices: 17 us -> 15.3 us
    all_to_all x1 -> x0, blocking collectives: 27.1 us -> none  [local(): own = lax.all_to_all(outgoing, 'row', 0, 0).reshape(features, half)]
    ppermute x1 -> x7, starting transfers between devices: 0.01 us -> 10.4 us  [the longest x3 4.47 us: from_y(): lax.ppermute(array, 'col', [(i, (i + back * side) % cols_n) for i in rang...]
    all_to_all x1, waiting for transfers between devices: 10.5 us -> 0.96 us  [local(): own = lax.all_to_all(outgoing, 'row', 0, 0).reshape(features, half)]
    ppermute x1 -> x7, waiting for transfers between devices: 0.01 us -> 7.89 us  [the longest x3 4.77 us: from_y(): lax.ppermute(array, 'col', [(i, (i + back * side) % cols_n) for i in rang...]
    all_to_all x1, starting transfers between devices: 6.75 us -> 9.99 us  [local(): own = lax.all_to_all(outgoing, 'row', 0, 0).reshape(features, half)]
    all_to_all x2, blocking collectives: 25.3 us -> 27.8 us  [local(): got = lax.all_to_all(lines, 'row', 0, 0)]
    all_to_all x1, starting transfers between devices: 3.51 us -> 5.48 us  [local(): got = lax.all_to_all(lines, 'col', 0, 0)]
    pallas_call x6 -> x10, Pallas kernels: 7.6 us -> 8.25 us  [kernel_call(): pl.pallas_call(body, out_shape=out_shape, in_specs=[smem] * scalars + [wh...]
  transfers between devices with their start and end apart: 3 -> 9, of which waited for: 2 -> 8; matrix products, arithmetic and copies ran while one was open for 1% -> 0% of each run, Pallas kernels for 0% -> 1%
where the time goes in v2:
time: 109 us; the launch traced here: 108 us
  blocking collectives  57.1 us (52%)
  starting transfers between devices  25.9 us (24%)
  waiting for transfers between devices  15.3 us (14%)
  Pallas kernels  8.25 us (8%)
    all_to_all x2, blocking collectives, local(): got = lax.all_to_all(lines, 'col', 0, 0)  29.2 us
    all_to_all x2, blocking collectives, local(): got = lax.all_to_all(lines, 'row', 0, 0)  27.8 us
    all_to_all x1, starting transfers between devices, local(): own = lax.all_to_all(outgoing, 'row', 0, 0).reshape(features, half)  9.99 us
    pallas_call x10, Pallas kernels, kernel_call(): pl.pallas_call(body, out_shape=out_shape, in_specs=[smem] * scalars + [wh...  8.25 us
    all_to_all x1, waiting for transfers between devices, local(): got = lax.all_to_all(lines, 'col', 0, 0)  6.45 us
    all_to_all x1, starting transfers between devices, local(): got = lax.all_to_all(lines, 'col', 0, 0)  5.48 us
    ppermute x3, waiting for transfers between devices, from_y(): lax.ppermute(array, 'col', [(i, (i + back * side) % cols_n) for i in rang...  4.77 us
    ppermute x3, starting transfers between devices, from_y(): lax.ppermute(array, 'col', [(i, (i + back * side) % cols_n) for i in rang...  4.47 us
  transfers between devices with their start and end apart: 9, of which 8 were waited for; matrix products, arithmetic and copies ran while one was open for 0% of the time, Pallas kernels for 1%

profile of v2, /device:TPU:1, one launch (start us, length us, event | category | flops | bytes accessed | tf_op | source)
XLA Modules:
  0.0 108.3 jit_solution(10677345957654429605)
XLA Ops:
  0.6 0.0 copy-start.3
  0.6 0.0 copy-start
  0.7 0.8 copy-done
  1.5 0.0 copy-start.1
  1.5 0.9 shard_map.68
  2.4 10.0 %all-to-all-start = ((bf16[16,32,512]{2,1,0:T(8,128)(2,1)}), bf16[16,32,512]{2,1,0:T(8,128)(2,1)S(1)}, u32[]{:S(2)}, u32[]{:S(2)}) async-start(bf16[16,32,512]{2,1,0:T(8,128)(2,1)} %shard_map.68), calls=%async_computation | async-start | bytes 1048576 | tf_op jit(solution)/shard_map/all_to_all | solution.py:240
  12.4 0.0 copy-done.1
  12.4 0.0 copy-start.2
  12.5 2.6 %collective-permute-start.1 = (bf16[32,512]{1,0:T(8,128)(2,1)S(1)}, bf16[32,512]{1,0:T(8,128)(2,1)S(1)}, u32[]{:S(2)}, u32[]{:S(2)}) collective-permute-start(bf16[32,512]{1,0:T(8,128)(2,1)S(1)} %copy-done.1), channel_id=1, source_target_pairs={{0,3},{1,0},{2,1},{3,2},{4,7},{5,4},{6,5},{7,6},{8,11},{9,8},{10,9... | collective-permute-start | bytes 98312 | tf_op jit(solution)/shard_map/ppermute | solution.py:227
  15.0 0.0 collective-permute-start
  15.0 1.7 %collective-permute-start.2 = (bf16[32,512]{1,0:T(8,128)(2,1)S(1)}, bf16[32,512]{1,0:T(8,128)(2,1)S(1)}, u32[]{:S(2)}, u32[]{:S(2)}) collective-permute-start(bf16[32,512]{1,0:T(8,128)(2,1)S(1)} %copy-done.1), channel_id=1, source_target_pairs={{0,2},{1,3},{2,0},{3,1},{4,6},{5,7},{6,4},{7,5},{8,10},{9,11},{10,... | collective-permute-start | bytes 98312 | tf_op jit(solution)/shard_map/ppermute | solution.py:227
  16.8 0.0 collective-permute-done.1.refs_2_
  16.8 2.5 %collective-permute-done.refs_1_ = bf16[32,512]{1,0:T(8,128)(2,1)S(1)} collective-permute-done((bf16[32,512]{1,0:T(8,128)(2,1)S(1)}, bf16[32,512]{1,0:T(8,128)(2,1)S(1)}, u32[]{:S(2)}, u32[]{:S(2)}) %collective-permute-start) | collective-permute-done | bytes 32800 | tf_op jit(solution)/shard_map/ppermute | solution.py:227
  19.3 0.2 collective-permute-done.2.refs_3_
  19.5 3.0 %collective-permute-start.5 = (bf16[4,32,512]{2,1,0:T(8,128)(2,1)S(1)}, bf16[4,32,512]{2,1,0:T(8,128)(2,1)S(1)}, u32[]{:S(2)}, u32[]{:S(2)}) collective-permute-start(bf16[4,32,512]{2,1,0:T(8,128)(2,1)S(1)} %shard_map.67.g0), channel_id=1, source_target_pairs={{0,8},{1,9},{2,10},{3,11},{4,12},{5,13},{6,14},{7,15},{8,0},{9,1},... | collective-permute-start | bytes 393224 | tf_op jit(solution)/shard_map/ppermute | solution.py:230
  22.5 0.8 collective-permute-start.4
  23.3 0.7 collective-permute-start.3
  24.0 0.0 copy-done.3
  24.0 1.1 collective-permute-done.5.__3_.g3
  25.1 2.8 %collective-permute-done.4.__2_.g2 = bf16[4,32,512]{2,1,0:T(8,128)(2,1)S(1)} collective-permute-done((bf16[4,32,512]{2,1,0:T(8,128)(2,1)S(1)}, bf16[4,32,512]{2,1,0:T(8,128)(2,1)S(1)}, u32[]{:S(2)}, u32[]{:S(2)}) %collective-permute-start.4) | collective-permute-done | bytes 131104 | tf_op jit(solution)/shard_map/ppermute | solution.py:230
  27.9 0.9 collective-permute-done.3.__1_.g1
  28.8 1.0 all-to-all-done
  29.8 1.7 %collective-permute-start.6 = (bf16[512,512]{1,0:T(8,128)(2,1)S(1)}, bf16[512,512]{1,0:T(8,128)(2,1)S(1)}, u32[]{:S(2)}, u32[]{:S(2)}) collective-permute-start(bf16[512,512]{1,0:T(8,128)(2,1)S(1)} %shard_map.69.data_ref.refs_4_), channel_id=1, source_target_pairs={{0,16},{16,0},{32,48},{48,32},{64,80},{80,64},{96,112},{112,96},{1... | collective-permute-start | bytes 1572872 | tf_op jit(solution)/shard_map/ppermute | solution.py:253
  31.4 0.1 broadcast_add_fusion
  31.5 0.1 add.41.place_ref
  31.6 0.0 copy-done.2
  31.6 1.0 shard_map.70
  32.6 0.4 collective-permute-done.6.data_ref.refs_5_
  32.9 1.6 %shard_map.71 = (f32[512,512]{1,0:T(8,128)S(1)}, f32[16,4,128]{2,1,0:T(4,128)}) custom-call(bf16[512,512]{1,0:T(8,128)(2,1)S(1)} %get-tuple-element.12.gen_ref, bf16[512,512]{1,0:T(8,128)(2,1)S(1)} %collective-permute-done.6.data_ref.refs_5_, f32[512,512]{1,0:T(8,128)S(1)} %get-tuple-element.11.own_ref.refs_0_, f32[8,128]{1,0:T(8,128)S(1)} %bitcast.8), custom_call_target="tpu_custom_call" | custom-call | tf_op jit(solution)/shard_map/pallas_call | solution.py:25
  34.6 5.5 %all-to-all-start.1 = ((f32[16,4,128]{2,1,0:T(4,128)}), f32[16,4,128]{2,1,0:T(4,128)S(1)}, u32[]{:S(2)}, u32[]{:S(2)}) async-start(f32[16,4,128]{2,1,0:T(4,128)} %get-tuple-element.14), calls=%async_computation.1 | async-start | bytes 65536 | tf_op jit(solution)/shard_map/all_to_all | solution.py:273
  40.0 6.4 %all-to-all-done.1.refs_2_ = f32[16,4,128]{2,1,0:T(4,128)S(1)} async-done(((f32[16,4,128]{2,1,0:T(4,128)}), f32[16,4,128]{2,1,0:T(4,128)S(1)}, u32[]{:S(2)}, u32[]{:S(2)}) %all-to-all-start.1) | async-done | bytes 32800 | tf_op jit(solution)/shard_map/all_to_all | solution.py:273
  46.5 0.5 shard_map.72
  47.1 16.0 %all_to_all.30.refs_2_ = f32[16,8,128]{2,1,0:T(8,128)S(1)} all-to-all(f32[16,8,128]{2,1,0:T(8,128)S(1)} %shard_map.72), channel_id=1, replica_groups=mesh['row'=16,'col'=16] {'row'}, dimensions={0} | all-to-all | bytes 131072 | tf_op jit(solution)/shard_map/all_to_all | solution.py:280
  63.1 0.6 shard_map.73
  63.7 9.2 %all_to_all.31.refs_2_ = f32[16,4,128]{2,1,0:T(4,128)S(1)} all-to-all(f32[16,4,128]{2,1,0:T(4,128)S(1)} %shard_map.73), channel_id=1, replica_groups=mesh['row'=16,'col'=16] {'col'}, dimensions={0} | all-to-all | bytes 65536 | tf_op jit(solution)/shard_map/all_to_all | solution.py:273
  72.9 0.5 shard_map.74
  73.5 11.8 %all_to_all.32.refs_2_ = f32[16,8,128]{2,1,0:T(8,128)S(1)} all-to-all(f32[16,8,128]{2,1,0:T(8,128)S(1)} %shard_map.74), channel_id=1, replica_groups=mesh['row'=16,'col'=16] {'row'}, dimensions={0} | all-to-all | bytes 131072 | tf_op jit(solution)/shard_map/all_to_all | solution.py:280
  85.3 2.2 %shard_map.75 = (f32[8,128]{1,0:T(8,128)}, f32[16,136,128]{2,1,0:T(8,128)S(1)}) custom-call(f32[512,512]{1,0:T(8,128)S(1)} %get-tuple-element.11.own_ref.refs_0_, f32[512,512]{1,0:T(8,128)S(1)} %get-tuple-element.13.refs_1_, f32[16,8,128]{2,1,0:T(8,128)S(1)} %all_to_all.32.refs_2_, f32[8,128]{1,0:T(8,128)S(1)} %broadcast_in_dim.2.refs_3_, ...), custom_call_target="tpu_custom_call" | custom-call | tf_op jit(solution)/shard_map/pallas_call | solution.py:25
  87.5 20.0 %all_to_all.33.refs_0_ = f32[16,136,128]{2,1,0:T(8,128)S(1)} all-to-all(f32[16,136,128]{2,1,0:T(8,128)S(1)} %get-tuple-element.15), channel_id=1, replica_groups=mesh['row'=16,'col'=16] {'col'}, dimensions={0} | all-to-all | bytes 2228224 | tf_op jit(solution)/shard_map/all_to_all | solution.py:289
  107.5 0.8 shard_map.76
  (6 shorter events, 0.0 us)
Async XLA Ops:
  0.6 23.4 %copy-start.3 = (s32[4]{0:T(128)S(1)}, s32[4]{0:T(128)}, u32[]{:S(2)}) copy-start(s32[4]{0:T(128)} %constant.62) | copy-start | bytes 52
  0.6 0.8 copy-start
  1.5 10.9 %copy-start.1 = (bf16[32,512]{1,0:T(8,128)(2,1)S(1)}, bf16[32,512]{1,0:T(8,128)(2,1)}, u32[]{:S(2)}) copy-start(bf16[32,512]{1,0:T(8,128)(2,1)} %refs_0_.1) | copy-start | bytes 98308
  2.4 27.3 %all-to-all-start = ((bf16[16,32,512]{2,1,0:T(8,128)(2,1)}), bf16[16,32,512]{2,1,0:T(8,128)(2,1)S(1)}, u32[]{:S(2)}, u32[]{:S(2)}) async-start(bf16[16,32,512]{2,1,0:T(8,128)(2,1)} %shard_map.68), calls=%async_computation | async-start | bytes 1048576 | tf_op jit(solution)/shard_map/all_to_all | solution.py:240
  12.4 19.1 %copy-start.2 = (f32[1024]{0:T(1024)S(1)}, f32[1024]{0:T(1024)}, u32[]{:S(2)}) copy-start(f32[1024]{0:T(1024)} %param.6) | copy-start | bytes 12292
  12.5 4.3 %collective-permute-start.1 = (bf16[32,512]{1,0:T(8,128)(2,1)S(1)}, bf16[32,512]{1,0:T(8,128)(2,1)S(1)}, u32[]{:S(2)}, u32[]{:S(2)}) collective-permute-start(bf16[32,512]{1,0:T(8,128)(2,1)S(1)} %copy-done.1), channel_id=1, source_target_pairs={{0,3},{1,0},{2,1},{3,2},{4,7},{5,4},{6,5},{7,6},{8,11},{9,8},{10,9... | collective-permute-start | bytes 98312 | tf_op jit(solution)/shard_map/ppermute | solution.py:227
  15.0 4.3 %collective-permute-start = (bf16[32,512]{1,0:T(8,128)(2,1)S(1)}, bf16[32,512]{1,0:T(8,128)(2,1)S(1)}, u32[]{:S(2)}, u32[]{:S(2)}) collective-permute-start(bf16[32,512]{1,0:T(8,128)(2,1)S(1)} %copy-done.1), channel_id=1, source_target_pairs={{0,1},{1,2},{2,3},{3,0},{4,5},{5,6},{6,7},{7,4},{8,9},{9,10},{10,1... | collective-permute-start | bytes 98312 | tf_op jit(solution)/shard_map/ppermute | solution.py:227
  15.0 4.5 %collective-permute-start.2 = (bf16[32,512]{1,0:T(8,128)(2,1)S(1)}, bf16[32,512]{1,0:T(8,128)(2,1)S(1)}, u32[]{:S(2)}, u32[]{:S(2)}) collective-permute-start(bf16[32,512]{1,0:T(8,128)(2,1)S(1)} %copy-done.1), channel_id=1, source_target_pairs={{0,2},{1,3},{2,0},{3,1},{4,6},{5,7},{6,4},{7,5},{8,10},{9,11},{10,... | collective-permute-start | bytes 98312 | tf_op jit(solution)/shard_map/ppermute | solution.py:227
  19.5 5.5 %collective-permute-start.5 = (bf16[4,32,512]{2,1,0:T(8,128)(2,1)S(1)}, bf16[4,32,512]{2,1,0:T(8,128)(2,1)S(1)}, u32[]{:S(2)}, u32[]{:S(2)}) collective-permute-start(bf16[4,32,512]{2,1,0:T(8,128)(2,1)S(1)} %shard_map.67.g0), channel_id=1, source_target_pairs={{0,8},{1,9},{2,10},{3,11},{4,12},{5,13},{6,14},{7,15},{8,0},{9,1},... | collective-permute-start | bytes 393224 | tf_op jit(solution)/shard_map/ppermute | solution.py:230
  22.5 5.4 %collective-permute-start.4 = (bf16[4,32,512]{2,1,0:T(8,128)(2,1)S(1)}, bf16[4,32,512]{2,1,0:T(8,128)(2,1)S(1)}, u32[]{:S(2)}, u32[]{:S(2)}) collective-permute-start(bf16[4,32,512]{2,1,0:T(8,128)(2,1)S(1)} %shard_map.67.g0), channel_id=1, source_target_pairs={{0,12},{1,13},{2,14},{3,15},{4,0},{5,1},{6,2},{7,3},{8,4},{9,5},{1... | collective-permute-start | bytes 393224 | tf_op jit(solution)/shard_map/ppermute | solution.py:230
  23.3 5.5 %collective-permute-start.3 = (bf16[4,32,512]{2,1,0:T(8,128)(2,1)S(1)}, bf16[4,32,512]{2,1,0:T(8,128)(2,1)S(1)}, u32[]{:S(2)}, u32[]{:S(2)}) collective-permute-start(bf16[4,32,512]{2,1,0:T(8,128)(2,1)S(1)} %shard_map.67.g0), channel_id=1, source_target_pairs={{0,4},{1,5},{2,6},{3,7},{4,8},{5,9},{6,10},{7,11},{8,12},{9,13},{1... | collective-permute-start | bytes 393224 | tf_op jit(solution)/shard_map/ppermute | solution.py:230
  29.8 3.2 %collective-permute-start.6 = (bf16[512,512]{1,0:T(8,128)(2,1)S(1)}, bf16[512,512]{1,0:T(8,128)(2,1)S(1)}, u32[]{:S(2)}, u32[]{:S(2)}) collective-permute-start(bf16[512,512]{1,0:T(8,128)(2,1)S(1)} %shard_map.69.data_ref.refs_4_), channel_id=1, source_target_pairs={{0,16},{16,0},{32,48},{48,32},{64,80},{80,64},{96,112},{112,96},{1... | collective-permute-start | bytes 1572872 | tf_op jit(solution)/shard_map/ppermute | solution.py:253
  34.6 11.9 %all-to-all-start.1 = ((f32[16,4,128]{2,1,0:T(4,128)}), f32[16,4,128]{2,1,0:T(4,128)S(1)}, u32[]{:S(2)}, u32[]{:S(2)}) async-start(f32[16,4,128]{2,1,0:T(4,128)} %get-tuple-element.14), calls=%async_computation.1 | async-start | bytes 65536 | tf_op jit(solution)/shard_map/all_to_all | solution.py:273

commit v3 on v2

--- a/solution.py
+++ b/solution.py
@@ -13,19 +13,19 @@
 LN2 = math.log(2.0)
 SCALE = 1.0 / (EPS * LN2)
 LANES = 128
+OFFSETS = (0, 1, -1, 2)
 
 
 def in_vmem(array):
     return pltpu.with_memory_space_constraint(array, pltpu.VMEM)
 
 
-def kernel_call(body, out_shape, args, scratch=(), scalars=0, flops=None, aliases=(), space=pltpu.VMEM):
+def kernel_call(body, out_shape, args, scratch=(), flops=None, aliases=(), space=pltpu.VMEM):
     whole = pl.BlockSpec(memory_space=space)
-    smem = pl.BlockSpec(memory_space=pltpu.SMEM)
     return pl.pallas_call(
         body,
         out_shape=out_shape,
-        in_specs=[smem] * scalars + [whole] * (len(args) - scalars),
+        in_specs=[whole] * len(args),
         out_specs=jax.tree.map(lambda _: whole, out_shape),
         scratch_shapes=list(scratch),
         input_output_aliases=dict(aliases),
@@ -73,14 +73,18 @@
         out_ref[:, n : n + 1, :] = jnp.broadcast_to(line[None], (out_ref.shape[0], 1, LANES))
 
 
-def layout_kernel(data_ref, out_ref, sems):
+def layout_kernel(data_ref, out_ref, held, sems):
     half = out_ref.shape[2]
-    copies = [
-        pltpu.make_async_copy(data_ref.at[:, pl.ds(n % 2 * half, half)], out_ref.at[n], sems.at[n])
-        for n in range(out_ref.shape[0])
+    arrivals = [
+        pltpu.make_async_copy(data_ref.at[:, pl.ds(part * half, half)], held.at[part], sems.at[part]) for part in range(2)
     ]
-    for copy in copies:
-        copy.start()
+    copies = [pltpu.make_async_copy(held.at[n % 2], out_ref.at[n], sems.at[2 + n]) for n in range(out_ref.shape[0])]
+    for arrival in arrivals:
+        arrival.start()
+    for part, arrival in enumerate(arrivals):
+        arrival.wait()
+        for copy in copies[part::2]:
+            copy.start()
     for copy in copies:
         copy.wait()
 
@@ -94,35 +98,47 @@
     pass
 
 
-def affinity_of(gen, data):
-    gen_f32, data_f32 = gen.astype(jnp.float32), data.astype(jnp.float32)
-    gen_sq = jnp.sum(gen_f32 * gen_f32, axis=1, keepdims=True)
+def affinity_chunks(gen_ref, data_ref):
+    data = data_ref[...]
+    data_f32 = data.astype(jnp.float32)
     data_sq = jnp.sum(data_f32 * data_f32, axis=0, keepdims=True)
-    cross = jnp.dot(gen, data, preferred_element_type=jnp.float32)
-    return (2.0 * cross - (gen_sq + data_sq)) * (SCALE / gen.shape[1])
-
-
-def own_kernel(place_ref, g0, g1, g2, g3, data_ref, gen_ref, affinity_ref):
-    rows = g0.shape[1]
-    for a, ref in enumerate((g0, g1, g2, g3)):
-        for b in range(ref.shape[0]):
-            start = pl.multiple_of(place_ref[a * ref.shape[0] + b] * rows, rows)
-            gen_ref[pl.ds(start, rows), :] = ref[b, :, :]
-    affinity_ref[...] = affinity_of(gen_ref[...], data_ref[...])
-
-
-def other_kernel(gen_ref, data_ref, own_ref, pot_ref, affinity_ref, out_ref):
-    affinity_ref[...] = affinity_of(gen_ref[...], data_ref[...])
-    send_row_log_sums([own_ref, affinity_ref], halves(pot_ref[...]), out_ref)
-
-
-def swap_halves(chunks, swap_ref):
+    for n in range(gen_ref.shape[0] // LANES):
+        gen = gen_ref[chunk(n), :]
+        gen_f32 = gen.astype(jnp.float32)
+        gen_sq = jnp.sum(gen_f32 * gen_f32, axis=1, keepdims=True)
+        cross = jnp.dot(gen, data, preferred_element_type=jnp.float32)
+        yield chunk(n), (2.0 * cross - (gen_sq + data_sq)) * (SCALE / gen.shape[1])
+
+
+def own_kernel(g0, g1, g2, g3, data_ref, gen_ref, affinity_ref):
+    side, size = g0.shape[:2]
+    column, core = lax.axis_index("col"), lax.axis_index("row") % 2
+    for second, ref in zip(OFFSETS, (g0, g1, g2, g3)):
+        for n, first in enumerate(OFFSETS):
+            y_back = jnp.where(core == 0, second, first)
+            x_back = jnp.where(core == 0, first, second)
+            place = (column // side - y_back + side) % side * side + (column % side - x_back + side) % side
+            gen_ref[pl.ds(pl.multiple_of(place * size, size), size), :] = ref[n, :, :]
+    for rows, tile in affinity_chunks(gen_ref, data_ref):
+        affinity_ref[rows, :] = tile
+
+
+def other_kernel(gen_ref, data_ref, affinity_ref):
+    for rows, tile in affinity_chunks(gen_ref, data_ref):
+        affinity_ref[rows, :] = tile
+
+
+def first_kernel(own_ref, other_ref, pot_ref, out_ref):
+    send_row_log_sums((own_ref, other_ref), halves(swap_halves(pot_ref[...] * SCALE)), out_ref)
+
+
+def swap_halves(chunks):
     half = chunks.shape[0] // 2
     swapped = jnp.concatenate([chunks[half:], chunks[:half]], axis=0)
-    return jnp.where(swap_ref[...] > 0.0, swapped, chunks)
-
-
-def col_kernel(log_data, own_ref, other_ref, got_ref, swap_ref, out_ref, pot_ref):
+    return jnp.where(lax.axis_index("row") % 2 == 1, swapped, chunks)
+
+
+def col_kernel(log_data, own_ref, other_ref, got_ref, out_ref, pot_ref):
     gen_rows, half = own_ref.shape
     row_pot = log_data - log_sum(got_ref[...])
     for n in range(gen_rows // LANES):
@@ -144,16 +160,16 @@
         for n in range(gen_rows // LANES):
             total = total + jnp.sum(folded(jnp.exp2(tile(n) - top)), axis=0)
         lines.append(line_to_chunks(top + jnp.log2(jnp.sum(total, axis=0, keepdims=True))))
-    chunks = swap_halves(jnp.concatenate(lines, axis=0), swap_ref)
+    chunks = swap_halves(jnp.concatenate(lines, axis=0))
     out_ref[...] = jnp.broadcast_to(chunks[None], out_ref.shape)
 
 
-def row_kernel(log_gen, own_ref, other_ref, got_ref, swap_ref, out_ref):
-    pot = swap_halves(log_gen - log_sum(got_ref[...]), swap_ref)
-    send_row_log_sums([own_ref, other_ref], halves(pot), out_ref)
-
-
-def target_kernel(log_gen, own_ref, other_ref, got_ref, swap_ref, data_ref, more_ref, pot_ref, out_ref, high, low):
+def row_kernel(log_gen, own_ref, other_ref, got_ref, out_ref):
+    lines = halves(swap_halves(log_gen - log_sum(got_ref[...])))
+    send_row_log_sums((own_ref, other_ref), lines, out_ref)
+
+
+def target_kernel(log_gen, own_ref, other_ref, got_ref, data_ref, more_ref, pot_ref, out_ref, high, low):
     gen_rows, half = own_ref.shape
     receivers = out_ref.shape[0]
     chunks = gen_rows // LANES
@@ -162,7 +178,7 @@
     base = chunks * feats
     pot = log_gen - log_sum(got_ref[...])
     pot_ref[...] = pot * (1.0 / SCALE)
-    lines = halves(swap_halves(pot, swap_ref))
+    lines = halves(swap_halves(pot))
     dims = (((1,), (1,)), ((), ()))
     group = 2
     for first in range(0, chunks, group):
@@ -221,33 +237,30 @@
     shaped = jax.ShapeDtypeStruct
 
     side = math.isqrt(cols_n)
-    offsets = (0, 1, side - 1, 2)
-
-    def from_x(array, back):
-        return lax.ppermute(array, "col", [(i, i - i % side + (i + back) % side) for i in range(cols_n)])
-
-    def from_y(array, back):
-        return lax.ppermute(array, "col", [(i, (i + back * side) % cols_n) for i in range(cols_n)])
-
-    along_x = [from_x(gen_points, back) for back in offsets[1:]]
+
+    def hop(array, phase, back):
+        pairs = []
+        for row in range(rows_n):
+            for y in range(side):
+                for x in range(side):
+                    along_y = (row + phase) % 2
+                    to_y, to_x = (y + back * along_y) % side, (x + back * (1 - along_y)) % side
+                    pairs.append(((row * side + y) * side + x, (row * side + to_y) * side + to_x))
+        return lax.ppermute(array, ("row", "col"), pairs)
+
+    feats_held = data_points.shape[1]
     outgoing = kernel_call(
         layout_kernel,
-        shaped((rows_n, data_points.shape[1], half), dtype),
-        (data_points.T,),
-        scratch=[pltpu.SemaphoreType.DMA((rows_n,))],
-        space=pl.ANY,
+        shaped((rows_n, feats_held, half), dtype),
+        (pltpu.with_memory_space_constraint(data_points.T, pltpu.HBM),),
+        scratch=[pltpu.VMEM((2, feats_held, half), dtype), pltpu.SemaphoreType.DMA((2 + rows_n,))],
+        space=pltpu.HBM,
     )
     own = lax.all_to_all(outgoing, "row", 0, 0).reshape(features, half)
-    stack = kernel_call(stack_kernel, shaped((side,) + gen_points.shape, dtype), (gen_points, *along_x))
-    stacks = (stack,) + tuple(from_y(stack, back) for back in offsets[1:])
-
-    core = lax.axis_index("row") % 2
-    place = lax.axis_index("col")
-    back = jnp.array(offsets, jnp.int32)
-    places = (((place // side - back) % side)[:, None] * side + ((place % side - back) % side)[None, :]).reshape(-1)
-    swap = jnp.broadcast_to(core.astype(f32), (data_chunks, LANES))
-    start = (data_potential * SCALE).reshape(2, data_chunks // 2, LANES)
-    start = jnp.where(core == 1, start[::-1], start).reshape(data_chunks, LANES)
+    stack = kernel_call(stack_kernel, shaped((side,) + gen_points.shape, dtype), (gen_points, *(hop(gen_points, 0, back) for back in OFFSETS[1:])))
+    stacks = (stack,) + tuple(hop(stack, 1, back) for back in OFFSETS[1:])
+
+    start = data_potential.reshape(data_chunks, LANES)
 
     own = kernel_call(ordered_kernel, pltpu.VMEM(own.shape, dtype), (own, *stacks[1:]), aliases={0: 0})
     other = in_vmem(lax.ppermute(own, "row", [(i, i ^ 1) for i in range(rows_n)]))
@@ -262,28 +275,27 @@
     gen, own_affinity = kernel_call(
         own_kernel,
         (pltpu.VMEM((gen_rows, features), dtype), block),
-        (places, *stacks, own),
-        scalars=1,
+        (*stacks, own),
         flops=2 * gen_rows * half * features,
     )
     own_affinity = in_vmem(own_affinity)
-    other_affinity, lines = kernel_call(other_kernel, (block, row_out), (gen, other, own_affinity, start))
-    affinity = (own_affinity, in_vmem(other_affinity))
+    affinity = (own_affinity, in_vmem(kernel_call(other_kernel, block, (gen, other))))
+    lines = kernel_call(first_kernel, row_out, (*affinity, start))
     for step in range(ITERS):
         got = lax.all_to_all(lines, "col", 0, 0)
         lines = kernel_call(
             at(col_kernel, log_data),
             col_out,
-            (*affinity, got, swap),
+            (*affinity, got),
             scratch=[pltpu.VMEM((gen_rows, LANES), f32)],
         )
         got = lax.all_to_all(lines, "row", 0, 0)
         if step < ITERS - 1:
-            lines = kernel_call(at(row_kernel, log_gen), row_out, (*affinity, got, swap))
+            lines = kernel_call(at(row_kernel, log_gen), row_out, (*affinity, got))
     potential, lines = kernel_call(
         at(target_kernel, log_gen),
         (shaped((data_chunks, LANES), f32), shaped((cols_n, gen_chunks * (feats + 2), LANES), f32)),
-        (*affinity, got, swap, own, other),
+        (*affinity, got, own, other),
         scratch=[pltpu.VMEM((gen_rows, data_cols), dtype)] * 2,
     )
     got = lax.all_to_all(lines, "col", 0, 0)

time: 109 us -> 107 us (0.982)
  blocking collectives: 57.1 us -> 68.3 us
  waiting for transfers between devices: 15.3 us -> 9.51 us
  starting transfers between devices: 25.9 us -> 20.4 us
    all_to_all x2 -> x3, blocking collectives: 29.2 us -> 41 us  [local(): got = lax.all_to_all(lines, 'col', 0, 0)]
    all_to_all x1 -> x0, waiting for transfers between devices: 6.45 us -> none  [local(): got = lax.all_to_all(lines, 'col', 0, 0)]
    all_to_all x1 -> x0, starting transfers between devices: 5.48 us -> none  [local(): got = lax.all_to_all(lines, 'col', 0, 0)]
    pallas_call x10 -> x11, Pallas kernels: 8.25 us -> 8.03 us  [kernel_call(): pl.pallas_call(body, out_shape=out_shape, in_specs=[whole] * len(args), o...]
  transfers between devices with their start and end apart: 9 -> 8, of which waited for: 8 -> 6; matrix products, arithmetic and copies ran while one was open for 0% -> 0% of each run, Pallas kernels for 1% -> 1%
where the time goes in v3:
time: 107 us
  blocking collectives  68.3 us (64%)
  starting transfers between devices  20.4 us (19%)
  waiting for transfers between devices  9.51 us (9%)
  Pallas kernels  8.03 us (8%)
    all_to_all x3, blocking collectives, local(): got = lax.all_to_all(lines, 'col', 0, 0)  41 us
    all_to_all x2, blocking collectives, local(): got = lax.all_to_all(lines, 'row', 0, 0)  27.2 us
    all_to_all x1, starting transfers between devices, local(): own = lax.all_to_all(outgoing, 'row', 0, 0).reshape(features, half)  9.99 us
    ppermute x6, starting transfers between devices, hop(): return lax.ppermute(array, ('row', 'col'), pairs)  8.75 us
    pallas_call x11, Pallas kernels, kernel_call(): pl.pallas_call(body, out_shape=out_shape, in_specs=[whole] * len(args), o...  8.03 us
    ppermute x6, waiting for transfers between devices, hop(): return lax.ppermute(array, ('row', 'col'), pairs)  7.1 us
  transfers between devices with their start and end apart: 8, of which 6 were waited for; matrix products, arithmetic and copies ran while one was open for 0% of the time, Pallas kernels for 1%

profile of v3, /device:TPU:1, one launch (start us, length us, event | category | flops | bytes accessed | tf_op | source)
XLA Modules:
  0.0 106.9 jit_solution(8157518239407294661)
XLA Ops:
  0.6 0.0 copy-start
  0.6 1.7 %shard_map.59 = bf16[16,32,512]{2,1,0:T(8,128)(2,1)} custom-call(bf16[32,1024]{1,0:T(8,128)(2,1)} %bitcast.7), custom_call_target="tpu_custom_call" | custom-call | tf_op jit(solution)/shard_map/pallas_call | solution.py:25
  2.4 10.0 %all-to-all-start = ((bf16[16,32,512]{2,1,0:T(8,128)(2,1)}), bf16[16,32,512]{2,1,0:T(8,128)(2,1)S(1)}, u32[]{:S(2)}, u32[]{:S(2)}) async-start(bf16[16,32,512]{2,1,0:T(8,128)(2,1)} %shard_map.59), calls=%async_computation | async-start | bytes 1048576 | tf_op jit(solution)/shard_map/all_to_all | solution.py:259
  12.4 0.0 copy-done
  12.4 2.8 %collective-permute-start.1 = (bf16[32,512]{1,0:T(8,128)(2,1)S(1)}, bf16[32,512]{1,0:T(8,128)(2,1)S(1)}, u32[]{:S(2)}, u32[]{:S(2)}) collective-permute-start(bf16[32,512]{1,0:T(8,128)(2,1)S(1)} %copy-done), channel_id=1, source_target_pairs={{0,3},{1,0},{2,1},{3,2},{4,7},{5,4},{6,5},{7,6},{8,11},{9,8},{10,9... | collective-permute-start | bytes 98312 | tf_op jit(solution)/shard_map/ppermute | solution.py:249
  15.2 0.0 collective-permute-start
  15.2 1.6 %collective-permute-start.2 = (bf16[32,512]{1,0:T(8,128)(2,1)S(1)}, bf16[32,512]{1,0:T(8,128)(2,1)S(1)}, u32[]{:S(2)}, u32[]{:S(2)}) collective-permute-start(bf16[32,512]{1,0:T(8,128)(2,1)S(1)} %copy-done), channel_id=1, source_target_pairs={{0,2},{1,3},{2,0},{3,1},{4,6},{5,7},{6,4},{7,5},{8,10},{9,11},{10,... | collective-permute-start | bytes 98312 | tf_op jit(solution)/shard_map/ppermute | solution.py:249
  16.8 0.0 collective-permute-done.1.refs_2_
  16.8 2.6 %collective-permute-done.refs_1_ = bf16[32,512]{1,0:T(8,128)(2,1)S(1)} collective-permute-done((bf16[32,512]{1,0:T(8,128)(2,1)S(1)}, bf16[32,512]{1,0:T(8,128)(2,1)S(1)}, u32[]{:S(2)}, u32[]{:S(2)}) %collective-permute-start) | collective-permute-done | bytes 32800 | tf_op jit(solution)/shard_map/ppermute | solution.py:249
  19.5 0.0 collective-permute-done.2.refs_3_
  19.5 2.8 %collective-permute-start.5 = (bf16[4,32,512]{2,1,0:T(8,128)(2,1)S(1)}, bf16[4,32,512]{2,1,0:T(8,128)(2,1)S(1)}, u32[]{:S(2)}, u32[]{:S(2)}) collective-permute-start(bf16[4,32,512]{2,1,0:T(8,128)(2,1)S(1)} %shard_map.58.g0), channel_id=1, source_target_pairs={{0,8},{1,9},{2,10},{3,11},{4,12},{5,13},{6,14},{7,15},{8,0},{9,1},... | collective-permute-start | bytes 393224 | tf_op jit(solution)/shard_map/ppermute | solution.py:249
  22.4 0.9 collective-permute-start.4
  23.2 0.6 collective-permute-start.3
  23.8 1.2 %collective-permute-done.5.__3_.g3 = bf16[4,32,512]{2,1,0:T(8,128)(2,1)S(1)} collective-permute-done((bf16[4,32,512]{2,1,0:T(8,128)(2,1)S(1)}, bf16[4,32,512]{2,1,0:T(8,128)(2,1)S(1)}, u32[]{:S(2)}, u32[]{:S(2)}) %collective-permute-start.5) | collective-permute-done | bytes 131104 | tf_op jit(solution)/shard_map/ppermute | solution.py:249
  25.0 1.7 %collective-permute-done.4.__2_.g2 = bf16[4,32,512]{2,1,0:T(8,128)(2,1)S(1)} collective-permute-done((bf16[4,32,512]{2,1,0:T(8,128)(2,1)S(1)}, bf16[4,32,512]{2,1,0:T(8,128)(2,1)S(1)}, u32[]{:S(2)}, u32[]{:S(2)}) %collective-permute-start.4) | collective-permute-done | bytes 131104 | tf_op jit(solution)/shard_map/ppermute | solution.py:249
  26.7 1.5 %collective-permute-done.3.__1_.g1 = bf16[4,32,512]{2,1,0:T(8,128)(2,1)S(1)} collective-permute-done((bf16[4,32,512]{2,1,0:T(8,128)(2,1)S(1)}, bf16[4,32,512]{2,1,0:T(8,128)(2,1)S(1)}, u32[]{:S(2)}, u32[]{:S(2)}) %collective-permute-start.3) | collective-permute-done | bytes 131104 | tf_op jit(solution)/shard_map/ppermute | solution.py:249
  28.2 1.4 %all-to-all-done = bf16[16,32,512]{2,1,0:T(8,128)(2,1)S(1)} async-done(((bf16[16,32,512]{2,1,0:T(8,128)(2,1)}), bf16[16,32,512]{2,1,0:T(8,128)(2,1)S(1)}, u32[]{:S(2)}, u32[]{:S(2)}) %all-to-all-start) | async-done | bytes 524320 | tf_op jit(solution)/shard_map/all_to_all | solution.py:259
  29.7 1.6 %collective-permute-start.6 = (bf16[512,512]{1,0:T(8,128)(2,1)S(1)}, bf16[512,512]{1,0:T(8,128)(2,1)S(1)}, u32[]{:S(2)}, u32[]{:S(2)}) collective-permute-start(bf16[512,512]{1,0:T(8,128)(2,1)S(1)} %shard_map.60.data_ref.refs_3_), channel_id=1, source_target_pairs={{0,16},{16,0},{32,48},{48,32},{64,80},{80,64},{96,112},{112,96},{1... | collective-permute-start | bytes 1572872 | tf_op jit(solution)/shard_map/ppermute | solution.py:266
  31.3 0.6 shard_map.61
  31.9 0.0 copy-start.1
  31.9 1.0 collective-permute-done.6.data_ref.refs_4_
  32.9 0.5 shard_map.62.other_ref.refs_1_
  33.3 0.0 copy-done.1
  33.4 0.6 shard_map.63
  33.9 11.7 %all_to_all.30.refs_2_ = f32[16,4,128]{2,1,0:T(4,128)S(1)} all-to-all(f32[16,4,128]{2,1,0:T(4,128)S(1)} %shard_map.63), channel_id=1, replica_groups=mesh['row'=16,'col'=16] {'col'}, dimensions={0} | all-to-all | bytes 65536 | tf_op jit(solution)/shard_map/all_to_all | solution.py:285
  45.7 0.5 shard_map.64
  46.2 15.4 %all_to_all.31.refs_2_ = f32[16,8,128]{2,1,0:T(8,128)S(1)} all-to-all(f32[16,8,128]{2,1,0:T(8,128)S(1)} %shard_map.64), channel_id=1, replica_groups=mesh['row'=16,'col'=16] {'row'}, dimensions={0} | all-to-all | bytes 131072 | tf_op jit(solution)/shard_map/all_to_all | solution.py:292
  61.6 0.6 shard_map.65
  62.2 9.2 %all_to_all.32.refs_2_ = f32[16,4,128]{2,1,0:T(4,128)S(1)} all-to-all(f32[16,4,128]{2,1,0:T(4,128)S(1)} %shard_map.65), channel_id=1, replica_groups=mesh['row'=16,'col'=16] {'col'}, dimensions={0} | all-to-all | bytes 65536 | tf_op jit(solution)/shard_map/all_to_all | solution.py:285
  71.5 0.5 shard_map.66
  72.0 11.8 %all_to_all.33.refs_2_ = f32[16,8,128]{2,1,0:T(8,128)S(1)} all-to-all(f32[16,8,128]{2,1,0:T(8,128)S(1)} %shard_map.66), channel_id=1, replica_groups=mesh['row'=16,'col'=16] {'row'}, dimensions={0} | all-to-all | bytes 131072 | tf_op jit(solution)/shard_map/all_to_all | solution.py:292
  83.9 2.2 %shard_map.67 = (f32[8,128]{1,0:T(8,128)}, f32[16,136,128]{2,1,0:T(8,128)S(1)}) custom-call(f32[512,512]{1,0:T(8,128)S(1)} %get-tuple-element.9.own_ref.refs_0_, f32[512,512]{1,0:T(8,128)S(1)} %shard_map.62.other_ref.refs_1_, f32[16,8,128]{2,1,0:T(8,128)S(1)} %all_to_all.33.refs_2_, bf16[512,512]{1,0:T(8,128)(2,1)S(1)} %shard_map.60.data_ref.refs_3_, ...), custom_call_target="tpu_custom_call" | custom-call | tf_op jit(solution)/shard_map/pallas_call | solution.py:25
  86.1 20.1 %all_to_all.34.refs_0_ = f32[16,136,128]{2,1,0:T(8,128)S(1)} all-to-all(f32[16,136,128]{2,1,0:T(8,128)S(1)} %get-tuple-element.11), channel_id=1, replica_groups=mesh['row'=16,'col'=16] {'col'}, dimensions={0} | all-to-all | bytes 2228224 | tf_op jit(solution)/shard_map/all_to_all | solution.py:301
  106.2 0.8 shard_map.68
  (2 shorter events, 0.0 us)
Async XLA Ops:
  0.6 11.7 %copy-start = (bf16[32,512]{1,0:T(8,128)(2,1)S(1)}, bf16[32,512]{1,0:T(8,128)(2,1)}, u32[]{:S(2)}) copy-start(bf16[32,512]{1,0:T(8,128)(2,1)} %refs_0_.1) | copy-start | bytes 98308
  2.4 27.3 %all-to-all-start = ((bf16[16,32,512]{2,1,0:T(8,128)(2,1)}), bf16[16,32,512]{2,1,0:T(8,128)(2,1)S(1)}, u32[]{:S(2)}, u32[]{:S(2)}) async-start(bf16[16,32,512]{2,1,0:T(8,128)(2,1)} %shard_map.59), calls=%async_computation | async-start | bytes 1048576 | tf_op jit(solution)/shard_map/all_to_all | solution.py:259
  12.4 4.5 %collective-permute-start.1 = (bf16[32,512]{1,0:T(8,128)(2,1)S(1)}, bf16[32,512]{1,0:T(8,128)(2,1)S(1)}, u32[]{:S(2)}, u32[]{:S(2)}) collective-permute-start(bf16[32,512]{1,0:T(8,128)(2,1)S(1)} %copy-done), channel_id=1, source_target_pairs={{0,3},{1,0},{2,1},{3,2},{4,7},{5,4},{6,5},{7,6},{8,11},{9,8},{10,9... | collective-permute-start | bytes 98312 | tf_op jit(solution)/shard_map/ppermute | solution.py:249
  15.2 4.3 %collective-permute-start = (bf16[32,512]{1,0:T(8,128)(2,1)S(1)}, bf16[32,512]{1,0:T(8,128)(2,1)S(1)}, u32[]{:S(2)}, u32[]{:S(2)}) collective-permute-start(bf16[32,512]{1,0:T(8,128)(2,1)S(1)} %copy-done), channel_id=1, source_target_pairs={{0,1},{1,2},{2,3},{3,0},{4,5},{5,6},{6,7},{7,4},{8,9},{9,10},{10,1... | collective-permute-start | bytes 98312 | tf_op jit(solution)/shard_map/ppermute | solution.py:249
  15.2 4.3 %collective-permute-start.2 = (bf16[32,512]{1,0:T(8,128)(2,1)S(1)}, bf16[32,512]{1,0:T(8,128)(2,1)S(1)}, u32[]{:S(2)}, u32[]{:S(2)}) collective-permute-start(bf16[32,512]{1,0:T(8,128)(2,1)S(1)} %copy-done), channel_id=1, source_target_pairs={{0,2},{1,3},{2,0},{3,1},{4,6},{5,7},{6,4},{7,5},{8,10},{9,11},{10,... | collective-permute-start | bytes 98312 | tf_op jit(solution)/shard_map/ppermute | solution.py:249
  19.5 5.5 %collective-permute-start.5 = (bf16[4,32,512]{2,1,0:T(8,128)(2,1)S(1)}, bf16[4,32,512]{2,1,0:T(8,128)(2,1)S(1)}, u32[]{:S(2)}, u32[]{:S(2)}) collective-permute-start(bf16[4,32,512]{2,1,0:T(8,128)(2,1)S(1)} %shard_map.58.g0), channel_id=1, source_target_pairs={{0,8},{1,9},{2,10},{3,11},{4,12},{5,13},{6,14},{7,15},{8,0},{9,1},... | collective-permute-start | bytes 393224 | tf_op jit(solution)/shard_map/ppermute | solution.py:249
  22.4 4.4 %collective-permute-start.4 = (bf16[4,32,512]{2,1,0:T(8,128)(2,1)S(1)}, bf16[4,32,512]{2,1,0:T(8,128)(2,1)S(1)}, u32[]{:S(2)}, u32[]{:S(2)}) collective-permute-start(bf16[4,32,512]{2,1,0:T(8,128)(2,1)S(1)} %shard_map.58.g0), channel_id=1, source_target_pairs={{0,12},{1,13},{2,14},{3,15},{4,0},{5,1},{6,2},{7,3},{8,4},{9,5},{1... | collective-permute-start | bytes 393224 | tf_op jit(solution)/shard_map/ppermute | solution.py:249
  23.2 5.0 %collective-permute-start.3 = (bf16[4,32,512]{2,1,0:T(8,128)(2,1)S(1)}, bf16[4,32,512]{2,1,0:T(8,128)(2,1)S(1)}, u32[]{:S(2)}, u32[]{:S(2)}) collective-permute-start(bf16[4,32,512]{2,1,0:T(8,128)(2,1)S(1)} %shard_map.58.g0), channel_id=1, source_target_pairs={{0,4},{1,5},{2,6},{3,7},{4,8},{5,9},{6,10},{7,11},{8,12},{9,13},{1... | collective-permute-start | bytes 393224 | tf_op jit(solution)/shard_map/ppermute | solution.py:249
  29.7 3.2 %collective-permute-start.6 = (bf16[512,512]{1,0:T(8,128)(2,1)S(1)}, bf16[512,512]{1,0:T(8,128)(2,1)S(1)}, u32[]{:S(2)}, u32[]{:S(2)}) collective-permute-start(bf16[512,512]{1,0:T(8,128)(2,1)S(1)} %shard_map.60.data_ref.refs_3_), channel_id=1, source_target_pairs={{0,16},{16,0},{32,48},{48,32},{64,80},{80,64},{96,112},{112,96},{1... | collective-permute-start | bytes 1572872 | tf_op jit(solution)/shard_map/ppermute | solution.py:266
  31.9 1.5 %copy-start.1 = (f32[1024]{0:T(1024)S(1)}, f32[1024]{0:T(1024)}, u32[]{:S(2)}) copy-start(f32[1024]{0:T(1024)} %param.5) | copy-start | bytes 12292

commit v4 on v3

--- a/solution.py
+++ b/solution.py
@@ -13,7 +13,8 @@
 LN2 = math.log(2.0)
 SCALE = 1.0 / (EPS * LN2)
 LANES = 128
-OFFSETS = (0, 1, -1, 2)
+OFFSETS = (0, 2, 1, -1)
+STATS = 8
 
 
 def in_vmem(array):
@@ -169,13 +170,21 @@
     send_row_log_sums((own_ref, other_ref), lines, out_ref)
 
 
-def target_kernel(log_gen, own_ref, other_ref, got_ref, data_ref, more_ref, pot_ref, out_ref, high, low):
+def merged(refs):
+    stats = jnp.stack([ref[ref.shape[0] - STATS :, :] for ref in refs])
+    tops, totals = stats[:, : STATS // 2, :], stats[:, STATS // 2 :, :]
+    top = jnp.max(tops, axis=0)
+    factors = jnp.exp2(tops - top[None])
+    return top, jnp.sum(factors * totals, axis=0), factors
+
+
+def target_kernel(log_gen, own_ref, other_ref, got_ref, data_ref, more_ref, pot_ref, *refs):
+    *outs, sums_ref, high, low = refs
     gen_rows, half = own_ref.shape
-    receivers = out_ref.shape[0]
     chunks = gen_rows // LANES
     features = data_ref.shape[0]
-    feats = features // receivers
-    base = chunks * feats
+    side = len(outs)
+    feats = features // side**2
     pot = log_gen - log_sum(got_ref[...])
     pot_ref[...] = pot * (1.0 / SCALE)
     lines = halves(swap_halves(pot))
@@ -194,32 +203,58 @@
                 high[chunk(n), cols] = upper
                 low[chunk(n), cols] = (weights - upper.astype(jnp.float32)).astype(jnp.bfloat16)
             total = jnp.sum(total, axis=1, keepdims=True)
-            for place, column in ((base + n, top), (base + chunks + n, total)):
-                out_ref[:, place : place + 1, :] = jnp.broadcast_to(rows_to_lanes(column)[None], (receivers, 1, LANES))
+            for place, column in ((n, top), (chunks + n, total)):
+                line = rows_to_lanes(column)
+                for out_ref in outs:
+                    out_ref[side * chunks * feats + place, :] = line[0]
         rows = slice(first * LANES, (first + group) * LANES)
         sums = jnp.zeros((features, group * LANES), jnp.float32)
         for part, ref in enumerate((data_ref, more_ref)):
             cols = slice(part * half, (part + 1) * half)
             for piece in (high, low):
                 sums = sums + lax.dot_general(ref[...], piece[rows, cols], dims, preferred_element_type=jnp.float32)
-        for n in range(group):
-            out_ref[:, (first + n) * feats : (first + n + 1) * feats, :] = sums[:, chunk(n)].reshape(receivers, feats, LANES)
-
-
-def merge_kernel(log_data, got_ref, gen_pot_ref, target_ref):
+        sums_ref[:, rows] = sums
+    column, core = lax.axis_index("col"), lax.axis_index("row") % 2
+    for offset, out_ref in zip(OFFSETS, outs):
+        for second in range(side):
+            y = jnp.where(core == 0, second, (column // side + offset + side) % side)
+            x = jnp.where(core == 0, (column % side + offset + side) % side, second)
+            source = pl.ds(pl.multiple_of((y * side + x) * feats, feats), feats)
+            for n in range(chunks):
+                place = (second * chunks + n) * feats
+                out_ref[place : place + feats, :] = sums_ref[source, chunk(n)]
+
+
+def relay_kernel(*refs):
+    side = len(refs) // 2
+    got, outs = refs[:side], refs[side:]
+    top, total, factors = merged(got)
+    chunks = top.shape[0]
+    size = outs[0].shape[0] - STATS
+    feats = size // chunks
+    column, core = lax.axis_index("col"), lax.axis_index("row") % 2
+    place = jnp.where(core == 0, column // side, column % side)
+    for offset, out_ref in zip(OFFSETS, outs):
+        start = (place + offset + side) % side * size
+        for n in range(chunks):
+            source = pl.ds(pl.multiple_of(start + n * feats, feats), feats)
+            out_ref[n * feats : (n + 1) * feats, :] = sum(
+                ref[source, :] * factors[sender, n : n + 1, :] for sender, ref in enumerate(got)
+            )
+        out_ref[size : size + chunks, :] = top
+        out_ref[size + chunks :, :] = total
+
+
+def merge_kernel(log_data, *refs):
+    *got, gen_pot_ref, target_ref = refs
+    top, total, factors = merged(got)
     feats = target_ref.shape[0]
-    chunks = target_ref.shape[1] // LANES
-    base = chunks * feats
-    tops = got_ref[:, base : base + chunks, :]
-    totals = got_ref[:, base + chunks : base + 2 * chunks, :]
-    top = jnp.max(tops, axis=0)
-    factors = jnp.exp2(tops - top[None])
-    total = jnp.sum(factors * totals, axis=0)
     gen_pot_ref[...] = (log_data - (top + jnp.log2(total))) * (1.0 / SCALE)
     factors = factors / total[None]
-    for n in range(chunks):
-        piece = got_ref[:, n * feats : (n + 1) * feats, :]
-        target_ref[:, chunk(n)] = jnp.sum(piece * factors[:, n : n + 1, :], axis=0)
+    for n in range(top.shape[0]):
+        target_ref[:, chunk(n)] = sum(
+            ref[n * feats : (n + 1) * feats, :] * factors[sender, n : n + 1, :] for sender, ref in enumerate(got)
+        )
 
 
 def local(gen_points, data_points, data_potential):
@@ -292,17 +327,22 @@
         got = lax.all_to_all(lines, "row", 0, 0)
         if step < ITERS - 1:
             lines = kernel_call(at(row_kernel, log_gen), row_out, (*affinity, got))
-    potential, lines = kernel_call(
+    block_rows = gen_chunks * feats
+    potential, *blocks = kernel_call(
         at(target_kernel, log_gen),
-        (shaped((data_chunks, LANES), f32), shaped((cols_n, gen_chunks * (feats + 2), LANES), f32)),
+        (shaped((data_chunks, LANES), f32),) + (shaped((side * block_rows + STATS, LANES), f32),) * side,
         (*affinity, got, own, other),
-        scratch=[pltpu.VMEM((gen_rows, data_cols), dtype)] * 2,
-    )
-    got = lax.all_to_all(lines, "col", 0, 0)
+        scratch=[pltpu.VMEM((features, gen_rows), f32)] + [pltpu.VMEM((gen_rows, data_cols), dtype)] * 2,
+    )
+    blocks = kernel_call(
+        relay_kernel,
+        (shaped((block_rows + STATS, LANES), f32),) * side,
+        [blocks[0]] + [hop(block, 0, back) for block, back in zip(blocks[1:], OFFSETS[1:])],
+    )
     gen_pot, target = kernel_call(
         at(merge_kernel, log_data),
         (shaped((gen_chunks, LANES), f32), shaped((feats, gen_rows), f32)),
-        (got,),
+        [blocks[0]] + [hop(block, 1, back) for block, back in zip(blocks[1:], OFFSETS[1:])],
     )
     return (gen_pot.reshape(gen_rows), potential.reshape(data_cols), target)
 

time: 107 us -> 105 us (0.981); the launches traced: 107 us -> 104 us
  blocking collectives: 68.3 us -> 49.1 us
  waiting for transfers between devices: 9.51 us -> 17.6 us
  starting transfers between devices: 20.4 us -> 28.2 us
    all_to_all x3 -> x2, blocking collectives: 41 us -> 20.8 us  [local(): got = lax.all_to_all(lines, 'col', 0, 0)]
    ppermute x6 -> x12, waiting for transfers between devices: 7.1 us -> 15.7 us  [hop(): return lax.ppermute(array, ('row', 'col'), pairs)]
    ppermute x6 -> x12, starting transfers between devices: 8.75 us -> 16.4 us  [hop(): return lax.ppermute(array, ('row', 'col'), pairs)]
    pallas_call x11 -> x12, Pallas kernels: 8.03 us -> 8.08 us  [kernel_call(): pl.pallas_call(body, out_shape=out_shape, in_specs=[whole] * len(args), o...]
  transfers between devices with their start and end apart: 8 -> 14, of which waited for: 6 -> 10; matrix products, arithmetic and copies ran while one was open for 0% -> 0% of each run, Pallas kernels for 1% -> 1%
where the time goes in v4:
time: 105 us; the launch traced here: 104 us
  blocking collectives  49.1 us (47%)
  starting transfers between devices  28.2 us (27%)
  waiting for transfers between devices  17.6 us (17%)
  Pallas kernels  8.08 us (8%)
    all_to_all x2, blocking collectives, local(): got = lax.all_to_all(lines, 'row', 0, 0)  28.2 us
    all_to_all x2, blocking collectives, local(): got = lax.all_to_all(lines, 'col', 0, 0)  20.8 us
    ppermute x12, starting transfers between devices, hop(): return lax.ppermute(array, ('row', 'col'), pairs)  16.4 us
    ppermute x12, waiting for transfers between devices, hop(): return lax.ppermute(array, ('row', 'col'), pairs)  15.7 us
    all_to_all x1, starting transfers between devices, local(): own = lax.all_to_all(outgoing, 'row', 0, 0).reshape(features, half)  9.99 us
    pallas_call x12, Pallas kernels, kernel_call(): pl.pallas_call(body, out_shape=out_shape, in_specs=[whole] * len(args), o...  8.08 us
  transfers between devices with their start and end apart: 14, of which 10 were waited for; matrix products, arithmetic and copies ran while one was open for 0% of the time, Pallas kernels for 1%

profile of v4, /device:TPU:1, one launch (start us, length us, event | category | flops | bytes accessed | tf_op | source)
XLA Modules:
  0.0 103.8 jit_solution(5949296317271225079)
XLA Ops:
  0.6 1.7 %shard_map.59 = bf16[16,32,512]{2,1,0:T(8,128)(2,1)} custom-call(bf16[32,1024]{1,0:T(8,128)(2,1)} %bitcast.7), custom_call_target="tpu_custom_call" | custom-call | tf_op jit(solution)/shard_map/pallas_call | solution.py:26
  2.4 0.0 copy-start
  2.4 10.0 %all-to-all-start = ((bf16[16,32,512]{2,1,0:T(8,128)(2,1)}), bf16[16,32,512]{2,1,0:T(8,128)(2,1)S(1)}, u32[]{:S(2)}, u32[]{:S(2)}) async-start(bf16[16,32,512]{2,1,0:T(8,128)(2,1)} %shard_map.59), calls=%async_computation | async-start | bytes 1048576 | tf_op jit(solution)/shard_map/all_to_all | solution.py:294
  12.4 0.0 copy-done
  12.4 1.4 %collective-permute-start.1 = (bf16[32,512]{1,0:T(8,128)(2,1)S(1)}, bf16[32,512]{1,0:T(8,128)(2,1)S(1)}, u32[]{:S(2)}, u32[]{:S(2)}) collective-permute-start(bf16[32,512]{1,0:T(8,128)(2,1)S(1)} %copy-done), channel_id=1, source_target_pairs={{0,1},{1,2},{2,3},{3,0},{4,5},{5,6},{6,7},{7,4},{8,9},{9,10},{10,1... | collective-permute-start | bytes 98312 | tf_op jit(solution)/shard_map/ppermute | solution.py:284
  13.8 2.6 %collective-permute-start = (bf16[32,512]{1,0:T(8,128)(2,1)S(1)}, bf16[32,512]{1,0:T(8,128)(2,1)S(1)}, u32[]{:S(2)}, u32[]{:S(2)}) collective-permute-start(bf16[32,512]{1,0:T(8,128)(2,1)S(1)} %copy-done), channel_id=1, source_target_pairs={{0,2},{1,3},{2,0},{3,1},{4,6},{5,7},{6,4},{7,5},{8,10},{9,11},{10,... | collective-permute-start | bytes 98312 | tf_op jit(solution)/shard_map/ppermute | solution.py:284
  16.4 1.1 %collective-permute-start.2 = (bf16[32,512]{1,0:T(8,128)(2,1)S(1)}, bf16[32,512]{1,0:T(8,128)(2,1)S(1)}, u32[]{:S(2)}, u32[]{:S(2)}) collective-permute-start(bf16[32,512]{1,0:T(8,128)(2,1)S(1)} %copy-done), channel_id=1, source_target_pairs={{0,3},{1,0},{2,1},{3,2},{4,7},{5,4},{6,5},{7,6},{8,11},{9,8},{10,9... | collective-permute-start | bytes 98312 | tf_op jit(solution)/shard_map/ppermute | solution.py:284
  17.4 0.0 collective-permute-done.1.refs_2_
  17.4 0.9 collective-permute-done.refs_1_
  18.3 1.1 %collective-permute-done.2.refs_3_ = bf16[32,512]{1,0:T(8,128)(2,1)S(1)} collective-permute-done((bf16[32,512]{1,0:T(8,128)(2,1)S(1)}, bf16[32,512]{1,0:T(8,128)(2,1)S(1)}, u32[]{:S(2)}, u32[]{:S(2)}) %collective-permute-start.2) | collective-permute-done | bytes 32800 | tf_op jit(solution)/shard_map/ppermute | solution.py:284
  19.4 2.6 %collective-permute-start.5 = (bf16[4,32,512]{2,1,0:T(8,128)(2,1)S(1)}, bf16[4,32,512]{2,1,0:T(8,128)(2,1)S(1)}, u32[]{:S(2)}, u32[]{:S(2)}) collective-permute-start(bf16[4,32,512]{2,1,0:T(8,128)(2,1)S(1)} %shard_map.58.g0), channel_id=1, source_target_pairs={{0,12},{1,13},{2,14},{3,15},{4,0},{5,1},{6,2},{7,3},{8,4},{9,5},{1... | collective-permute-start | bytes 393224 | tf_op jit(solution)/shard_map/ppermute | solution.py:284
  22.0 0.0 collective-permute-start.4
  22.0 1.7 %collective-permute-start.3 = (bf16[4,32,512]{2,1,0:T(8,128)(2,1)S(1)}, bf16[4,32,512]{2,1,0:T(8,128)(2,1)S(1)}, u32[]{:S(2)}, u32[]{:S(2)}) collective-permute-start(bf16[4,32,512]{2,1,0:T(8,128)(2,1)S(1)} %shard_map.58.g0), channel_id=1, source_target_pairs={{0,8},{1,9},{2,10},{3,11},{4,12},{5,13},{6,14},{7,15},{8,0},{9,1},... | collective-permute-start | bytes 393224 | tf_op jit(solution)/shard_map/ppermute | solution.py:284
  23.7 0.2 collective-permute-done.5.__3_.g3
  24.0 4.8 %collective-permute-done.4.__2_.g2 = bf16[4,32,512]{2,1,0:T(8,128)(2,1)S(1)} collective-permute-done((bf16[4,32,512]{2,1,0:T(8,128)(2,1)S(1)}, bf16[4,32,512]{2,1,0:T(8,128)(2,1)S(1)}, u32[]{:S(2)}, u32[]{:S(2)}) %collective-permute-start.4) | collective-permute-done | bytes 131104 | tf_op jit(solution)/shard_map/ppermute | solution.py:284
  28.7 0.0 collective-permute-done.3.__1_.g1
  28.7 1.0 all-to-all-done
  29.7 1.8 %collective-permute-start.6 = (bf16[512,512]{1,0:T(8,128)(2,1)S(1)}, bf16[512,512]{1,0:T(8,128)(2,1)S(1)}, u32[]{:S(2)}, u32[]{:S(2)}) collective-permute-start(bf16[512,512]{1,0:T(8,128)(2,1)S(1)} %shard_map.60.data_ref.refs_3_), channel_id=1, source_target_pairs={{0,16},{16,0},{32,48},{48,32},{64,80},{80,64},{96,112},{112,96},{1... | collective-permute-start | bytes 1572872 | tf_op jit(solution)/shard_map/ppermute | solution.py:301
  31.5 0.5 shard_map.61
  32.0 1.0 collective-permute-done.6.data_ref.refs_4_
  33.0 0.0 copy-start.1
  33.0 0.5 shard_map.62.other_ref.refs_1_
  33.5 0.2 copy-done.1
  33.7 0.6 shard_map.63
  34.3 11.6 %all_to_all.25.refs_2_ = f32[16,4,128]{2,1,0:T(4,128)S(1)} all-to-all(f32[16,4,128]{2,1,0:T(4,128)S(1)} %shard_map.63), channel_id=1, replica_groups=mesh['row'=16,'col'=16] {'col'}, dimensions={0} | all-to-all | bytes 65536 | tf_op jit(solution)/shard_map/all_to_all | solution.py:320
  45.9 0.5 shard_map.64
  46.4 16.4 %all_to_all.26.refs_2_ = f32[16,8,128]{2,1,0:T(8,128)S(1)} all-to-all(f32[16,8,128]{2,1,0:T(8,128)S(1)} %shard_map.64), channel_id=1, replica_groups=mesh['row'=16,'col'=16] {'row'}, dimensions={0} | all-to-all | bytes 131072 | tf_op jit(solution)/shard_map/all_to_all | solution.py:327
  62.8 0.6 shard_map.65
  63.4 9.2 %all_to_all.27.refs_2_ = f32[16,4,128]{2,1,0:T(4,128)S(1)} all-to-all(f32[16,4,128]{2,1,0:T(4,128)S(1)} %shard_map.65), channel_id=1, replica_groups=mesh['row'=16,'col'=16] {'col'}, dimensions={0} | all-to-all | bytes 65536 | tf_op jit(solution)/shard_map/all_to_all | solution.py:320
  72.7 0.5 shard_map.66
  73.2 11.8 %all_to_all.28.refs_2_ = f32[16,8,128]{2,1,0:T(8,128)S(1)} all-to-all(f32[16,8,128]{2,1,0:T(8,128)S(1)} %shard_map.66), channel_id=1, replica_groups=mesh['row'=16,'col'=16] {'row'}, dimensions={0} | all-to-all | bytes 131072 | tf_op jit(solution)/shard_map/all_to_all | solution.py:327
  85.1 2.3 %shard_map.67 = (f32[8,128]{1,0:T(8,128)}, f32[520,128]{1,0:T(8,128)S(1)}, f32[520,128]{1,0:T(8,128)S(1)}, f32[520,128]{1,0:T(8,128)S(1)}, f32[520,128]{1,0:T(8,128)S(1)}) custom-call(f32[512,512]{1,0:T(8,128)S(1)} %get-tuple-element.16.own_ref.refs_0_, f32[512,512]{1,0:T(8,128)S(1)} %shard_map.62.other_ref.refs_1_, f32[16,8,128]{2,1,0:T(8,128)S(1)} %all_to_all.28.refs_2_, ...), custom_call_target="tpu_custom_call" | custom-call | tf_op jit(solution)/shard_map/pallas_call | solution.py:26
  87.3 0.9 collective-permute-start.7
  88.2 0.6 collective-permute-start.8
  88.8 2.1 %collective-permute-start.9 = (f32[520,128]{1,0:T(8,128)S(1)}, f32[520,128]{1,0:T(8,128)S(1)}, u32[]{:S(2)}, u32[]{:S(2)}) collective-permute-start(f32[520,128]{1,0:T(8,128)S(1)} %get-tuple-element.21), channel_id=1, source_target_pairs={{0,3},{1,0},{2,1},{3,2},{4,7},{5,4},{6,5},{7,6},{8,11},{9,8},{10,9... | collective-permute-start | bytes 798728 | tf_op jit(solution)/shard_map/ppermute | solution.py:284
  90.9 3.5 %collective-permute-done.7.refs_1_ = f32[520,128]{1,0:T(8,128)S(1)} collective-permute-done((f32[520,128]{1,0:T(8,128)S(1)}, f32[520,128]{1,0:T(8,128)S(1)}, u32[]{:S(2)}, u32[]{:S(2)}) %collective-permute-start.7) | collective-permute-done | bytes 266272 | tf_op jit(solution)/shard_map/ppermute | solution.py:284
  94.4 2.8 %collective-permute-done.8.refs_2_ = f32[520,128]{1,0:T(8,128)S(1)} collective-permute-done((f32[520,128]{1,0:T(8,128)S(1)}, f32[520,128]{1,0:T(8,128)S(1)}, u32[]{:S(2)}, u32[]{:S(2)}) %collective-permute-start.8) | collective-permute-done | bytes 266272 | tf_op jit(solution)/shard_map/ppermute | solution.py:284
  97.2 0.0 collective-permute-done.9.refs_3_
  97.2 0.1 shard_map.68
  97.4 0.8 collective-permute-start.10
  98.1 0.8 collective-permute-start.11
  98.9 1.9 %collective-permute-start.12 = (f32[136,128]{1,0:T(8,128)S(1)}, f32[136,128]{1,0:T(8,128)S(1)}, u32[]{:S(2)}, u32[]{:S(2)}) collective-permute-start(f32[136,128]{1,0:T(8,128)S(1)} %get-tuple-element.25), channel_id=1, source_target_pairs={{0,12},{1,13},{2,14},{3,15},{4,0},{5,1},{6,2},{7,3},{8,4},{9,5},{1... | collective-permute-start | bytes 208904 | tf_op jit(solution)/shard_map/ppermute | solution.py:284
  100.8 1.3 %collective-permute-done.10.refs_1_ = f32[136,128]{1,0:T(8,128)S(1)} collective-permute-done((f32[136,128]{1,0:T(8,128)S(1)}, f32[136,128]{1,0:T(8,128)S(1)}, u32[]{:S(2)}, u32[]{:S(2)}) %collective-permute-start.10) | collective-permute-done | bytes 69664 | tf_op jit(solution)/shard_map/ppermute | solution.py:284
  102.2 1.0 collective-permute-done.11.refs_2_
  103.2 0.0 collective-permute-done.12.refs_3_
  103.2 0.7 shard_map.69
  (2 shorter events, 0.0 us)
Async XLA Ops:
  2.4 10.0 %copy-start = (bf16[32,512]{1,0:T(8,128)(2,1)S(1)}, bf16[32,512]{1,0:T(8,128)(2,1)}, u32[]{:S(2)}) copy-start(bf16[32,512]{1,0:T(8,128)(2,1)} %refs_0_.1) | copy-start | bytes 98308
  2.4 27.3 %all-to-all-start = ((bf16[16,32,512]{2,1,0:T(8,128)(2,1)}), bf16[16,32,512]{2,1,0:T(8,128)(2,1)S(1)}, u32[]{:S(2)}, u32[]{:S(2)}) async-start(bf16[16,32,512]{2,1,0:T(8,128)(2,1)} %shard_map.59), calls=%async_computation | async-start | bytes 1048576 | tf_op jit(solution)/shard_map/all_to_all | solution.py:294
  12.4 5.1 %collective-permute-start.1 = (bf16[32,512]{1,0:T(8,128)(2,1)S(1)}, bf16[32,512]{1,0:T(8,128)(2,1)S(1)}, u32[]{:S(2)}, u32[]{:S(2)}) collective-permute-start(bf16[32,512]{1,0:T(8,128)(2,1)S(1)} %copy-done), channel_id=1, source_target_pairs={{0,1},{1,2},{2,3},{3,0},{4,5},{5,6},{6,7},{7,4},{8,9},{9,10},{10,1... | collective-permute-start | bytes 98312 | tf_op jit(solution)/shard_map/ppermute | solution.py:284
  13.8 4.6 %collective-permute-start = (bf16[32,512]{1,0:T(8,128)(2,1)S(1)}, bf16[32,512]{1,0:T(8,128)(2,1)S(1)}, u32[]{:S(2)}, u32[]{:S(2)}) collective-permute-start(bf16[32,512]{1,0:T(8,128)(2,1)S(1)} %copy-done), channel_id=1, source_target_pairs={{0,2},{1,3},{2,0},{3,1},{4,6},{5,7},{6,4},{7,5},{8,10},{9,11},{10,... | collective-permute-start | bytes 98312 | tf_op jit(solution)/shard_map/ppermute | solution.py:284
  16.4 3.1 %collective-permute-start.2 = (bf16[32,512]{1,0:T(8,128)(2,1)S(1)}, bf16[32,512]{1,0:T(8,128)(2,1)S(1)}, u32[]{:S(2)}, u32[]{:S(2)}) collective-permute-start(bf16[32,512]{1,0:T(8,128)(2,1)S(1)} %copy-done), channel_id=1, source_target_pairs={{0,3},{1,0},{2,1},{3,2},{4,7},{5,4},{6,5},{7,6},{8,11},{9,8},{10,9... | collective-permute-start | bytes 98312 | tf_op jit(solution)/shard_map/ppermute | solution.py:284
  19.4 4.5 %collective-permute-start.5 = (bf16[4,32,512]{2,1,0:T(8,128)(2,1)S(1)}, bf16[4,32,512]{2,1,0:T(8,128)(2,1)S(1)}, u32[]{:S(2)}, u32[]{:S(2)}) collective-permute-start(bf16[4,32,512]{2,1,0:T(8,128)(2,1)S(1)} %shard_map.58.g0), channel_id=1, source_target_pairs={{0,12},{1,13},{2,14},{3,15},{4,0},{5,1},{6,2},{7,3},{8,4},{9,5},{1... | collective-permute-start | bytes 393224 | tf_op jit(solution)/shard_map/ppermute | solution.py:284
  22.0 6.7 %collective-permute-start.4 = (bf16[4,32,512]{2,1,0:T(8,128)(2,1)S(1)}, bf16[4,32,512]{2,1,0:T(8,128)(2,1)S(1)}, u32[]{:S(2)}, u32[]{:S(2)}) collective-permute-start(bf16[4,32,512]{2,1,0:T(8,128)(2,1)S(1)} %shard_map.58.g0), channel_id=1, source_target_pairs={{0,4},{1,5},{2,6},{3,7},{4,8},{5,9},{6,10},{7,11},{8,12},{9,13},{1... | collective-permute-start | bytes 393224 | tf_op jit(solution)/shard_map/ppermute | solution.py:284
  22.0 6.7 %collective-permute-start.3 = (bf16[4,32,512]{2,1,0:T(8,128)(2,1)S(1)}, bf16[4,32,512]{2,1,0:T(8,128)(2,1)S(1)}, u32[]{:S(2)}, u32[]{:S(2)}) collective-permute-start(bf16[4,32,512]{2,1,0:T(8,128)(2,1)S(1)} %shard_map.58.g0), channel_id=1, source_target_pairs={{0,8},{1,9},{2,10},{3,11},{4,12},{5,13},{6,14},{7,15},{8,0},{9,1},... | collective-permute-start | bytes 393224 | tf_op jit(solution)/shard_map/ppermute | solution.py:284
  29.7 3.3 %collective-permute-start.6 = (bf16[512,512]{1,0:T(8,128)(2,1)S(1)}, bf16[512,512]{1,0:T(8,128)(2,1)S(1)}, u32[]{:S(2)}, u32[]{:S(2)}) collective-permute-start(bf16[512,512]{1,0:T(8,128)(2,1)S(1)} %shard_map.60.data_ref.refs_3_), channel_id=1, source_target_pairs={{0,16},{16,0},{32,48},{48,32},{64,80},{80,64},{96,112},{112,96},{1... | collective-permute-start | bytes 1572872 | tf_op jit(solution)/shard_map/ppermute | solution.py:301
  33.0 0.7 copy-start.1
  87.3 7.1 %collective-permute-start.7 = (f32[520,128]{1,0:T(8,128)S(1)}, f32[520,128]{1,0:T(8,128)S(1)}, u32[]{:S(2)}, u32[]{:S(2)}) collective-permute-start(f32[520,128]{1,0:T(8,128)S(1)} %get-tuple-element.19), channel_id=1, source_target_pairs={{0,2},{1,3},{2,0},{3,1},{4,6},{5,7},{6,4},{7,5},{8,10},{9,11},{10,... | collective-permute-start | bytes 798728 | tf_op jit(solution)/shard_map/ppermute | solution.py:284
  88.2 9.0 %collective-permute-start.8 = (f32[520,128]{1,0:T(8,128)S(1)}, f32[520,128]{1,0:T(8,128)S(1)}, u32[]{:S(2)}, u32[]{:S(2)}) collective-permute-start(f32[520,128]{1,0:T(8,128)S(1)} %get-tuple-element.20), channel_id=1, source_target_pairs={{0,1},{1,2},{2,3},{3,0},{4,5},{5,6},{6,7},{7,4},{8,9},{9,10},{10,1... | collective-permute-start | bytes 798728 | tf_op jit(solution)/shard_map/ppermute | solution.py:284
  88.8 8.5 %collective-permute-start.9 = (f32[520,128]{1,0:T(8,128)S(1)}, f32[520,128]{1,0:T(8,128)S(1)}, u32[]{:S(2)}, u32[]{:S(2)}) collective-permute-start(f32[520,128]{1,0:T(8,128)S(1)} %get-tuple-element.21), channel_id=1, source_target_pairs={{0,3},{1,0},{2,1},{3,2},{4,7},{5,4},{6,5},{7,6},{8,11},{9,8},{10,9... | collective-permute-start | bytes 798728 | tf_op jit(solution)/shard_map/ppermute | solution.py:284
  97.4 4.8 %collective-permute-start.10 = (f32[136,128]{1,0:T(8,128)S(1)}, f32[136,128]{1,0:T(8,128)S(1)}, u32[]{:S(2)}, u32[]{:S(2)}) collective-permute-start(f32[136,128]{1,0:T(8,128)S(1)} %get-tuple-element.23), channel_id=1, source_target_pairs={{0,8},{1,9},{2,10},{3,11},{4,12},{5,13},{6,14},{7,15},{8,0},{9,1},... | collective-permute-start | bytes 208904 | tf_op jit(solution)/shard_map/ppermute | solution.py:284
  98.1 5.0 %collective-permute-start.11 = (f32[136,128]{1,0:T(8,128)S(1)}, f32[136,128]{1,0:T(8,128)S(1)}, u32[]{:S(2)}, u32[]{:S(2)}) collective-permute-start(f32[136,128]{1,0:T(8,128)S(1)} %get-tuple-element.24), channel_id=1, source_target_pairs={{0,4},{1,5},{2,6},{3,7},{4,8},{5,9},{6,10},{7,11},{8,12},{9,13},{1... | collective-permute-start | bytes 208904 | tf_op jit(solution)/shard_map/ppermute | solution.py:284
  98.9 4.2 %collective-permute-start.12 = (f32[136,128]{1,0:T(8,128)S(1)}, f32[136,128]{1,0:T(8,128)S(1)}, u32[]{:S(2)}, u32[]{:S(2)}) collective-permute-start(f32[136,128]{1,0:T(8,128)S(1)} %get-tuple-element.25), channel_id=1, source_target_pairs={{0,12},{1,13},{2,14},{3,15},{4,0},{5,1},{6,2},{7,3},{8,4},{9,5},{1... | collective-permute-start | bytes 208904 | tf_op jit(solution)/shard_map/ppermute | solution.py:284

commit v5 on v4

--- a/solution.py
+++ b/solution.py
@@ -65,13 +65,10 @@
     return [chunks_to_line(chunks[:half]), chunks_to_line(chunks[half:])]
 
 
-def send_row_log_sums(refs, lines, out_ref):
-    for n in range(refs[0].shape[0] // LANES):
-        tiles = [ref[chunk(n), :] + line for ref, line in zip(refs, lines)]
-        top = jnp.max(functools.reduce(jnp.maximum, tiles), axis=1, keepdims=True)
-        total = jnp.sum(sum(jnp.exp2(tile - top) for tile in tiles), axis=1, keepdims=True)
-        line = rows_to_lanes(top + jnp.log2(total))
-        out_ref[:, n : n + 1, :] = jnp.broadcast_to(line[None], (out_ref.shape[0], 1, LANES))
+def row_log_sums(tiles):
+    top = jnp.max(functools.reduce(jnp.maximum, tiles), axis=1, keepdims=True)
+    total = jnp.sum(sum(jnp.exp2(tile - top) for tile in tiles), axis=1, keepdims=True)
+    return rows_to_lanes(top + jnp.log2(total))
 
 
 def layout_kernel(data_ref, out_ref, held, sems):
@@ -111,7 +108,7 @@
         yield chunk(n), (2.0 * cross - (gen_sq + data_sq)) * (SCALE / gen.shape[1])
 
 
-def own_kernel(g0, g1, g2, g3, data_ref, gen_ref, affinity_ref):
+def own_kernel(g0, g1, g2, g3, data_ref, pot_ref, gen_ref, affinity_ref, log_ref):
     side, size = g0.shape[:2]
     column, core = lax.axis_index("col"), lax.axis_index("row") % 2
     for second, ref in zip(OFFSETS, (g0, g1, g2, g3)):
@@ -120,8 +117,10 @@
             x_back = jnp.where(core == 0, first, second)
             place = (column // side - y_back + side) % side * side + (column % side - x_back + side) % side
             gen_ref[pl.ds(pl.multiple_of(place * size, size), size), :] = ref[n, :, :]
-    for rows, tile in affinity_chunks(gen_ref, data_ref):
+    line = halves(swap_halves(pot_ref[...] * SCALE))[0]
+    for n, (rows, tile) in enumerate(affinity_chunks(gen_ref, data_ref)):
         affinity_ref[rows, :] = tile
+        log_ref[n : n + 1, :] = row_log_sums([tile + line])
 
 
 def other_kernel(gen_ref, data_ref, affinity_ref):
@@ -129,8 +128,11 @@
         affinity_ref[rows, :] = tile
 
 
-def first_kernel(own_ref, other_ref, pot_ref, out_ref):
-    send_row_log_sums((own_ref, other_ref), halves(swap_halves(pot_ref[...] * SCALE)), out_ref)
+def first_kernel(other_ref, pot_ref, log_ref, out_ref):
+    line = halves(swap_halves(pot_ref[...] * SCALE))[1]
+    for n in range(other_ref.shape[0] // LANES):
+        logs = log_sum(jnp.stack([log_ref[n : n + 1, :], row_log_sums([other_ref[chunk(n), :] + line])]))
+        out_ref[:, n : n + 1, :] = jnp.broadcast_to(logs[None], (out_ref.shape[0], 1, LANES))
 
 
 def swap_halves(chunks):
@@ -167,7 +169,9 @@
 
 def row_kernel(log_gen, own_ref, other_ref, got_ref, out_ref):
     lines = halves(swap_halves(log_gen - log_sum(got_ref[...])))
-    send_row_log_sums((own_ref, other_ref), lines, out_ref)
+    for n in range(own_ref.shape[0] // LANES):
+        logs = row_log_sums([ref[chunk(n), :] + line for ref, line in zip((own_ref, other_ref), lines)])
+        out_ref[:, n : n + 1, :] = jnp.broadcast_to(logs[None], (out_ref.shape[0], 1, LANES))
 
 
 def merged(refs):
@@ -178,20 +182,45 @@
     return top, jnp.sum(factors * totals, axis=0), factors
 
 
+def add_blocks(offsets, data_refs, pieces, rows, out_refs):
+    side = len(OFFSETS)
+    feats = data_refs[0].shape[0] // side**2
+    half = data_refs[0].shape[1]
+    column, core = lax.axis_index("col"), lax.axis_index("row") % 2
+    sources = []
+    for offset in offsets:
+        for second in range(side):
+            y = jnp.where(core == 0, second, (column // side + offset + side) % side)
+            x = jnp.where(core == 0, (column % side + offset + side) % side, second)
+            sources.append(pl.ds(pl.multiple_of((y * side + x) * feats, feats), feats))
+    dims = (((1,), (1,)), ((), ()))
+    sums = 0.0
+    for part, ref in enumerate(data_refs):
+        data = jnp.concatenate([ref[source, :] for source in sources], axis=0)
+        cols = slice(part * half, (part + 1) * half)
+        for piece in pieces:
+            sums = sums + lax.dot_general(data, piece[rows, cols], dims, preferred_element_type=jnp.float32)
+    chunks = pieces[0].shape[0] // LANES
+    for place in range(len(sources)):
+        out_ref, second = out_refs[place // side], place % side
+        for n in range(rows.start // LANES, rows.stop // LANES):
+            lines = sums[place * feats : (place + 1) * feats, n * LANES - rows.start : (n + 1) * LANES - rows.start]
+            start = (second * chunks + n) * feats
+            out_ref[start : start + feats, :] = lines
+
+
+GROUP = 2 * LANES
+
+
 def target_kernel(log_gen, own_ref, other_ref, got_ref, data_ref, more_ref, pot_ref, *refs):
-    *outs, sums_ref, high, low = refs
+    *outs, stats_ref, high, low = refs
     gen_rows, half = own_ref.shape
     chunks = gen_rows // LANES
-    features = data_ref.shape[0]
-    side = len(outs)
-    feats = features // side**2
     pot = log_gen - log_sum(got_ref[...])
     pot_ref[...] = pot * (1.0 / SCALE)
     lines = halves(swap_halves(pot))
-    dims = (((1,), (1,)), ((), ()))
-    group = 2
-    for first in range(0, chunks, group):
-        for n in range(first, first + group):
+    for first in range(0, gen_rows, GROUP):
+        for n in range(first // LANES, (first + GROUP) // LANES):
             tiles = [ref[chunk(n), :] + line for ref, line in zip((own_ref, other_ref), lines)]
             top = jnp.max(jnp.maximum(*tiles), axis=1, keepdims=True)
             total = 0.0
@@ -204,25 +233,10 @@
                 low[chunk(n), cols] = (weights - upper.astype(jnp.float32)).astype(jnp.bfloat16)
             total = jnp.sum(total, axis=1, keepdims=True)
             for place, column in ((n, top), (chunks + n, total)):
-                line = rows_to_lanes(column)
-                for out_ref in outs:
-                    out_ref[side * chunks * feats + place, :] = line[0]
-        rows = slice(first * LANES, (first + group) * LANES)
-        sums = jnp.zeros((features, group * LANES), jnp.float32)
-        for part, ref in enumerate((data_ref, more_ref)):
-            cols = slice(part * half, (part + 1) * half)
-            for piece in (high, low):
-                sums = sums + lax.dot_general(ref[...], piece[rows, cols], dims, preferred_element_type=jnp.float32)
-        sums_ref[:, rows] = sums
-    column, core = lax.axis_index("col"), lax.axis_index("row") % 2
-    for offset, out_ref in zip(OFFSETS, outs):
-        for second in range(side):
-            y = jnp.where(core == 0, second, (column // side + offset + side) % side)
-            x = jnp.where(core == 0, (column % side + offset + side) % side, second)
-            source = pl.ds(pl.multiple_of((y * side + x) * feats, feats), feats)
-            for n in range(chunks):
-                place = (second * chunks + n) * feats
-                out_ref[place : place + feats, :] = sums_ref[source, chunk(n)]
+                stats_ref[place : place + 1, :] = rows_to_lanes(column)
+        add_blocks(OFFSETS, (data_ref, more_ref), (high, low), slice(first, first + GROUP), outs)
+    for out_ref in outs:
+        out_ref[out_ref.shape[0] - STATS :, :] = stats_ref[...]
 
 
 def relay_kernel(*refs):
@@ -307,15 +321,14 @@
     def at(body, number):
         return lambda *refs: body(number, *refs)
 
-    gen, own_affinity = kernel_call(
+    gen, own_affinity, logs = kernel_call(
         own_kernel,
-        (pltpu.VMEM((gen_rows, features), dtype), block),
-        (*stacks, own),
+        (pltpu.VMEM((gen_rows, features), dtype), block, pltpu.VMEM((gen_chunks, LANES), f32)),
+        (*stacks, own, start),
         flops=2 * gen_rows * half * features,
     )
-    own_affinity = in_vmem(own_affinity)
-    affinity = (own_affinity, in_vmem(kernel_call(other_kernel, block, (gen, other))))
-    lines = kernel_call(first_kernel, row_out, (*affinity, start))
+    affinity = (in_vmem(own_affinity), in_vmem(kernel_call(other_kernel, block, (gen, other))))
+    lines = kernel_call(first_kernel, row_out, (affinity[1], start, in_vmem(logs)))
     for step in range(ITERS):
         got = lax.all_to_all(lines, "col", 0, 0)
         lines = kernel_call(
@@ -328,11 +341,12 @@
         if step < ITERS - 1:
             lines = kernel_call(at(row_kernel, log_gen), row_out, (*affinity, got))
     block_rows = gen_chunks * feats
+    sent = pltpu.VMEM((side * block_rows + STATS, LANES), f32)
     potential, *blocks = kernel_call(
         at(target_kernel, log_gen),
-        (shaped((data_chunks, LANES), f32),) + (shaped((side * block_rows + STATS, LANES), f32),) * side,
+        (pltpu.VMEM((data_chunks, LANES), f32),) + (sent,) * side,
         (*affinity, got, own, other),
-        scratch=[pltpu.VMEM((features, gen_rows), f32)] + [pltpu.VMEM((gen_rows, data_cols), dtype)] * 2,
+        scratch=[pltpu.VMEM((STATS, LANES), f32)] + [pltpu.VMEM((gen_rows, data_cols), dtype)] * 2,
     )
     blocks = kernel_call(
         relay_kernel,

time: 105 us -> 104 us (level)
  transfers between devices with their start and end apart: 14 -> 14, of which waited for: 10 -> 10; matrix products, arithmetic and copies ran while one was open for 0% -> 1% of each run, Pallas kernels for 1% -> 1%
where the time goes in v5:
time: 104 us; the launch traced here: 103 us
  blocking collectives  49.1 us (47%)
  starting transfers between devices  28.3 us (27%)
  waiting for transfers between devices  16.6 us (16%)
  Pallas kernels  7.86 us (8%)
    all_to_all x2, blocking collectives, local(): got = lax.all_to_all(lines, 'row', 0, 0)  28.2 us
    all_to_all x2, blocking collectives, local(): got = lax.all_to_all(lines, 'col', 0, 0)  20.8 us
    ppermute x12, starting transfers between devices, hop(): return lax.ppermute(array, ('row', 'col'), pairs)  16.5 us
    ppermute x12, waiting for transfers between devices, hop(): return lax.ppermute(array, ('row', 'col'), pairs)  15.1 us
    all_to_all x1, starting transfers between devices, local(): own = lax.all_to_all(outgoing, 'row', 0, 0).reshape(features, half)  9.99 us
    pallas_call x12, Pallas kernels, kernel_call(): pl.pallas_call(body, out_shape=out_shape, in_specs=[whole] * len(args), o...  7.86 us
  transfers between devices with their start and end apart: 14, of which 10 were waited for; matrix products, arithmetic and copies ran while one was open for 1% of the time, Pallas kernels for 1%

profile of v5, /device:TPU:1, one launch (start us, length us, event | category | flops | bytes accessed | tf_op | source)
XLA Modules:
  0.0 103.1 jit_solution(51578819867147481)
XLA Ops:
  0.6 1.7 %shard_map.59 = bf16[16,32,512]{2,1,0:T(8,128)(2,1)} custom-call(bf16[32,1024]{1,0:T(8,128)(2,1)} %bitcast.9), custom_call_target="tpu_custom_call" | custom-call | tf_op jit(solution)/shard_map/pallas_call | solution.py:26
  2.4 0.0 copy-start
  2.4 10.0 %all-to-all-start = ((bf16[16,32,512]{2,1,0:T(8,128)(2,1)}), bf16[16,32,512]{2,1,0:T(8,128)(2,1)S(1)}, u32[]{:S(2)}, u32[]{:S(2)}) async-start(bf16[16,32,512]{2,1,0:T(8,128)(2,1)} %shard_map.59), calls=%async_computation | async-start | bytes 1048576 | tf_op jit(solution)/shard_map/all_to_all | solution.py:308
  12.4 0.0 copy-done
  12.4 1.4 %collective-permute-start.1 = (bf16[32,512]{1,0:T(8,128)(2,1)S(1)}, bf16[32,512]{1,0:T(8,128)(2,1)S(1)}, u32[]{:S(2)}, u32[]{:S(2)}) collective-permute-start(bf16[32,512]{1,0:T(8,128)(2,1)S(1)} %copy-done), channel_id=1, source_target_pairs={{0,1},{1,2},{2,3},{3,0},{4,5},{5,6},{6,7},{7,4},{8,9},{9,10},{10,1... | collective-permute-start | bytes 98312 | tf_op jit(solution)/shard_map/ppermute | solution.py:298
  13.8 2.6 %collective-permute-start = (bf16[32,512]{1,0:T(8,128)(2,1)S(1)}, bf16[32,512]{1,0:T(8,128)(2,1)S(1)}, u32[]{:S(2)}, u32[]{:S(2)}) collective-permute-start(bf16[32,512]{1,0:T(8,128)(2,1)S(1)} %copy-done), channel_id=1, source_target_pairs={{0,2},{1,3},{2,0},{3,1},{4,6},{5,7},{6,4},{7,5},{8,10},{9,11},{10,... | collective-permute-start | bytes 98312 | tf_op jit(solution)/shard_map/ppermute | solution.py:298
  16.4 1.1 %collective-permute-start.2 = (bf16[32,512]{1,0:T(8,128)(2,1)S(1)}, bf16[32,512]{1,0:T(8,128)(2,1)S(1)}, u32[]{:S(2)}, u32[]{:S(2)}) collective-permute-start(bf16[32,512]{1,0:T(8,128)(2,1)S(1)} %copy-done), channel_id=1, source_target_pairs={{0,3},{1,0},{2,1},{3,2},{4,7},{5,4},{6,5},{7,6},{8,11},{9,8},{10,9... | collective-permute-start | bytes 98312 | tf_op jit(solution)/shard_map/ppermute | solution.py:298
  17.4 0.0 collective-permute-done.1.refs_2_
  17.4 0.9 collective-permute-done.refs_1_
  18.3 1.1 %collective-permute-done.2.refs_3_ = bf16[32,512]{1,0:T(8,128)(2,1)S(1)} collective-permute-done((bf16[32,512]{1,0:T(8,128)(2,1)S(1)}, bf16[32,512]{1,0:T(8,128)(2,1)S(1)}, u32[]{:S(2)}, u32[]{:S(2)}) %collective-permute-start.2) | collective-permute-done | bytes 32800 | tf_op jit(solution)/shard_map/ppermute | solution.py:298
  19.4 2.6 %collective-permute-start.5 = (bf16[4,32,512]{2,1,0:T(8,128)(2,1)S(1)}, bf16[4,32,512]{2,1,0:T(8,128)(2,1)S(1)}, u32[]{:S(2)}, u32[]{:S(2)}) collective-permute-start(bf16[4,32,512]{2,1,0:T(8,128)(2,1)S(1)} %shard_map.58.g0), channel_id=1, source_target_pairs={{0,12},{1,13},{2,14},{3,15},{4,0},{5,1},{6,2},{7,3},{8,4},{9,5},{1... | collective-permute-start | bytes 393224 | tf_op jit(solution)/shard_map/ppermute | solution.py:298
  22.0 0.0 collective-permute-start.4
  22.0 1.7 %collective-permute-start.3 = (bf16[4,32,512]{2,1,0:T(8,128)(2,1)S(1)}, bf16[4,32,512]{2,1,0:T(8,128)(2,1)S(1)}, u32[]{:S(2)}, u32[]{:S(2)}) collective-permute-start(bf16[4,32,512]{2,1,0:T(8,128)(2,1)S(1)} %shard_map.58.g0), channel_id=1, source_target_pairs={{0,8},{1,9},{2,10},{3,11},{4,12},{5,13},{6,14},{7,15},{8,0},{9,1},... | collective-permute-start | bytes 393224 | tf_op jit(solution)/shard_map/ppermute | solution.py:298
  23.7 0.2 collective-permute-done.5.__3_.g3
  24.0 4.8 %collective-permute-done.4.__2_.g2 = bf16[4,32,512]{2,1,0:T(8,128)(2,1)S(1)} collective-permute-done((bf16[4,32,512]{2,1,0:T(8,128)(2,1)S(1)}, bf16[4,32,512]{2,1,0:T(8,128)(2,1)S(1)}, u32[]{:S(2)}, u32[]{:S(2)}) %collective-permute-start.4) | collective-permute-done | bytes 131104 | tf_op jit(solution)/shard_map/ppermute | solution.py:298
  28.7 0.0 collective-permute-done.3.__1_.g1
  28.7 1.0 all-to-all-done
  29.7 0.0 copy-start.1
  29.7 1.8 %collective-permute-start.6 = (bf16[512,512]{1,0:T(8,128)(2,1)S(1)}, bf16[512,512]{1,0:T(8,128)(2,1)S(1)}, u32[]{:S(2)}, u32[]{:S(2)}) collective-permute-start(bf16[512,512]{1,0:T(8,128)(2,1)S(1)} %shard_map.60.data_ref.refs_3_), channel_id=1, source_target_pairs={{0,16},{16,0},{32,48},{48,32},{64,80},{80,64},{96,112},{112,96},{1... | collective-permute-start | bytes 1572872 | tf_op jit(solution)/shard_map/ppermute | solution.py:315
  31.5 0.0 copy-done.1
  31.5 1.0 shard_map.61
  32.5 0.6 collective-permute-done.6.data_ref.refs_4_
  33.0 0.5 shard_map.62.other_ref.refs_1_
  33.5 0.4 shard_map.63
  34.0 11.6 %all_to_all.25.refs_2_ = f32[16,4,128]{2,1,0:T(4,128)S(1)} all-to-all(f32[16,4,128]{2,1,0:T(4,128)S(1)} %shard_map.63), channel_id=1, replica_groups=mesh['row'=16,'col'=16] {'col'}, dimensions={0} | all-to-all | bytes 65536 | tf_op jit(solution)/shard_map/all_to_all | solution.py:333
  45.5 0.5 shard_map.64
  46.1 16.4 %all_to_all.26.refs_2_ = f32[16,8,128]{2,1,0:T(8,128)S(1)} all-to-all(f32[16,8,128]{2,1,0:T(8,128)S(1)} %shard_map.64), channel_id=1, replica_groups=mesh['row'=16,'col'=16] {'row'}, dimensions={0} | all-to-all | bytes 131072 | tf_op jit(solution)/shard_map/all_to_all | solution.py:340
  62.5 0.6 shard_map.65
  63.1 9.2 %all_to_all.27.refs_2_ = f32[16,4,128]{2,1,0:T(4,128)S(1)} all-to-all(f32[16,4,128]{2,1,0:T(4,128)S(1)} %shard_map.65), channel_id=1, replica_groups=mesh['row'=16,'col'=16] {'col'}, dimensions={0} | all-to-all | bytes 65536 | tf_op jit(solution)/shard_map/all_to_all | solution.py:333
  72.4 0.5 shard_map.66
  72.9 11.8 %all_to_all.28.refs_2_ = f32[16,8,128]{2,1,0:T(8,128)S(1)} all-to-all(f32[16,8,128]{2,1,0:T(8,128)S(1)} %shard_map.66), channel_id=1, replica_groups=mesh['row'=16,'col'=16] {'row'}, dimensions={0} | all-to-all | bytes 131072 | tf_op jit(solution)/shard_map/all_to_all | solution.py:340
  84.7 1.7 %shard_map.67 = (f32[8,128]{1,0:T(8,128)S(1)}, f32[520,128]{1,0:T(8,128)S(1)}, f32[520,128]{1,0:T(8,128)S(1)}, f32[520,128]{1,0:T(8,128)S(1)}, f32[520,128]{1,0:T(8,128)S(1)}) custom-call(f32[512,512]{1,0:T(8,128)S(1)} %get-tuple-element.17.refs_0_, f32[512,512]{1,0:T(8,128)S(1)} %shard_map.62.other_ref.refs_1_, f32[16,8,128]{2,1,0:T(8,128)S(1)} %all_to_all.28.refs_2_, ...), custom_call_target="tpu_custom_call" | custom-call | tf_op jit(solution)/shard_map/pallas_call | solution.py:26
  86.5 1.0 collective-permute-start.7
  87.5 0.5 collective-permute-start.8
  88.0 2.1 %collective-permute-start.9 = (f32[520,128]{1,0:T(8,128)S(1)}, f32[520,128]{1,0:T(8,128)S(1)}, u32[]{:S(2)}, u32[]{:S(2)}) collective-permute-start(f32[520,128]{1,0:T(8,128)S(1)} %get-tuple-element.23), channel_id=1, source_target_pairs={{0,3},{1,0},{2,1},{3,2},{4,7},{5,4},{6,5},{7,6},{8,11},{9,8},{10,9... | collective-permute-start | bytes 798728 | tf_op jit(solution)/shard_map/ppermute | solution.py:298
  90.2 3.5 %collective-permute-done.7.refs_1_ = f32[520,128]{1,0:T(8,128)S(1)} collective-permute-done((f32[520,128]{1,0:T(8,128)S(1)}, f32[520,128]{1,0:T(8,128)S(1)}, u32[]{:S(2)}, u32[]{:S(2)}) %collective-permute-start.7) | collective-permute-done | bytes 266272 | tf_op jit(solution)/shard_map/ppermute | solution.py:298
  93.7 2.8 %collective-permute-done.8.refs_2_ = f32[520,128]{1,0:T(8,128)S(1)} collective-permute-done((f32[520,128]{1,0:T(8,128)S(1)}, f32[520,128]{1,0:T(8,128)S(1)}, u32[]{:S(2)}, u32[]{:S(2)}) %collective-permute-start.8) | collective-permute-done | bytes 266272 | tf_op jit(solution)/shard_map/ppermute | solution.py:298
  96.5 0.0 collective-permute-done.9.refs_3_
  96.5 0.1 shard_map.68
  96.6 0.8 collective-permute-start.10
  97.4 0.8 collective-permute-start.11
  98.2 1.9 %collective-permute-start.12 = (f32[136,128]{1,0:T(8,128)S(1)}, f32[136,128]{1,0:T(8,128)S(1)}, u32[]{:S(2)}, u32[]{:S(2)}) collective-permute-start(f32[136,128]{1,0:T(8,128)S(1)} %get-tuple-element.27), channel_id=1, source_target_pairs={{0,12},{1,13},{2,14},{3,15},{4,0},{5,1},{6,2},{7,3},{8,4},{9,5},{1... | collective-permute-start | bytes 208904 | tf_op jit(solution)/shard_map/ppermute | solution.py:298
  100.1 0.6 copy.8
  100.7 0.7 collective-permute-done.10.refs_1_
  101.4 1.0 collective-permute-done.11.refs_2_
  102.4 0.0 collective-permute-done.12.refs_3_
  102.4 0.7 shard_map.69
  (2 shorter events, 0.0 us)
Async XLA Ops:
  2.4 10.0 %copy-start = (bf16[32,512]{1,0:T(8,128)(2,1)S(1)}, bf16[32,512]{1,0:T(8,128)(2,1)}, u32[]{:S(2)}) copy-start(bf16[32,512]{1,0:T(8,128)(2,1)} %refs_0_.1) | copy-start | bytes 98308
  2.4 27.3 %all-to-all-start = ((bf16[16,32,512]{2,1,0:T(8,128)(2,1)}), bf16[16,32,512]{2,1,0:T(8,128)(2,1)S(1)}, u32[]{:S(2)}, u32[]{:S(2)}) async-start(bf16[16,32,512]{2,1,0:T(8,128)(2,1)} %shard_map.59), calls=%async_computation | async-start | bytes 1048576 | tf_op jit(solution)/shard_map/all_to_all | solution.py:308
  12.4 5.1 %collective-permute-start.1 = (bf16[32,512]{1,0:T(8,128)(2,1)S(1)}, bf16[32,512]{1,0:T(8,128)(2,1)S(1)}, u32[]{:S(2)}, u32[]{:S(2)}) collective-permute-start(bf16[32,512]{1,0:T(8,128)(2,1)S(1)} %copy-done), channel_id=1, source_target_pairs={{0,1},{1,2},{2,3},{3,0},{4,5},{5,6},{6,7},{7,4},{8,9},{9,10},{10,1... | collective-permute-start | bytes 98312 | tf_op jit(solution)/shard_map/ppermute | solution.py:298
  13.8 4.6 %collective-permute-start = (bf16[32,512]{1,0:T(8,128)(2,1)S(1)}, bf16[32,512]{1,0:T(8,128)(2,1)S(1)}, u32[]{:S(2)}, u32[]{:S(2)}) collective-permute-start(bf16[32,512]{1,0:T(8,128)(2,1)S(1)} %copy-done), channel_id=1, source_target_pairs={{0,2},{1,3},{2,0},{3,1},{4,6},{5,7},{6,4},{7,5},{8,10},{9,11},{10,... | collective-permute-start | bytes 98312 | tf_op jit(solution)/shard_map/ppermute | solution.py:298
  16.4 3.1 %collective-permute-start.2 = (bf16[32,512]{1,0:T(8,128)(2,1)S(1)}, bf16[32,512]{1,0:T(8,128)(2,1)S(1)}, u32[]{:S(2)}, u32[]{:S(2)}) collective-permute-start(bf16[32,512]{1,0:T(8,128)(2,1)S(1)} %copy-done), channel_id=1, source_target_pairs={{0,3},{1,0},{2,1},{3,2},{4,7},{5,4},{6,5},{7,6},{8,11},{9,8},{10,9... | collective-permute-start | bytes 98312 | tf_op jit(solution)/shard_map/ppermute | solution.py:298
  19.4 4.5 %collective-permute-start.5 = (bf16[4,32,512]{2,1,0:T(8,128)(2,1)S(1)}, bf16[4,32,512]{2,1,0:T(8,128)(2,1)S(1)}, u32[]{:S(2)}, u32[]{:S(2)}) collective-permute-start(bf16[4,32,512]{2,1,0:T(8,128)(2,1)S(1)} %shard_map.58.g0), channel_id=1, source_target_pairs={{0,12},{1,13},{2,14},{3,15},{4,0},{5,1},{6,2},{7,3},{8,4},{9,5},{1... | collective-permute-start | bytes 393224 | tf_op jit(solution)/shard_map/ppermute | solution.py:298
  22.0 6.7 %collective-permute-start.4 = (bf16[4,32,512]{2,1,0:T(8,128)(2,1)S(1)}, bf16[4,32,512]{2,1,0:T(8,128)(2,1)S(1)}, u32[]{:S(2)}, u32[]{:S(2)}) collective-permute-start(bf16[4,32,512]{2,1,0:T(8,128)(2,1)S(1)} %shard_map.58.g0), channel_id=1, source_target_pairs={{0,4},{1,5},{2,6},{3,7},{4,8},{5,9},{6,10},{7,11},{8,12},{9,13},{1... | collective-permute-start | bytes 393224 | tf_op jit(solution)/shard_map/ppermute | solution.py:298
  22.0 6.7 %collective-permute-start.3 = (bf16[4,32,512]{2,1,0:T(8,128)(2,1)S(1)}, bf16[4,32,512]{2,1,0:T(8,128)(2,1)S(1)}, u32[]{:S(2)}, u32[]{:S(2)}) collective-permute-start(bf16[4,32,512]{2,1,0:T(8,128)(2,1)S(1)} %shard_map.58.g0), channel_id=1, source_target_pairs={{0,8},{1,9},{2,10},{3,11},{4,12},{5,13},{6,14},{7,15},{8,0},{9,1},... | collective-permute-start | bytes 393224 | tf_op jit(solution)/shard_map/ppermute | solution.py:298
  29.7 1.8 %copy-start.1 = (f32[1024]{0:T(1024)S(1)}, f32[1024]{0:T(1024)}, u32[]{:S(2)}) copy-start(f32[1024]{0:T(1024)} %param.5) | copy-start | bytes 12292
  29.7 3.3 %collective-permute-start.6 = (bf16[512,512]{1,0:T(8,128)(2,1)S(1)}, bf16[512,512]{1,0:T(8,128)(2,1)S(1)}, u32[]{:S(2)}, u32[]{:S(2)}) collective-permute-start(bf16[512,512]{1,0:T(8,128)(2,1)S(1)} %shard_map.60.data_ref.refs_3_), channel_id=1, source_target_pairs={{0,16},{16,0},{32,48},{48,32},{64,80},{80,64},{96,112},{112,96},{1... | collective-permute-start | bytes 1572872 | tf_op jit(solution)/shard_map/ppermute | solution.py:315
  86.5 7.2 %collective-permute-start.7 = (f32[520,128]{1,0:T(8,128)S(1)}, f32[520,128]{1,0:T(8,128)S(1)}, u32[]{:S(2)}, u32[]{:S(2)}) collective-permute-start(f32[520,128]{1,0:T(8,128)S(1)} %get-tuple-element.21), channel_id=1, source_target_pairs={{0,2},{1,3},{2,0},{3,1},{4,6},{5,7},{6,4},{7,5},{8,10},{9,11},{10,... | collective-permute-start | bytes 798728 | tf_op jit(solution)/shard_map/ppermute | solution.py:298
  87.5 9.0 %collective-permute-start.8 = (f32[520,128]{1,0:T(8,128)S(1)}, f32[520,128]{1,0:T(8,128)S(1)}, u32[]{:S(2)}, u32[]{:S(2)}) collective-permute-start(f32[520,128]{1,0:T(8,128)S(1)} %get-tuple-element.22), channel_id=1, source_target_pairs={{0,1},{1,2},{2,3},{3,0},{4,5},{5,6},{6,7},{7,4},{8,9},{9,10},{10,1... | collective-permute-start | bytes 798728 | tf_op jit(solution)/shard_map/ppermute | solution.py:298
  88.0 8.5 %collective-permute-start.9 = (f32[520,128]{1,0:T(8,128)S(1)}, f32[520,128]{1,0:T(8,128)S(1)}, u32[]{:S(2)}, u32[]{:S(2)}) collective-permute-start(f32[520,128]{1,0:T(8,128)S(1)} %get-tuple-element.23), channel_id=1, source_target_pairs={{0,3},{1,0},{2,1},{3,2},{4,7},{5,4},{6,5},{7,6},{8,11},{9,8},{10,9... | collective-permute-start | bytes 798728 | tf_op jit(solution)/shard_map/ppermute | solution.py:298
  96.6 4.8 %collective-permute-start.10 = (f32[136,128]{1,0:T(8,128)S(1)}, f32[136,128]{1,0:T(8,128)S(1)}, u32[]{:S(2)}, u32[]{:S(2)}) collective-permute-start(f32[136,128]{1,0:T(8,128)S(1)} %get-tuple-element.25), channel_id=1, source_target_pairs={{0,8},{1,9},{2,10},{3,11},{4,12},{5,13},{6,14},{7,15},{8,0},{9,1},... | collective-permute-start | bytes 208904 | tf_op jit(solution)/shard_map/ppermute | solution.py:298
  97.4 5.0 %collective-permute-start.11 = (f32[136,128]{1,0:T(8,128)S(1)}, f32[136,128]{1,0:T(8,128)S(1)}, u32[]{:S(2)}, u32[]{:S(2)}) collective-permute-start(f32[136,128]{1,0:T(8,128)S(1)} %get-tuple-element.26), channel_id=1, source_target_pairs={{0,4},{1,5},{2,6},{3,7},{4,8},{5,9},{6,10},{7,11},{8,12},{9,13},{1... | collective-permute-start | bytes 208904 | tf_op jit(solution)/shard_map/ppermute | solution.py:298
  98.2 4.2 %collective-permute-start.12 = (f32[136,128]{1,0:T(8,128)S(1)}, f32[136,128]{1,0:T(8,128)S(1)}, u32[]{:S(2)}, u32[]{:S(2)}) collective-permute-start(f32[136,128]{1,0:T(8,128)S(1)} %get-tuple-element.27), channel_id=1, source_target_pairs={{0,12},{1,13},{2,14},{3,15},{4,0},{5,1},{6,2},{7,3},{8,4},{9,5},{1... | collective-permute-start | bytes 208904 | tf_op jit(solution)/shard_map/ppermute | solution.py:298

commit v6 on v5

--- a/solution.py
+++ b/solution.py
@@ -14,6 +14,7 @@
 SCALE = 1.0 / (EPS * LN2)
 LANES = 128
 OFFSETS = (0, 2, 1, -1)
+GATHER = ((0, 1, 2, -1), (0, 1, 2, -1))
 STATS = 8
 
 
@@ -111,8 +112,8 @@
 def own_kernel(g0, g1, g2, g3, data_ref, pot_ref, gen_ref, affinity_ref, log_ref):
     side, size = g0.shape[:2]
     column, core = lax.axis_index("col"), lax.axis_index("row") % 2
-    for second, ref in zip(OFFSETS, (g0, g1, g2, g3)):
-        for n, first in enumerate(OFFSETS):
+    for second, ref in zip(GATHER[1], (g0, g1, g2, g3)):
+        for n, first in enumerate(GATHER[0]):
             y_back = jnp.where(core == 0, second, first)
             x_back = jnp.where(core == 0, first, second)
             place = (column // side - y_back + side) % side * side + (column % side - x_back + side) % side
@@ -213,7 +214,7 @@
 
 
 def target_kernel(log_gen, own_ref, other_ref, got_ref, data_ref, more_ref, pot_ref, *refs):
-    *outs, stats_ref, high, low = refs
+    stats_ref, high, low, *outs = refs
     gen_rows, half = own_ref.shape
     chunks = gen_rows // LANES
     pot = log_gen - log_sum(got_ref[...])
@@ -234,9 +235,15 @@
             total = jnp.sum(total, axis=1, keepdims=True)
             for place, column in ((n, top), (chunks + n, total)):
                 stats_ref[place : place + 1, :] = rows_to_lanes(column)
-        add_blocks(OFFSETS, (data_ref, more_ref), (high, low), slice(first, first + GROUP), outs)
+        add_blocks(OFFSETS[1:], (data_ref, more_ref), (high, low), slice(first, first + GROUP), outs)
     for out_ref in outs:
         out_ref[out_ref.shape[0] - STATS :, :] = stats_ref[...]
+
+
+def near_kernel(stats_ref, high, low, data_ref, more_ref, out_ref):
+    for first in range(0, high.shape[0], GROUP):
+        add_blocks(OFFSETS[:1], (data_ref, more_ref), (high, low), slice(first, first + GROUP), (out_ref,))
+    out_ref[out_ref.shape[0] - STATS :, :] = stats_ref[...]
 
 
 def relay_kernel(*refs):
@@ -306,8 +313,8 @@
         space=pltpu.HBM,
     )
     own = lax.all_to_all(outgoing, "row", 0, 0).reshape(features, half)
-    stack = kernel_call(stack_kernel, shaped((side,) + gen_points.shape, dtype), (gen_points, *(hop(gen_points, 0, back) for back in OFFSETS[1:])))
-    stacks = (stack,) + tuple(hop(stack, 1, back) for back in OFFSETS[1:])
+    stack = kernel_call(stack_kernel, shaped((side,) + gen_points.shape, dtype), (gen_points, *(hop(gen_points, 0, back) for back in GATHER[0][1:])))
+    stacks = (stack,) + tuple(hop(stack, 1, back) for back in GATHER[1][1:])
 
     start = data_potential.reshape(data_chunks, LANES)
 
@@ -342,16 +349,17 @@
             lines = kernel_call(at(row_kernel, log_gen), row_out, (*affinity, got))
     block_rows = gen_chunks * feats
     sent = pltpu.VMEM((side * block_rows + STATS, LANES), f32)
-    potential, *blocks = kernel_call(
+    weights = pltpu.VMEM((gen_rows, data_cols), dtype)
+    potential, stats, high, low, *blocks = kernel_call(
         at(target_kernel, log_gen),
-        (pltpu.VMEM((data_chunks, LANES), f32),) + (sent,) * side,
+        (pltpu.VMEM((data_chunks, LANES), f32), pltpu.VMEM((STATS, LANES), f32), weights, weights) + (sent,) * (side - 1),
         (*affinity, got, own, other),
-        scratch=[pltpu.VMEM((STATS, LANES), f32)] + [pltpu.VMEM((gen_rows, data_cols), dtype)] * 2,
-    )
+    )
+    kept = kernel_call(near_kernel, sent, (in_vmem(stats), in_vmem(high), in_vmem(low), own, other), flops=10**9)
     blocks = kernel_call(
         relay_kernel,
         (shaped((block_rows + STATS, LANES), f32),) * side,
-        [blocks[0]] + [hop(block, 0, back) for block, back in zip(blocks[1:], OFFSETS[1:])],
+        [in_vmem(kept)] + [hop(block, 0, back) for block, back in zip(blocks, OFFSETS[1:])],
     )
     gen_pot, target = kernel_call(
         at(merge_kernel, log_data),

time: 104 us -> 104 us (level)
    pallas_call x12 -> x13, Pallas kernels: 7.86 us -> 8.51 us  [kernel_call(): pl.pallas_call(body, out_shape=out_shape, in_specs=[whole] * len(args), o...]
  transfers between devices with their start and end apart: 14 -> 14, of which waited for: 10 -> 10; matrix products, arithmetic and copies ran while one was open for 1% -> 1% of each run, Pallas kernels for 1% -> 2%
where the time goes in v6:
time: 104 us; the launch traced here: 102 us
  blocking collectives  48.2 us (46%)
  starting transfers between devices  28.5 us (27%)
  waiting for transfers between devices  15.8 us (15%)
  Pallas kernels  8.51 us (8%)
    all_to_all x2, blocking collectives, local(): got = lax.all_to_all(lines, 'row', 0, 0)  27.6 us
    all_to_all x2, blocking collectives, local(): got = lax.all_to_all(lines, 'col', 0, 0)  20.6 us
    ppermute x12, starting transfers between devices, hop(): return lax.ppermute(array, ('row', 'col'), pairs)  16.5 us
    ppermute x12, waiting for transfers between devices, hop(): return lax.ppermute(array, ('row', 'col'), pairs)  14.8 us
    all_to_all x1, starting transfers between devices, local(): own = lax.all_to_all(outgoing, 'row', 0, 0).reshape(features, half)  9.99 us
    pallas_call x13, Pallas kernels, kernel_call(): pl.pallas_call(body, out_shape=out_shape, in_specs=[whole] * len(args), o...  8.51 us
  transfers between devices with their start and end apart: 14, of which 10 were waited for; matrix products, arithmetic and copies ran while one was open for 1% of the time, Pallas kernels for 2%

profile of v6, /device:TPU:1, one launch (start us, length us, event | category | flops | bytes accessed | tf_op | source)
XLA Modules:
  0.0 102.3 jit_solution(2091355066476449342)
XLA Ops:
  0.6 1.7 %shard_map.59 = bf16[16,32,512]{2,1,0:T(8,128)(2,1)} custom-call(bf16[32,1024]{1,0:T(8,128)(2,1)} %bitcast.9), custom_call_target="tpu_custom_call" | custom-call | tf_op jit(solution)/shard_map/pallas_call | solution.py:27
  2.4 0.0 copy-start
  2.4 10.0 %all-to-all-start = ((bf16[16,32,512]{2,1,0:T(8,128)(2,1)}), bf16[16,32,512]{2,1,0:T(8,128)(2,1)S(1)}, u32[]{:S(2)}, u32[]{:S(2)}) async-start(bf16[16,32,512]{2,1,0:T(8,128)(2,1)} %shard_map.59), calls=%async_computation | async-start | bytes 1048576 | tf_op jit(solution)/shard_map/all_to_all | solution.py:315
  12.4 0.0 copy-done
  12.4 3.0 %collective-permute-start.1 = (bf16[32,512]{1,0:T(8,128)(2,1)S(1)}, bf16[32,512]{1,0:T(8,128)(2,1)S(1)}, u32[]{:S(2)}, u32[]{:S(2)}) collective-permute-start(bf16[32,512]{1,0:T(8,128)(2,1)S(1)} %copy-done), channel_id=1, source_target_pairs={{0,2},{1,3},{2,0},{3,1},{4,6},{5,7},{6,4},{7,5},{8,10},{9,11},{10,... | collective-permute-start | bytes 98312 | tf_op jit(solution)/shard_map/ppermute | solution.py:305
  15.4 0.4 collective-permute-start
  15.8 2.3 %collective-permute-start.2 = (bf16[32,512]{1,0:T(8,128)(2,1)S(1)}, bf16[32,512]{1,0:T(8,128)(2,1)S(1)}, u32[]{:S(2)}, u32[]{:S(2)}) collective-permute-start(bf16[32,512]{1,0:T(8,128)(2,1)S(1)} %copy-done), channel_id=1, source_target_pairs={{0,3},{1,0},{2,1},{3,2},{4,7},{5,4},{6,5},{7,6},{8,11},{9,8},{10,9... | collective-permute-start | bytes 98312 | tf_op jit(solution)/shard_map/ppermute | solution.py:305
  18.1 0.0 collective-permute-done.1.refs_2_
  18.1 1.6 %collective-permute-done.refs_1_ = bf16[32,512]{1,0:T(8,128)(2,1)S(1)} collective-permute-done((bf16[32,512]{1,0:T(8,128)(2,1)S(1)}, bf16[32,512]{1,0:T(8,128)(2,1)S(1)}, u32[]{:S(2)}, u32[]{:S(2)}) %collective-permute-start) | collective-permute-done | bytes 32800 | tf_op jit(solution)/shard_map/ppermute | solution.py:305
  19.7 0.0 collective-permute-done.2.refs_3_
  19.7 2.6 %collective-permute-start.5 = (bf16[4,32,512]{2,1,0:T(8,128)(2,1)S(1)}, bf16[4,32,512]{2,1,0:T(8,128)(2,1)S(1)}, u32[]{:S(2)}, u32[]{:S(2)}) collective-permute-start(bf16[4,32,512]{2,1,0:T(8,128)(2,1)S(1)} %shard_map.58.g0), channel_id=1, source_target_pairs={{0,12},{1,13},{2,14},{3,15},{4,0},{5,1},{6,2},{7,3},{8,4},{9,5},{1... | collective-permute-start | bytes 393224 | tf_op jit(solution)/shard_map/ppermute | solution.py:305
  22.2 0.5 collective-permute-start.4
  22.7 0.6 collective-permute-start.3
  23.4 2.2 %collective-permute-done.5.__3_.g3 = bf16[4,32,512]{2,1,0:T(8,128)(2,1)S(1)} collective-permute-done((bf16[4,32,512]{2,1,0:T(8,128)(2,1)S(1)}, bf16[4,32,512]{2,1,0:T(8,128)(2,1)S(1)}, u32[]{:S(2)}, u32[]{:S(2)}) %collective-permute-start.5) | collective-permute-done | bytes 131104 | tf_op jit(solution)/shard_map/ppermute | solution.py:305
  25.5 2.3 %collective-permute-done.4.__2_.g2 = bf16[4,32,512]{2,1,0:T(8,128)(2,1)S(1)} collective-permute-done((bf16[4,32,512]{2,1,0:T(8,128)(2,1)S(1)}, bf16[4,32,512]{2,1,0:T(8,128)(2,1)S(1)}, u32[]{:S(2)}, u32[]{:S(2)}) %collective-permute-start.4) | collective-permute-done | bytes 131104 | tf_op jit(solution)/shard_map/ppermute | solution.py:305
  27.8 1.4 %collective-permute-done.3.__1_.g1 = bf16[4,32,512]{2,1,0:T(8,128)(2,1)S(1)} collective-permute-done((bf16[4,32,512]{2,1,0:T(8,128)(2,1)S(1)}, bf16[4,32,512]{2,1,0:T(8,128)(2,1)S(1)}, u32[]{:S(2)}, u32[]{:S(2)}) %collective-permute-start.3) | collective-permute-done | bytes 131104 | tf_op jit(solution)/shard_map/ppermute | solution.py:305
  29.2 0.4 all-to-all-done
  29.7 0.0 copy-start.1
  29.7 2.0 %collective-permute-start.6 = (bf16[512,512]{1,0:T(8,128)(2,1)S(1)}, bf16[512,512]{1,0:T(8,128)(2,1)S(1)}, u32[]{:S(2)}, u32[]{:S(2)}) collective-permute-start(bf16[512,512]{1,0:T(8,128)(2,1)S(1)} %shard_map.60.data_ref.refs_3_), channel_id=1, source_target_pairs={{0,16},{16,0},{32,48},{48,32},{64,80},{80,64},{96,112},{112,96},{1... | collective-permute-start | bytes 1572872 | tf_op jit(solution)/shard_map/ppermute | solution.py:322
  31.7 0.0 copy-done.1
  31.7 1.0 shard_map.61
  32.7 0.6 collective-permute-done.6.data_ref.refs_4_.more_ref
  33.3 0.5 shard_map.62.other_ref.refs_1_
  33.7 0.4 shard_map.63
  34.2 11.4 %all_to_all.25.refs_2_ = f32[16,4,128]{2,1,0:T(4,128)S(1)} all-to-all(f32[16,4,128]{2,1,0:T(4,128)S(1)} %shard_map.63), channel_id=1, replica_groups=mesh['row'=16,'col'=16] {'col'}, dimensions={0} | all-to-all | bytes 65536 | tf_op jit(solution)/shard_map/all_to_all | solution.py:340
  45.5 0.5 shard_map.64
  46.1 15.8 %all_to_all.26.refs_2_ = f32[16,8,128]{2,1,0:T(8,128)S(1)} all-to-all(f32[16,8,128]{2,1,0:T(8,128)S(1)} %shard_map.64), channel_id=1, replica_groups=mesh['row'=16,'col'=16] {'row'}, dimensions={0} | all-to-all | bytes 131072 | tf_op jit(solution)/shard_map/all_to_all | solution.py:347
  61.9 0.6 shard_map.65
  62.5 9.2 %all_to_all.27.refs_2_ = f32[16,4,128]{2,1,0:T(4,128)S(1)} all-to-all(f32[16,4,128]{2,1,0:T(4,128)S(1)} %shard_map.65), channel_id=1, replica_groups=mesh['row'=16,'col'=16] {'col'}, dimensions={0} | all-to-all | bytes 65536 | tf_op jit(solution)/shard_map/all_to_all | solution.py:340
  71.8 0.5 shard_map.66
  72.3 11.8 %all_to_all.28.refs_2_ = f32[16,8,128]{2,1,0:T(8,128)S(1)} all-to-all(f32[16,8,128]{2,1,0:T(8,128)S(1)} %shard_map.66), channel_id=1, replica_groups=mesh['row'=16,'col'=16] {'row'}, dimensions={0} | all-to-all | bytes 131072 | tf_op jit(solution)/shard_map/all_to_all | solution.py:347
  84.1 1.6 %shard_map.67 = (f32[8,128]{1,0:T(8,128)S(1)}, f32[8,128]{1,0:T(8,128)S(1)}, bf16[512,1024]{1,0:T(8,128)(2,1)S(1)}, bf16[512,1024]{1,0:T(8,128)(2,1)S(1)}, f32[5...) custom-call(f32[512,512]{1,0:T(8,128)S(1)} %get-tuple-element.19.refs_0_, ...), custom_call_target="tpu_custom_call" | custom-call | tf_op jit(solution)/shard_map/pallas_call | solution.py:27
  85.7 1.0 collective-permute-start.7
  86.7 0.6 collective-permute-start.8
  87.3 2.1 %collective-permute-start.9 = (f32[520,128]{1,0:T(8,128)S(1)}, f32[520,128]{1,0:T(8,128)S(1)}, u32[]{:S(2)}, u32[]{:S(2)}) collective-permute-start(f32[520,128]{1,0:T(8,128)S(1)} %get-tuple-element.27), channel_id=1, source_target_pairs={{0,3},{1,0},{2,1},{3,2},{4,7},{5,4},{6,5},{7,6},{8,11},{9,8},{10,9... | collective-permute-start | bytes 798728 | tf_op jit(solution)/shard_map/ppermute | solution.py:305
  89.4 0.8 shard_map.68.refs_0_
  90.2 2.7 %collective-permute-done.7.refs_1_ = f32[520,128]{1,0:T(8,128)S(1)} collective-permute-done((f32[520,128]{1,0:T(8,128)S(1)}, f32[520,128]{1,0:T(8,128)S(1)}, u32[]{:S(2)}, u32[]{:S(2)}) %collective-permute-start.7) | collective-permute-done | bytes 266272 | tf_op jit(solution)/shard_map/ppermute | solution.py:305
  92.9 2.8 %collective-permute-done.8.refs_2_ = f32[520,128]{1,0:T(8,128)S(1)} collective-permute-done((f32[520,128]{1,0:T(8,128)S(1)}, f32[520,128]{1,0:T(8,128)S(1)}, u32[]{:S(2)}, u32[]{:S(2)}) %collective-permute-start.8) | collective-permute-done | bytes 266272 | tf_op jit(solution)/shard_map/ppermute | solution.py:305
  95.7 0.0 collective-permute-done.9.refs_3_
  95.7 0.1 shard_map.69
  95.9 0.8 collective-permute-start.10
  96.6 0.8 collective-permute-start.11
  97.4 1.9 %collective-permute-start.12 = (f32[136,128]{1,0:T(8,128)S(1)}, f32[136,128]{1,0:T(8,128)S(1)}, u32[]{:S(2)}, u32[]{:S(2)}) collective-permute-start(f32[136,128]{1,0:T(8,128)S(1)} %get-tuple-element.31), channel_id=1, source_target_pairs={{0,12},{1,13},{2,14},{3,15},{4,0},{5,1},{6,2},{7,3},{8,4},{9,5},{1... | collective-permute-start | bytes 208904 | tf_op jit(solution)/shard_map/ppermute | solution.py:305
  99.3 0.6 copy.8
  99.9 0.7 collective-permute-done.10.refs_1_
  100.6 1.0 collective-permute-done.11.refs_2_
  101.7 0.0 collective-permute-done.12.refs_3_
  101.7 0.7 shard_map.70
  (2 shorter events, 0.0 us)
Async XLA Ops:
  2.4 10.0 %copy-start = (bf16[32,512]{1,0:T(8,128)(2,1)S(1)}, bf16[32,512]{1,0:T(8,128)(2,1)}, u32[]{:S(2)}) copy-start(bf16[32,512]{1,0:T(8,128)(2,1)} %refs_0_.1) | copy-start | bytes 98308
  2.4 27.3 %all-to-all-start = ((bf16[16,32,512]{2,1,0:T(8,128)(2,1)}), bf16[16,32,512]{2,1,0:T(8,128)(2,1)S(1)}, u32[]{:S(2)}, u32[]{:S(2)}) async-start(bf16[16,32,512]{2,1,0:T(8,128)(2,1)} %shard_map.59), calls=%async_computation | async-start | bytes 1048576 | tf_op jit(solution)/shard_map/all_to_all | solution.py:315
  12.4 5.7 %collective-permute-start.1 = (bf16[32,512]{1,0:T(8,128)(2,1)S(1)}, bf16[32,512]{1,0:T(8,128)(2,1)S(1)}, u32[]{:S(2)}, u32[]{:S(2)}) collective-permute-start(bf16[32,512]{1,0:T(8,128)(2,1)S(1)} %copy-done), channel_id=1, source_target_pairs={{0,2},{1,3},{2,0},{3,1},{4,6},{5,7},{6,4},{7,5},{8,10},{9,11},{10,... | collective-permute-start | bytes 98312 | tf_op jit(solution)/shard_map/ppermute | solution.py:305
  15.4 4.3 %collective-permute-start = (bf16[32,512]{1,0:T(8,128)(2,1)S(1)}, bf16[32,512]{1,0:T(8,128)(2,1)S(1)}, u32[]{:S(2)}, u32[]{:S(2)}) collective-permute-start(bf16[32,512]{1,0:T(8,128)(2,1)S(1)} %copy-done), channel_id=1, source_target_pairs={{0,1},{1,2},{2,3},{3,0},{4,5},{5,6},{6,7},{7,4},{8,9},{9,10},{10,1... | collective-permute-start | bytes 98312 | tf_op jit(solution)/shard_map/ppermute | solution.py:305
  15.8 3.9 %collective-permute-start.2 = (bf16[32,512]{1,0:T(8,128)(2,1)S(1)}, bf16[32,512]{1,0:T(8,128)(2,1)S(1)}, u32[]{:S(2)}, u32[]{:S(2)}) collective-permute-start(bf16[32,512]{1,0:T(8,128)(2,1)S(1)} %copy-done), channel_id=1, source_target_pairs={{0,3},{1,0},{2,1},{3,2},{4,7},{5,4},{6,5},{7,6},{8,11},{9,8},{10,9... | collective-permute-start | bytes 98312 | tf_op jit(solution)/shard_map/ppermute | solution.py:305
  19.7 5.9 %collective-permute-start.5 = (bf16[4,32,512]{2,1,0:T(8,128)(2,1)S(1)}, bf16[4,32,512]{2,1,0:T(8,128)(2,1)S(1)}, u32[]{:S(2)}, u32[]{:S(2)}) collective-permute-start(bf16[4,32,512]{2,1,0:T(8,128)(2,1)S(1)} %shard_map.58.g0), channel_id=1, source_target_pairs={{0,12},{1,13},{2,14},{3,15},{4,0},{5,1},{6,2},{7,3},{8,4},{9,5},{1... | collective-permute-start | bytes 393224 | tf_op jit(solution)/shard_map/ppermute | solution.py:305
  22.2 5.6 %collective-permute-start.4 = (bf16[4,32,512]{2,1,0:T(8,128)(2,1)S(1)}, bf16[4,32,512]{2,1,0:T(8,128)(2,1)S(1)}, u32[]{:S(2)}, u32[]{:S(2)}) collective-permute-start(bf16[4,32,512]{2,1,0:T(8,128)(2,1)S(1)} %shard_map.58.g0), channel_id=1, source_target_pairs={{0,8},{1,9},{2,10},{3,11},{4,12},{5,13},{6,14},{7,15},{8,0},{9,1},... | collective-permute-start | bytes 393224 | tf_op jit(solution)/shard_map/ppermute | solution.py:305
  22.7 6.5 %collective-permute-start.3 = (bf16[4,32,512]{2,1,0:T(8,128)(2,1)S(1)}, bf16[4,32,512]{2,1,0:T(8,128)(2,1)S(1)}, u32[]{:S(2)}, u32[]{:S(2)}) collective-permute-start(bf16[4,32,512]{2,1,0:T(8,128)(2,1)S(1)} %shard_map.58.g0), channel_id=1, source_target_pairs={{0,4},{1,5},{2,6},{3,7},{4,8},{5,9},{6,10},{7,11},{8,12},{9,13},{1... | collective-permute-start | bytes 393224 | tf_op jit(solution)/shard_map/ppermute | solution.py:305
  29.7 2.0 %copy-start.1 = (f32[1024]{0:T(1024)S(1)}, f32[1024]{0:T(1024)}, u32[]{:S(2)}) copy-start(f32[1024]{0:T(1024)} %param.5) | copy-start | bytes 12292
  29.7 3.6 %collective-permute-start.6 = (bf16[512,512]{1,0:T(8,128)(2,1)S(1)}, bf16[512,512]{1,0:T(8,128)(2,1)S(1)}, u32[]{:S(2)}, u32[]{:S(2)}) collective-permute-start(bf16[512,512]{1,0:T(8,128)(2,1)S(1)} %shard_map.60.data_ref.refs_3_), channel_id=1, source_target_pairs={{0,16},{16,0},{32,48},{48,32},{64,80},{80,64},{96,112},{112,96},{1... | collective-permute-start | bytes 1572872 | tf_op jit(solution)/shard_map/ppermute | solution.py:322
  85.7 7.2 %collective-permute-start.7 = (f32[520,128]{1,0:T(8,128)S(1)}, f32[520,128]{1,0:T(8,128)S(1)}, u32[]{:S(2)}, u32[]{:S(2)}) collective-permute-start(f32[520,128]{1,0:T(8,128)S(1)} %get-tuple-element.25), channel_id=1, source_target_pairs={{0,2},{1,3},{2,0},{3,1},{4,6},{5,7},{6,4},{7,5},{8,10},{9,11},{10,... | collective-permute-start | bytes 798728 | tf_op jit(solution)/shard_map/ppermute | solution.py:305
  86.7 9.0 %collective-permute-start.8 = (f32[520,128]{1,0:T(8,128)S(1)}, f32[520,128]{1,0:T(8,128)S(1)}, u32[]{:S(2)}, u32[]{:S(2)}) collective-permute-start(f32[520,128]{1,0:T(8,128)S(1)} %get-tuple-element.26), channel_id=1, source_target_pairs={{0,1},{1,2},{2,3},{3,0},{4,5},{5,6},{6,7},{7,4},{8,9},{9,10},{10,1... | collective-permute-start | bytes 798728 | tf_op jit(solution)/shard_map/ppermute | solution.py:305
  87.3 8.5 %collective-permute-start.9 = (f32[520,128]{1,0:T(8,128)S(1)}, f32[520,128]{1,0:T(8,128)S(1)}, u32[]{:S(2)}, u32[]{:S(2)}) collective-permute-start(f32[520,128]{1,0:T(8,128)S(1)} %get-tuple-element.27), channel_id=1, source_target_pairs={{0,3},{1,0},{2,1},{3,2},{4,7},{5,4},{6,5},{7,6},{8,11},{9,8},{10,9... | collective-permute-start | bytes 798728 | tf_op jit(solution)/shard_map/ppermute | solution.py:305
  95.9 4.8 %collective-permute-start.10 = (f32[136,128]{1,0:T(8,128)S(1)}, f32[136,128]{1,0:T(8,128)S(1)}, u32[]{:S(2)}, u32[]{:S(2)}) collective-permute-start(f32[136,128]{1,0:T(8,128)S(1)} %get-tuple-element.29), channel_id=1, source_target_pairs={{0,8},{1,9},{2,10},{3,11},{4,12},{5,13},{6,14},{7,15},{8,0},{9,1},... | collective-permute-start | bytes 208904 | tf_op jit(solution)/shard_map/ppermute | solution.py:305
  96.6 5.0 %collective-permute-start.11 = (f32[136,128]{1,0:T(8,128)S(1)}, f32[136,128]{1,0:T(8,128)S(1)}, u32[]{:S(2)}, u32[]{:S(2)}) collective-permute-start(f32[136,128]{1,0:T(8,128)S(1)} %get-tuple-element.30), channel_id=1, source_target_pairs={{0,4},{1,5},{2,6},{3,7},{4,8},{5,9},{6,10},{7,11},{8,12},{9,13},{1... | collective-permute-start | bytes 208904 | tf_op jit(solution)/shard_map/ppermute | solution.py:305
  97.4 4.2 %collective-permute-start.12 = (f32[136,128]{1,0:T(8,128)S(1)}, f32[136,128]{1,0:T(8,128)S(1)}, u32[]{:S(2)}, u32[]{:S(2)}) collective-permute-start(f32[136,128]{1,0:T(8,128)S(1)} %get-tuple-element.31), channel_id=1, source_target_pairs={{0,12},{1,13},{2,14},{3,15},{4,0},{5,1},{6,2},{7,3},{8,4},{9,5},{1... | collective-permute-start | bytes 208904 | tf_op jit(solution)/shard_map/ppermute | solution.py:305

commit v7 on v6

--- a/solution.py
+++ b/solution.py
@@ -14,7 +14,7 @@
 SCALE = 1.0 / (EPS * LN2)
 LANES = 128
 OFFSETS = (0, 2, 1, -1)
-GATHER = ((0, 1, 2, -1), (0, 1, 2, -1))
+GATHER = ((0, -1, 1, 2), (0, 1, -1, 2))
 STATS = 8
 
 

time: 104 us -> 102 us (0.981)
  blocking collectives: 48.2 us -> 46.8 us
    all_to_all x2, blocking collectives: 27.6 us -> 26.3 us  [local(): got = lax.all_to_all(lines, 'row', 0, 0)]
where the time goes in v7:
time: 102 us; the launch traced here: 101 us
  blocking collectives  46.8 us (46%)
  starting transfers between devices  27.9 us (27%)
  waiting for transfers between devices  16.4 us (16%)
  Pallas kernels  8.51 us (8%)
    all_to_all x2, blocking collectives, local(): got = lax.all_to_all(lines, 'row', 0, 0)  26.3 us
    all_to_all x2, blocking collectives, local(): got = lax.all_to_all(lines, 'col', 0, 0)  20.6 us
    ppermute x12, starting transfers between devices, hop(): return lax.ppermute(array, ('row', 'col'), pairs)  15.9 us
    ppermute x12, waiting for transfers between devices, hop(): return lax.ppermute(array, ('row', 'col'), pairs)  14.7 us
    all_to_all x1, starting transfers between devices, local(): own = lax.all_to_all(outgoing, 'row', 0, 0).reshape(features, half)  9.99 us
    pallas_call x13, Pallas kernels, kernel_call(): pl.pallas_call(body, out_shape=out_shape, in_specs=[whole] * len(args), o...  8.51 us
    ppermute x1, starting transfers between devices, local(): lax.ppermute(own, 'row', [(i, i ^ 1) for i in range(rows_n)])  2.06 us
  transfers between devices with their start and end apart: 14, of which 10 were waited for; matrix products, arithmetic and copies ran while one was open for 1% of the time, Pallas kernels for 2%

profile of v7, /device:TPU:1, one launch (start us, length us, event | category | flops | bytes accessed | tf_op | source)
XLA Modules:
  0.0 101.0 jit_solution(3224551564768163397)
XLA Ops:
  0.6 1.7 %shard_map.59 = bf16[16,32,512]{2,1,0:T(8,128)(2,1)} custom-call(bf16[32,1024]{1,0:T(8,128)(2,1)} %bitcast.9), custom_call_target="tpu_custom_call" | custom-call | tf_op jit(solution)/shard_map/pallas_call | solution.py:27
  2.4 0.0 copy-start
  2.4 10.0 %all-to-all-start = ((bf16[16,32,512]{2,1,0:T(8,128)(2,1)}), bf16[16,32,512]{2,1,0:T(8,128)(2,1)S(1)}, u32[]{:S(2)}, u32[]{:S(2)}) async-start(bf16[16,32,512]{2,1,0:T(8,128)(2,1)} %shard_map.59), calls=%async_computation | async-start | bytes 1048576 | tf_op jit(solution)/shard_map/all_to_all | solution.py:315
  12.4 0.0 copy-done
  12.4 1.4 %collective-permute-start.1 = (bf16[32,512]{1,0:T(8,128)(2,1)S(1)}, bf16[32,512]{1,0:T(8,128)(2,1)S(1)}, u32[]{:S(2)}, u32[]{:S(2)}) collective-permute-start(bf16[32,512]{1,0:T(8,128)(2,1)S(1)} %copy-done), channel_id=1, source_target_pairs={{0,1},{1,2},{2,3},{3,0},{4,5},{5,6},{6,7},{7,4},{8,9},{9,10},{10,1... | collective-permute-start | bytes 98312 | tf_op jit(solution)/shard_map/ppermute | solution.py:305
  13.8 1.5 %collective-permute-start = (bf16[32,512]{1,0:T(8,128)(2,1)S(1)}, bf16[32,512]{1,0:T(8,128)(2,1)S(1)}, u32[]{:S(2)}, u32[]{:S(2)}) collective-permute-start(bf16[32,512]{1,0:T(8,128)(2,1)S(1)} %copy-done), channel_id=1, source_target_pairs={{0,3},{1,0},{2,1},{3,2},{4,7},{5,4},{6,5},{7,6},{8,11},{9,8},{10,9... | collective-permute-start | bytes 98312 | tf_op jit(solution)/shard_map/ppermute | solution.py:305
  15.3 1.6 %collective-permute-start.2 = (bf16[32,512]{1,0:T(8,128)(2,1)S(1)}, bf16[32,512]{1,0:T(8,128)(2,1)S(1)}, u32[]{:S(2)}, u32[]{:S(2)}) collective-permute-start(bf16[32,512]{1,0:T(8,128)(2,1)S(1)} %copy-done), channel_id=1, source_target_pairs={{0,2},{1,3},{2,0},{3,1},{4,6},{5,7},{6,4},{7,5},{8,10},{9,11},{10,... | collective-permute-start | bytes 98312 | tf_op jit(solution)/shard_map/ppermute | solution.py:305
  16.8 0.0 collective-permute-done.1.refs_2_
  16.8 0.0 collective-permute-done.refs_1_
  16.8 3.0 %collective-permute-done.2.refs_3_ = bf16[32,512]{1,0:T(8,128)(2,1)S(1)} collective-permute-done((bf16[32,512]{1,0:T(8,128)(2,1)S(1)}, bf16[32,512]{1,0:T(8,128)(2,1)S(1)}, u32[]{:S(2)}, u32[]{:S(2)}) %collective-permute-start.2) | collective-permute-done | bytes 32800 | tf_op jit(solution)/shard_map/ppermute | solution.py:305
  19.9 2.8 %collective-permute-start.5 = (bf16[4,32,512]{2,1,0:T(8,128)(2,1)S(1)}, bf16[4,32,512]{2,1,0:T(8,128)(2,1)S(1)}, u32[]{:S(2)}, u32[]{:S(2)}) collective-permute-start(bf16[4,32,512]{2,1,0:T(8,128)(2,1)S(1)} %shard_map.58.g0), channel_id=1, source_target_pairs={{0,8},{1,9},{2,10},{3,11},{4,12},{5,13},{6,14},{7,15},{8,0},{9,1},... | collective-permute-start | bytes 393224 | tf_op jit(solution)/shard_map/ppermute | solution.py:305
  22.7 0.9 collective-permute-start.4
  23.6 0.6 collective-permute-start.3
  24.2 1.1 %collective-permute-done.5.__3_.g3 = bf16[4,32,512]{2,1,0:T(8,128)(2,1)S(1)} collective-permute-done((bf16[4,32,512]{2,1,0:T(8,128)(2,1)S(1)}, bf16[4,32,512]{2,1,0:T(8,128)(2,1)S(1)}, u32[]{:S(2)}, u32[]{:S(2)}) %collective-permute-start.5) | collective-permute-done | bytes 131104 | tf_op jit(solution)/shard_map/ppermute | solution.py:305
  25.3 1.8 %collective-permute-done.4.__2_.g2 = bf16[4,32,512]{2,1,0:T(8,128)(2,1)S(1)} collective-permute-done((bf16[4,32,512]{2,1,0:T(8,128)(2,1)S(1)}, bf16[4,32,512]{2,1,0:T(8,128)(2,1)S(1)}, u32[]{:S(2)}, u32[]{:S(2)}) %collective-permute-start.4) | collective-permute-done | bytes 131104 | tf_op jit(solution)/shard_map/ppermute | solution.py:305
  27.1 1.5 %collective-permute-done.3.__1_.g1 = bf16[4,32,512]{2,1,0:T(8,128)(2,1)S(1)} collective-permute-done((bf16[4,32,512]{2,1,0:T(8,128)(2,1)S(1)}, bf16[4,32,512]{2,1,0:T(8,128)(2,1)S(1)}, u32[]{:S(2)}, u32[]{:S(2)}) %collective-permute-start.3) | collective-permute-done | bytes 131104 | tf_op jit(solution)/shard_map/ppermute | solution.py:305
  28.6 1.1 %all-to-all-done = bf16[16,32,512]{2,1,0:T(8,128)(2,1)S(1)} async-done(((bf16[16,32,512]{2,1,0:T(8,128)(2,1)}), bf16[16,32,512]{2,1,0:T(8,128)(2,1)S(1)}, u32[]{:S(2)}, u32[]{:S(2)}) %all-to-all-start) | async-done | bytes 524320 | tf_op jit(solution)/shard_map/all_to_all | solution.py:315
  29.7 0.0 copy-start.1
  29.7 2.1 %collective-permute-start.6 = (bf16[512,512]{1,0:T(8,128)(2,1)S(1)}, bf16[512,512]{1,0:T(8,128)(2,1)S(1)}, u32[]{:S(2)}, u32[]{:S(2)}) collective-permute-start(bf16[512,512]{1,0:T(8,128)(2,1)S(1)} %shard_map.60.data_ref.refs_3_), channel_id=1, source_target_pairs={{0,16},{16,0},{32,48},{48,32},{64,80},{80,64},{96,112},{112,96},{1... | collective-permute-start | bytes 1572872 | tf_op jit(solution)/shard_map/ppermute | solution.py:322
  31.8 0.0 copy-done.1
  31.8 1.0 shard_map.61
  32.7 0.6 collective-permute-done.6.data_ref.refs_4_.more_ref
  33.3 0.5 shard_map.62.other_ref.refs_1_
  33.8 0.4 shard_map.63
  34.2 11.3 %all_to_all.25.refs_2_ = f32[16,4,128]{2,1,0:T(4,128)S(1)} all-to-all(f32[16,4,128]{2,1,0:T(4,128)S(1)} %shard_map.63), channel_id=1, replica_groups=mesh['row'=16,'col'=16] {'col'}, dimensions={0} | all-to-all | bytes 65536 | tf_op jit(solution)/shard_map/all_to_all | solution.py:340
  45.5 0.5 shard_map.64
  46.1 14.4 %all_to_all.26.refs_2_ = f32[16,8,128]{2,1,0:T(8,128)S(1)} all-to-all(f32[16,8,128]{2,1,0:T(8,128)S(1)} %shard_map.64), channel_id=1, replica_groups=mesh['row'=16,'col'=16] {'row'}, dimensions={0} | all-to-all | bytes 131072 | tf_op jit(solution)/shard_map/all_to_all | solution.py:347
  60.5 0.6 shard_map.65
  61.1 9.2 %all_to_all.27.refs_2_ = f32[16,4,128]{2,1,0:T(4,128)S(1)} all-to-all(f32[16,4,128]{2,1,0:T(4,128)S(1)} %shard_map.65), channel_id=1, replica_groups=mesh['row'=16,'col'=16] {'col'}, dimensions={0} | all-to-all | bytes 65536 | tf_op jit(solution)/shard_map/all_to_all | solution.py:340
  70.4 0.5 shard_map.66
  70.9 11.8 %all_to_all.28.refs_2_ = f32[16,8,128]{2,1,0:T(8,128)S(1)} all-to-all(f32[16,8,128]{2,1,0:T(8,128)S(1)} %shard_map.66), channel_id=1, replica_groups=mesh['row'=16,'col'=16] {'row'}, dimensions={0} | all-to-all | bytes 131072 | tf_op jit(solution)/shard_map/all_to_all | solution.py:347
  82.8 1.6 %shard_map.67 = (f32[8,128]{1,0:T(8,128)S(1)}, f32[8,128]{1,0:T(8,128)S(1)}, bf16[512,1024]{1,0:T(8,128)(2,1)S(1)}, bf16[512,1024]{1,0:T(8,128)(2,1)S(1)}, f32[5...) custom-call(f32[512,512]{1,0:T(8,128)S(1)} %get-tuple-element.19.refs_0_, ...), custom_call_target="tpu_custom_call" | custom-call | tf_op jit(solution)/shard_map/pallas_call | solution.py:27
  84.4 1.0 collective-permute-start.7
  85.4 0.6 collective-permute-start.8
  85.9 2.1 %collective-permute-start.9 = (f32[520,128]{1,0:T(8,128)S(1)}, f32[520,128]{1,0:T(8,128)S(1)}, u32[]{:S(2)}, u32[]{:S(2)}) collective-permute-start(f32[520,128]{1,0:T(8,128)S(1)} %get-tuple-element.27), channel_id=1, source_target_pairs={{0,3},{1,0},{2,1},{3,2},{4,7},{5,4},{6,5},{7,6},{8,11},{9,8},{10,9... | collective-permute-start | bytes 798728 | tf_op jit(solution)/shard_map/ppermute | solution.py:305
  88.0 0.8 shard_map.68.refs_0_
  88.9 2.7 %collective-permute-done.7.refs_1_ = f32[520,128]{1,0:T(8,128)S(1)} collective-permute-done((f32[520,128]{1,0:T(8,128)S(1)}, f32[520,128]{1,0:T(8,128)S(1)}, u32[]{:S(2)}, u32[]{:S(2)}) %collective-permute-start.7) | collective-permute-done | bytes 266272 | tf_op jit(solution)/shard_map/ppermute | solution.py:305
  91.6 2.8 %collective-permute-done.8.refs_2_ = f32[520,128]{1,0:T(8,128)S(1)} collective-permute-done((f32[520,128]{1,0:T(8,128)S(1)}, f32[520,128]{1,0:T(8,128)S(1)}, u32[]{:S(2)}, u32[]{:S(2)}) %collective-permute-start.8) | collective-permute-done | bytes 266272 | tf_op jit(solution)/shard_map/ppermute | solution.py:305
  94.4 0.0 collective-permute-done.9.refs_3_
  94.4 0.1 shard_map.69
  94.5 0.8 collective-permute-start.10
  95.3 0.8 collective-permute-start.11
  96.1 1.9 %collective-permute-start.12 = (f32[136,128]{1,0:T(8,128)S(1)}, f32[136,128]{1,0:T(8,128)S(1)}, u32[]{:S(2)}, u32[]{:S(2)}) collective-permute-start(f32[136,128]{1,0:T(8,128)S(1)} %get-tuple-element.31), channel_id=1, source_target_pairs={{0,12},{1,13},{2,14},{3,15},{4,0},{5,1},{6,2},{7,3},{8,4},{9,5},{1... | collective-permute-start | bytes 208904 | tf_op jit(solution)/shard_map/ppermute | solution.py:305
  97.9 0.6 copy.8
  98.5 0.8 collective-permute-done.10.refs_1_
  99.3 1.0 collective-permute-done.11.refs_2_
  100.3 0.0 collective-permute-done.12.refs_3_
  100.3 0.7 shard_map.70
  (2 shorter events, 0.0 us)
Async XLA Ops:
  2.4 10.0 %copy-start = (bf16[32,512]{1,0:T(8,128)(2,1)S(1)}, bf16[32,512]{1,0:T(8,128)(2,1)}, u32[]{:S(2)}) copy-start(bf16[32,512]{1,0:T(8,128)(2,1)} %refs_0_.1) | copy-start | bytes 98308
  2.4 27.3 %all-to-all-start = ((bf16[16,32,512]{2,1,0:T(8,128)(2,1)}), bf16[16,32,512]{2,1,0:T(8,128)(2,1)S(1)}, u32[]{:S(2)}, u32[]{:S(2)}) async-start(bf16[16,32,512]{2,1,0:T(8,128)(2,1)} %shard_map.59), calls=%async_computation | async-start | bytes 1048576 | tf_op jit(solution)/shard_map/all_to_all | solution.py:315
  12.4 4.5 %collective-permute-start.1 = (bf16[32,512]{1,0:T(8,128)(2,1)S(1)}, bf16[32,512]{1,0:T(8,128)(2,1)S(1)}, u32[]{:S(2)}, u32[]{:S(2)}) collective-permute-start(bf16[32,512]{1,0:T(8,128)(2,1)S(1)} %copy-done), channel_id=1, source_target_pairs={{0,1},{1,2},{2,3},{3,0},{4,5},{5,6},{6,7},{7,4},{8,9},{9,10},{10,1... | collective-permute-start | bytes 98312 | tf_op jit(solution)/shard_map/ppermute | solution.py:305
  13.8 3.1 %collective-permute-start = (bf16[32,512]{1,0:T(8,128)(2,1)S(1)}, bf16[32,512]{1,0:T(8,128)(2,1)S(1)}, u32[]{:S(2)}, u32[]{:S(2)}) collective-permute-start(bf16[32,512]{1,0:T(8,128)(2,1)S(1)} %copy-done), channel_id=1, source_target_pairs={{0,3},{1,0},{2,1},{3,2},{4,7},{5,4},{6,5},{7,6},{8,11},{9,8},{10,9... | collective-permute-start | bytes 98312 | tf_op jit(solution)/shard_map/ppermute | solution.py:305
  15.3 4.6 %collective-permute-start.2 = (bf16[32,512]{1,0:T(8,128)(2,1)S(1)}, bf16[32,512]{1,0:T(8,128)(2,1)S(1)}, u32[]{:S(2)}, u32[]{:S(2)}) collective-permute-start(bf16[32,512]{1,0:T(8,128)(2,1)S(1)} %copy-done), channel_id=1, source_target_pairs={{0,2},{1,3},{2,0},{3,1},{4,6},{5,7},{6,4},{7,5},{8,10},{9,11},{10,... | collective-permute-start | bytes 98312 | tf_op jit(solution)/shard_map/ppermute | solution.py:305
  19.9 5.4 %collective-permute-start.5 = (bf16[4,32,512]{2,1,0:T(8,128)(2,1)S(1)}, bf16[4,32,512]{2,1,0:T(8,128)(2,1)S(1)}, u32[]{:S(2)}, u32[]{:S(2)}) collective-permute-start(bf16[4,32,512]{2,1,0:T(8,128)(2,1)S(1)} %shard_map.58.g0), channel_id=1, source_target_pairs={{0,8},{1,9},{2,10},{3,11},{4,12},{5,13},{6,14},{7,15},{8,0},{9,1},... | collective-permute-start | bytes 393224 | tf_op jit(solution)/shard_map/ppermute | solution.py:305
  22.7 4.4 %collective-permute-start.4 = (bf16[4,32,512]{2,1,0:T(8,128)(2,1)S(1)}, bf16[4,32,512]{2,1,0:T(8,128)(2,1)S(1)}, u32[]{:S(2)}, u32[]{:S(2)}) collective-permute-start(bf16[4,32,512]{2,1,0:T(8,128)(2,1)S(1)} %shard_map.58.g0), channel_id=1, source_target_pairs={{0,12},{1,13},{2,14},{3,15},{4,0},{5,1},{6,2},{7,3},{8,4},{9,5},{1... | collective-permute-start | bytes 393224 | tf_op jit(solution)/shard_map/ppermute | solution.py:305
  23.6 5.0 %collective-permute-start.3 = (bf16[4,32,512]{2,1,0:T(8,128)(2,1)S(1)}, bf16[4,32,512]{2,1,0:T(8,128)(2,1)S(1)}, u32[]{:S(2)}, u32[]{:S(2)}) collective-permute-start(bf16[4,32,512]{2,1,0:T(8,128)(2,1)S(1)} %shard_map.58.g0), channel_id=1, source_target_pairs={{0,4},{1,5},{2,6},{3,7},{4,8},{5,9},{6,10},{7,11},{8,12},{9,13},{1... | collective-permute-start | bytes 393224 | tf_op jit(solution)/shard_map/ppermute | solution.py:305
  29.7 2.1 %copy-start.1 = (f32[1024]{0:T(1024)S(1)}, f32[1024]{0:T(1024)}, u32[]{:S(2)}) copy-start(f32[1024]{0:T(1024)} %param.5) | copy-start | bytes 12292
  29.7 3.6 %collective-permute-start.6 = (bf16[512,512]{1,0:T(8,128)(2,1)S(1)}, bf16[512,512]{1,0:T(8,128)(2,1)S(1)}, u32[]{:S(2)}, u32[]{:S(2)}) collective-permute-start(bf16[512,512]{1,0:T(8,128)(2,1)S(1)} %shard_map.60.data_ref.refs_3_), channel_id=1, source_target_pairs={{0,16},{16,0},{32,48},{48,32},{64,80},{80,64},{96,112},{112,96},{1... | collective-permute-start | bytes 1572872 | tf_op jit(solution)/shard_map/ppermute | solution.py:322
  84.4 7.2 %collective-permute-start.7 = (f32[520,128]{1,0:T(8,128)S(1)}, f32[520,128]{1,0:T(8,128)S(1)}, u32[]{:S(2)}, u32[]{:S(2)}) collective-permute-start(f32[520,128]{1,0:T(8,128)S(1)} %get-tuple-element.25), channel_id=1, source_target_pairs={{0,2},{1,3},{2,0},{3,1},{4,6},{5,7},{6,4},{7,5},{8,10},{9,11},{10,... | collective-permute-start | bytes 798728 | tf_op jit(solution)/shard_map/ppermute | solution.py:305
  85.4 9.0 %collective-permute-start.8 = (f32[520,128]{1,0:T(8,128)S(1)}, f32[520,128]{1,0:T(8,128)S(1)}, u32[]{:S(2)}, u32[]{:S(2)}) collective-permute-start(f32[520,128]{1,0:T(8,128)S(1)} %get-tuple-element.26), channel_id=1, source_target_pairs={{0,1},{1,2},{2,3},{3,0},{4,5},{5,6},{6,7},{7,4},{8,9},{9,10},{10,1... | collective-permute-start | bytes 798728 | tf_op jit(solution)/shard_map/ppermute | solution.py:305
  85.9 8.5 %collective-permute-start.9 = (f32[520,128]{1,0:T(8,128)S(1)}, f32[520,128]{1,0:T(8,128)S(1)}, u32[]{:S(2)}, u32[]{:S(2)}) collective-permute-start(f32[520,128]{1,0:T(8,128)S(1)} %get-tuple-element.27), channel_id=1, source_target_pairs={{0,3},{1,0},{2,1},{3,2},{4,7},{5,4},{6,5},{7,6},{8,11},{9,8},{10,9... | collective-permute-start | bytes 798728 | tf_op jit(solution)/shard_map/ppermute | solution.py:305
  94.5 4.8 %collective-permute-start.10 = (f32[136,128]{1,0:T(8,128)S(1)}, f32[136,128]{1,0:T(8,128)S(1)}, u32[]{:S(2)}, u32[]{:S(2)}) collective-permute-start(f32[136,128]{1,0:T(8,128)S(1)} %get-tuple-element.29), channel_id=1, source_target_pairs={{0,8},{1,9},{2,10},{3,11},{4,12},{5,13},{6,14},{7,15},{8,0},{9,1},... | collective-permute-start | bytes 208904 | tf_op jit(solution)/shard_map/ppermute | solution.py:305
  95.3 5.0 %collective-permute-start.11 = (f32[136,128]{1,0:T(8,128)S(1)}, f32[136,128]{1,0:T(8,128)S(1)}, u32[]{:S(2)}, u32[]{:S(2)}) collective-permute-start(f32[136,128]{1,0:T(8,128)S(1)} %get-tuple-element.30), channel_id=1, source_target_pairs={{0,4},{1,5},{2,6},{3,7},{4,8},{5,9},{6,10},{7,11},{8,12},{9,13},{1... | collective-permute-start | bytes 208904 | tf_op jit(solution)/shard_map/ppermute | solution.py:305
  96.1 4.2 %collective-permute-start.12 = (f32[136,128]{1,0:T(8,128)S(1)}, f32[136,128]{1,0:T(8,128)S(1)}, u32[]{:S(2)}, u32[]{:S(2)}) collective-permute-start(f32[136,128]{1,0:T(8,128)S(1)} %get-tuple-element.31), channel_id=1, source_target_pairs={{0,12},{1,13},{2,14},{3,15},{4,0},{5,1},{6,2},{7,3},{8,4},{9,5},{1... | collective-permute-start | bytes 208904 | tf_op jit(solution)/shard_map/ppermute | solution.py:305

commit v8 on v7

--- a/solution.py
+++ b/solution.py
@@ -114,8 +114,8 @@
     column, core = lax.axis_index("col"), lax.axis_index("row") % 2
     for second, ref in zip(GATHER[1], (g0, g1, g2, g3)):
         for n, first in enumerate(GATHER[0]):
-            y_back = jnp.where(core == 0, second, first)
-            x_back = jnp.where(core == 0, first, second)
+            y_back = jnp.where(core == 0, second, -first)
+            x_back = jnp.where(core == 0, first, -second)
             place = (column // side - y_back + side) % side * side + (column % side - x_back + side) % side
             gen_ref[pl.ds(pl.multiple_of(place * size, size), size), :] = ref[n, :, :]
     line = halves(swap_halves(pot_ref[...] * SCALE))[0]
@@ -294,13 +294,14 @@
 
     side = math.isqrt(cols_n)
 
-    def hop(array, phase, back):
+    def hop(array, phase, back, mirrored=False):
         pairs = []
         for row in range(rows_n):
             for y in range(side):
                 for x in range(side):
                     along_y = (row + phase) % 2
-                    to_y, to_x = (y + back * along_y) % side, (x + back * (1 - along_y)) % side
+                    way = -back if mirrored and row % 2 else back
+                    to_y, to_x = (y + way * along_y) % side, (x + way * (1 - along_y)) % side
                     pairs.append(((row * side + y) * side + x, (row * side + to_y) * side + to_x))
         return lax.ppermute(array, ("row", "col"), pairs)
 
@@ -313,8 +314,8 @@
         space=pltpu.HBM,
     )
     own = lax.all_to_all(outgoing, "row", 0, 0).reshape(features, half)
-    stack = kernel_call(stack_kernel, shaped((side,) + gen_points.shape, dtype), (gen_points, *(hop(gen_points, 0, back) for back in GATHER[0][1:])))
-    stacks = (stack,) + tuple(hop(stack, 1, back) for back in GATHER[1][1:])
+    stack = kernel_call(stack_kernel, shaped((side,) + gen_points.shape, dtype), (gen_points, *(hop(gen_points, 0, back, True) for back in GATHER[0][1:])))
+    stacks = (stack,) + tuple(hop(stack, 1, back, True) for back in GATHER[1][1:])
 
     start = data_potential.reshape(data_chunks, LANES)
 

time: 102 us -> 102 us (level)
  starting transfers between devices: 27.9 us -> 29.1 us
  waiting for transfers between devices: 16.4 us -> 15.2 us
    ppermute x12, waiting for transfers between devices: 14.7 us -> 12.6 us  [hop(): return lax.ppermute(array, ('row', 'col'), pairs)]
    ppermute x12, starting transfers between devices: 15.9 us -> 17.1 us  [hop(): return lax.ppermute(array, ('row', 'col'), pairs)]
  transfers between devices with their start and end apart: 14 -> 14, of which waited for: 10 -> 8; matrix products, arithmetic and copies ran while one was open for 1% -> 1% of each run, Pallas kernels for 2% -> 2%
where the time goes in v8:
time: 102 us; the launch traced here: 101 us
  blocking collectives  46.8 us (46%)
  starting transfers between devices  29.1 us (29%)
  waiting for transfers between devices  15.2 us (15%)
  Pallas kernels  8.51 us (8%)
    all_to_all x2, blocking collectives, local(): got = lax.all_to_all(lines, 'row', 0, 0)  26.3 us
    all_to_all x2, blocking collectives, local(): got = lax.all_to_all(lines, 'col', 0, 0)  20.6 us
    ppermute x12, starting transfers between devices, hop(): return lax.ppermute(array, ('row', 'col'), pairs)  17.1 us
    ppermute x12, waiting for transfers between devices, hop(): return lax.ppermute(array, ('row', 'col'), pairs)  12.6 us
    all_to_all x1, starting transfers between devices, local(): own = lax.all_to_all(outgoing, 'row', 0, 0).reshape(features, half)  9.99 us
    pallas_call x13, Pallas kernels, kernel_call(): pl.pallas_call(body, out_shape=out_shape, in_specs=[whole] * len(args), o...  8.51 us
    ppermute x1, starting transfers between devices, local(): lax.ppermute(own, 'row', [(i, i ^ 1) for i in range(rows_n)])  2.06 us
  transfers between devices with their start and end apart: 14, of which 8 were waited for; matrix products, arithmetic and copies ran while one was open for 1% of the time, Pallas kernels for 2%

profile of v8, /device:TPU:1, one launch (start us, length us, event | category | flops | bytes accessed | tf_op | source)
XLA Modules:
  0.0 101.0 jit_solution(14910600625792574767)
XLA Ops:
  0.6 1.7 %shard_map.59 = bf16[16,32,512]{2,1,0:T(8,128)(2,1)} custom-call(bf16[32,1024]{1,0:T(8,128)(2,1)} %bitcast.9), custom_call_target="tpu_custom_call" | custom-call | tf_op jit(solution)/shard_map/pallas_call | solution.py:27
  2.4 0.0 copy-start
  2.4 10.0 %all-to-all-start = ((bf16[16,32,512]{2,1,0:T(8,128)(2,1)}), bf16[16,32,512]{2,1,0:T(8,128)(2,1)S(1)}, u32[]{:S(2)}, u32[]{:S(2)}) async-start(bf16[16,32,512]{2,1,0:T(8,128)(2,1)} %shard_map.59), calls=%async_computation | async-start | bytes 1048576 | tf_op jit(solution)/shard_map/all_to_all | solution.py:316
  12.4 0.0 copy-done
  12.4 2.8 %collective-permute-start.1 = (bf16[32,512]{1,0:T(8,128)(2,1)S(1)}, bf16[32,512]{1,0:T(8,128)(2,1)S(1)}, u32[]{:S(2)}, u32[]{:S(2)}) collective-permute-start(bf16[32,512]{1,0:T(8,128)(2,1)S(1)} %copy-done), channel_id=1, source_target_pairs={{0,1},{1,2},{2,3},{3,0},{4,5},{5,6},{6,7},{7,4},{8,9},{9,10},{10,1... | collective-permute-start | bytes 98312 | tf_op jit(solution)/shard_map/ppermute | solution.py:306
  15.2 0.0 collective-permute-start
  15.2 1.6 %collective-permute-start.2 = (bf16[32,512]{1,0:T(8,128)(2,1)S(1)}, bf16[32,512]{1,0:T(8,128)(2,1)S(1)}, u32[]{:S(2)}, u32[]{:S(2)}) collective-permute-start(bf16[32,512]{1,0:T(8,128)(2,1)S(1)} %copy-done), channel_id=1, source_target_pairs={{0,2},{1,3},{2,0},{3,1},{4,6},{5,7},{6,4},{7,5},{8,10},{9,11},{10,... | collective-permute-start | bytes 98312 | tf_op jit(solution)/shard_map/ppermute | solution.py:306
  16.8 0.0 collective-permute-done.1.refs_2_
  16.8 2.6 %collective-permute-done.refs_1_ = bf16[32,512]{1,0:T(8,128)(2,1)S(1)} collective-permute-done((bf16[32,512]{1,0:T(8,128)(2,1)S(1)}, bf16[32,512]{1,0:T(8,128)(2,1)S(1)}, u32[]{:S(2)}, u32[]{:S(2)}) %collective-permute-start) | collective-permute-done | bytes 32800 | tf_op jit(solution)/shard_map/ppermute | solution.py:306
  19.5 0.0 collective-permute-done.2.refs_3_
  19.5 2.8 %collective-permute-start.5 = (bf16[4,32,512]{2,1,0:T(8,128)(2,1)S(1)}, bf16[4,32,512]{2,1,0:T(8,128)(2,1)S(1)}, u32[]{:S(2)}, u32[]{:S(2)}) collective-permute-start(bf16[4,32,512]{2,1,0:T(8,128)(2,1)S(1)} %shard_map.58.g0), channel_id=1, source_target_pairs={{0,8},{1,9},{2,10},{3,11},{4,12},{5,13},{6,14},{7,15},{8,0},{9,1},... | collective-permute-start | bytes 393224 | tf_op jit(solution)/shard_map/ppermute | solution.py:306
  22.4 0.4 collective-permute-start.4
  22.8 2.3 %collective-permute-start.3 = (bf16[4,32,512]{2,1,0:T(8,128)(2,1)S(1)}, bf16[4,32,512]{2,1,0:T(8,128)(2,1)S(1)}, u32[]{:S(2)}, u32[]{:S(2)}) collective-permute-start(bf16[4,32,512]{2,1,0:T(8,128)(2,1)S(1)} %shard_map.58.g0), channel_id=1, source_target_pairs={{0,4},{1,5},{2,6},{3,7},{4,8},{5,9},{6,10},{7,11},{8,12},{9,13},{1... | collective-permute-start | bytes 393224 | tf_op jit(solution)/shard_map/ppermute | solution.py:306
  25.0 0.0 collective-permute-done.5.__3_.g3
  25.0 2.6 %collective-permute-done.4.__2_.g2 = bf16[4,32,512]{2,1,0:T(8,128)(2,1)S(1)} collective-permute-done((bf16[4,32,512]{2,1,0:T(8,128)(2,1)S(1)}, bf16[4,32,512]{2,1,0:T(8,128)(2,1)S(1)}, u32[]{:S(2)}, u32[]{:S(2)}) %collective-permute-start.4) | collective-permute-done | bytes 131104 | tf_op jit(solution)/shard_map/ppermute | solution.py:306
  27.7 0.0 collective-permute-done.3.__1_.g1
  27.7 2.0 %all-to-all-done = bf16[16,32,512]{2,1,0:T(8,128)(2,1)S(1)} async-done(((bf16[16,32,512]{2,1,0:T(8,128)(2,1)}), bf16[16,32,512]{2,1,0:T(8,128)(2,1)S(1)}, u32[]{:S(2)}, u32[]{:S(2)}) %all-to-all-start) | async-done | bytes 524320 | tf_op jit(solution)/shard_map/all_to_all | solution.py:316
  29.7 0.0 copy-start.1
  29.7 2.1 %collective-permute-start.6 = (bf16[512,512]{1,0:T(8,128)(2,1)S(1)}, bf16[512,512]{1,0:T(8,128)(2,1)S(1)}, u32[]{:S(2)}, u32[]{:S(2)}) collective-permute-start(bf16[512,512]{1,0:T(8,128)(2,1)S(1)} %shard_map.60.data_ref.refs_3_), channel_id=1, source_target_pairs={{0,16},{16,0},{32,48},{48,32},{64,80},{80,64},{96,112},{112,96},{1... | collective-permute-start | bytes 1572872 | tf_op jit(solution)/shard_map/ppermute | solution.py:323
  31.8 0.0 copy-done.1
  31.8 1.0 shard_map.61
  32.7 0.6 collective-permute-done.6.data_ref.refs_4_.more_ref
  33.3 0.5 shard_map.62.other_ref.refs_1_
  33.8 0.4 shard_map.63
  34.2 11.3 %all_to_all.25.refs_2_ = f32[16,4,128]{2,1,0:T(4,128)S(1)} all-to-all(f32[16,4,128]{2,1,0:T(4,128)S(1)} %shard_map.63), channel_id=1, replica_groups=mesh['row'=16,'col'=16] {'col'}, dimensions={0} | all-to-all | bytes 65536 | tf_op jit(solution)/shard_map/all_to_all | solution.py:341
  45.5 0.5 shard_map.64
  46.1 14.4 %all_to_all.26.refs_2_ = f32[16,8,128]{2,1,0:T(8,128)S(1)} all-to-all(f32[16,8,128]{2,1,0:T(8,128)S(1)} %shard_map.64), channel_id=1, replica_groups=mesh['row'=16,'col'=16] {'row'}, dimensions={0} | all-to-all | bytes 131072 | tf_op jit(solution)/shard_map/all_to_all | solution.py:348
  60.5 0.6 shard_map.65
  61.1 9.2 %all_to_all.27.refs_2_ = f32[16,4,128]{2,1,0:T(4,128)S(1)} all-to-all(f32[16,4,128]{2,1,0:T(4,128)S(1)} %shard_map.65), channel_id=1, replica_groups=mesh['row'=16,'col'=16] {'col'}, dimensions={0} | all-to-all | bytes 65536 | tf_op jit(solution)/shard_map/all_to_all | solution.py:341
  70.4 0.5 shard_map.66
  70.9 11.8 %all_to_all.28.refs_2_ = f32[16,8,128]{2,1,0:T(8,128)S(1)} all-to-all(f32[16,8,128]{2,1,0:T(8,128)S(1)} %shard_map.66), channel_id=1, replica_groups=mesh['row'=16,'col'=16] {'row'}, dimensions={0} | all-to-all | bytes 131072 | tf_op jit(solution)/shard_map/all_to_all | solution.py:348
  82.8 1.6 %shard_map.67 = (f32[8,128]{1,0:T(8,128)S(1)}, f32[8,128]{1,0:T(8,128)S(1)}, bf16[512,1024]{1,0:T(8,128)(2,1)S(1)}, bf16[512,1024]{1,0:T(8,128)(2,1)S(1)}, f32[5...) custom-call(f32[512,512]{1,0:T(8,128)S(1)} %get-tuple-element.19.refs_0_, ...), custom_call_target="tpu_custom_call" | custom-call | tf_op jit(solution)/shard_map/pallas_call | solution.py:27
  84.4 1.0 collective-permute-start.7
  85.4 0.6 collective-permute-start.8
  85.9 2.1 %collective-permute-start.9 = (f32[520,128]{1,0:T(8,128)S(1)}, f32[520,128]{1,0:T(8,128)S(1)}, u32[]{:S(2)}, u32[]{:S(2)}) collective-permute-start(f32[520,128]{1,0:T(8,128)S(1)} %get-tuple-element.27), channel_id=1, source_target_pairs={{0,3},{1,0},{2,1},{3,2},{4,7},{5,4},{6,5},{7,6},{8,11},{9,8},{10,9... | collective-permute-start | bytes 798728 | tf_op jit(solution)/shard_map/ppermute | solution.py:306
  88.0 0.8 shard_map.68.refs_0_
  88.9 2.7 %collective-permute-done.7.refs_1_ = f32[520,128]{1,0:T(8,128)S(1)} collective-permute-done((f32[520,128]{1,0:T(8,128)S(1)}, f32[520,128]{1,0:T(8,128)S(1)}, u32[]{:S(2)}, u32[]{:S(2)}) %collective-permute-start.7) | collective-permute-done | bytes 266272 | tf_op jit(solution)/shard_map/ppermute | solution.py:306
  91.6 2.8 %collective-permute-done.8.refs_2_ = f32[520,128]{1,0:T(8,128)S(1)} collective-permute-done((f32[520,128]{1,0:T(8,128)S(1)}, f32[520,128]{1,0:T(8,128)S(1)}, u32[]{:S(2)}, u32[]{:S(2)}) %collective-permute-start.8) | collective-permute-done | bytes 266272 | tf_op jit(solution)/shard_map/ppermute | solution.py:306
  94.4 0.0 collective-permute-done.9.refs_3_
  94.4 0.1 shard_map.69
  94.5 0.8 collective-permute-start.10
  95.3 0.8 collective-permute-start.11
  96.1 1.9 %collective-permute-start.12 = (f32[136,128]{1,0:T(8,128)S(1)}, f32[136,128]{1,0:T(8,128)S(1)}, u32[]{:S(2)}, u32[]{:S(2)}) collective-permute-start(f32[136,128]{1,0:T(8,128)S(1)} %get-tuple-element.31), channel_id=1, source_target_pairs={{0,12},{1,13},{2,14},{3,15},{4,0},{5,1},{6,2},{7,3},{8,4},{9,5},{1... | collective-permute-start | bytes 208904 | tf_op jit(solution)/shard_map/ppermute | solution.py:306
  97.9 0.6 copy.8
  98.5 0.8 collective-permute-done.10.refs_1_
  99.3 1.0 collective-permute-done.11.refs_2_
  100.3 0.0 collective-permute-done.12.refs_3_
  100.3 0.7 shard_map.70
  (2 shorter events, 0.0 us)
Async XLA Ops:
  2.4 10.0 %copy-start = (bf16[32,512]{1,0:T(8,128)(2,1)S(1)}, bf16[32,512]{1,0:T(8,128)(2,1)}, u32[]{:S(2)}) copy-start(bf16[32,512]{1,0:T(8,128)(2,1)} %refs_0_.1) | copy-start | bytes 98308
  2.4 27.3 %all-to-all-start = ((bf16[16,32,512]{2,1,0:T(8,128)(2,1)}), bf16[16,32,512]{2,1,0:T(8,128)(2,1)S(1)}, u32[]{:S(2)}, u32[]{:S(2)}) async-start(bf16[16,32,512]{2,1,0:T(8,128)(2,1)} %shard_map.59), calls=%async_computation | async-start | bytes 1048576 | tf_op jit(solution)/shard_map/all_to_all | solution.py:316
  12.4 4.5 %collective-permute-start.1 = (bf16[32,512]{1,0:T(8,128)(2,1)S(1)}, bf16[32,512]{1,0:T(8,128)(2,1)S(1)}, u32[]{:S(2)}, u32[]{:S(2)}) collective-permute-start(bf16[32,512]{1,0:T(8,128)(2,1)S(1)} %copy-done), channel_id=1, source_target_pairs={{0,1},{1,2},{2,3},{3,0},{4,5},{5,6},{6,7},{7,4},{8,9},{9,10},{10,1... | collective-permute-start | bytes 98312 | tf_op jit(solution)/shard_map/ppermute | solution.py:306
  15.2 4.3 %collective-permute-start = (bf16[32,512]{1,0:T(8,128)(2,1)S(1)}, bf16[32,512]{1,0:T(8,128)(2,1)S(1)}, u32[]{:S(2)}, u32[]{:S(2)}) collective-permute-start(bf16[32,512]{1,0:T(8,128)(2,1)S(1)} %copy-done), channel_id=1, source_target_pairs={{0,3},{1,0},{2,1},{3,2},{4,7},{5,4},{6,5},{7,6},{8,11},{9,8},{10,9... | collective-permute-start | bytes 98312 | tf_op jit(solution)/shard_map/ppermute | solution.py:306
  15.2 4.3 %collective-permute-start.2 = (bf16[32,512]{1,0:T(8,128)(2,1)S(1)}, bf16[32,512]{1,0:T(8,128)(2,1)S(1)}, u32[]{:S(2)}, u32[]{:S(2)}) collective-permute-start(bf16[32,512]{1,0:T(8,128)(2,1)S(1)} %copy-done), channel_id=1, source_target_pairs={{0,2},{1,3},{2,0},{3,1},{4,6},{5,7},{6,4},{7,5},{8,10},{9,11},{10,... | collective-permute-start | bytes 98312 | tf_op jit(solution)/shard_map/ppermute | solution.py:306
  19.5 5.5 %collective-permute-start.5 = (bf16[4,32,512]{2,1,0:T(8,128)(2,1)S(1)}, bf16[4,32,512]{2,1,0:T(8,128)(2,1)S(1)}, u32[]{:S(2)}, u32[]{:S(2)}) collective-permute-start(bf16[4,32,512]{2,1,0:T(8,128)(2,1)S(1)} %shard_map.58.g0), channel_id=1, source_target_pairs={{0,8},{1,9},{2,10},{3,11},{4,12},{5,13},{6,14},{7,15},{8,0},{9,1},... | collective-permute-start | bytes 393224 | tf_op jit(solution)/shard_map/ppermute | solution.py:306
  22.4 5.3 %collective-permute-start.4 = (bf16[4,32,512]{2,1,0:T(8,128)(2,1)S(1)}, bf16[4,32,512]{2,1,0:T(8,128)(2,1)S(1)}, u32[]{:S(2)}, u32[]{:S(2)}) collective-permute-start(bf16[4,32,512]{2,1,0:T(8,128)(2,1)S(1)} %shard_map.58.g0), channel_id=1, source_target_pairs={{0,12},{1,13},{2,14},{3,15},{4,0},{5,1},{6,2},{7,3},{8,4},{9,5},{1... | collective-permute-start | bytes 393224 | tf_op jit(solution)/shard_map/ppermute | solution.py:306
  22.8 4.9 %collective-permute-start.3 = (bf16[4,32,512]{2,1,0:T(8,128)(2,1)S(1)}, bf16[4,32,512]{2,1,0:T(8,128)(2,1)S(1)}, u32[]{:S(2)}, u32[]{:S(2)}) collective-permute-start(bf16[4,32,512]{2,1,0:T(8,128)(2,1)S(1)} %shard_map.58.g0), channel_id=1, source_target_pairs={{0,4},{1,5},{2,6},{3,7},{4,8},{5,9},{6,10},{7,11},{8,12},{9,13},{1... | collective-permute-start | bytes 393224 | tf_op jit(solution)/shard_map/ppermute | solution.py:306
  29.7 2.1 %copy-start.1 = (f32[1024]{0:T(1024)S(1)}, f32[1024]{0:T(1024)}, u32[]{:S(2)}) copy-start(f32[1024]{0:T(1024)} %param.5) | copy-start | bytes 12292
  29.7 3.6 %collective-permute-start.6 = (bf16[512,512]{1,0:T(8,128)(2,1)S(1)}, bf16[512,512]{1,0:T(8,128)(2,1)S(1)}, u32[]{:S(2)}, u32[]{:S(2)}) collective-permute-start(bf16[512,512]{1,0:T(8,128)(2,1)S(1)} %shard_map.60.data_ref.refs_3_), channel_id=1, source_target_pairs={{0,16},{16,0},{32,48},{48,32},{64,80},{80,64},{96,112},{112,96},{1... | collective-permute-start | bytes 1572872 | tf_op jit(solution)/shard_map/ppermute | solution.py:323
  84.4 7.2 %collective-permute-start.7 = (f32[520,128]{1,0:T(8,128)S(1)}, f32[520,128]{1,0:T(8,128)S(1)}, u32[]{:S(2)}, u32[]{:S(2)}) collective-permute-start(f32[520,128]{1,0:T(8,128)S(1)} %get-tuple-element.25), channel_id=1, source_target_pairs={{0,2},{1,3},{2,0},{3,1},{4,6},{5,7},{6,4},{7,5},{8,10},{9,11},{10,... | collective-permute-start | bytes 798728 | tf_op jit(solution)/shard_map/ppermute | solution.py:306
  85.4 9.0 %collective-permute-start.8 = (f32[520,128]{1,0:T(8,128)S(1)}, f32[520,128]{1,0:T(8,128)S(1)}, u32[]{:S(2)}, u32[]{:S(2)}) collective-permute-start(f32[520,128]{1,0:T(8,128)S(1)} %get-tuple-element.26), channel_id=1, source_target_pairs={{0,1},{1,2},{2,3},{3,0},{4,5},{5,6},{6,7},{7,4},{8,9},{9,10},{10,1... | collective-permute-start | bytes 798728 | tf_op jit(solution)/shard_map/ppermute | solution.py:306
  85.9 8.5 %collective-permute-start.9 = (f32[520,128]{1,0:T(8,128)S(1)}, f32[520,128]{1,0:T(8,128)S(1)}, u32[]{:S(2)}, u32[]{:S(2)}) collective-permute-start(f32[520,128]{1,0:T(8,128)S(1)} %get-tuple-element.27), channel_id=1, source_target_pairs={{0,3},{1,0},{2,1},{3,2},{4,7},{5,4},{6,5},{7,6},{8,11},{9,8},{10,9... | collective-permute-start | bytes 798728 | tf_op jit(solution)/shard_map/ppermute | solution.py:306
  94.5 4.8 %collective-permute-start.10 = (f32[136,128]{1,0:T(8,128)S(1)}, f32[136,128]{1,0:T(8,128)S(1)}, u32[]{:S(2)}, u32[]{:S(2)}) collective-permute-start(f32[136,128]{1,0:T(8,128)S(1)} %get-tuple-element.29), channel_id=1, source_target_pairs={{0,8},{1,9},{2,10},{3,11},{4,12},{5,13},{6,14},{7,15},{8,0},{9,1},... | collective-permute-start | bytes 208904 | tf_op jit(solution)/shard_map/ppermute | solution.py:306
  95.3 5.0 %collective-permute-start.11 = (f32[136,128]{1,0:T(8,128)S(1)}, f32[136,128]{1,0:T(8,128)S(1)}, u32[]{:S(2)}, u32[]{:S(2)}) collective-permute-start(f32[136,128]{1,0:T(8,128)S(1)} %get-tuple-element.30), channel_id=1, source_target_pairs={{0,4},{1,5},{2,6},{3,7},{4,8},{5,9},{6,10},{7,11},{8,12},{9,13},{1... | collective-permute-start | bytes 208904 | tf_op jit(solution)/shard_map/ppermute | solution.py:306
  96.1 4.2 %collective-permute-start.12 = (f32[136,128]{1,0:T(8,128)S(1)}, f32[136,128]{1,0:T(8,128)S(1)}, u32[]{:S(2)}, u32[]{:S(2)}) collective-permute-start(f32[136,128]{1,0:T(8,128)S(1)} %get-tuple-element.31), channel_id=1, source_target_pairs={{0,12},{1,13},{2,14},{3,15},{4,0},{5,1},{6,2},{7,3},{8,4},{9,5},{1... | collective-permute-start | bytes 208904 | tf_op jit(solution)/shard_map/ppermute | solution.py:306

commit v9 on v8

--- a/solution.py
+++ b/solution.py
@@ -14,6 +14,7 @@
 SCALE = 1.0 / (EPS * LN2)
 LANES = 128
 OFFSETS = (0, 2, 1, -1)
+RELAY = (0, 1, 2, -1)
 GATHER = ((0, -1, 1, 2), (0, 1, -1, 2))
 STATS = 8
 
@@ -255,7 +256,7 @@
     feats = size // chunks
     column, core = lax.axis_index("col"), lax.axis_index("row") % 2
     place = jnp.where(core == 0, column // side, column % side)
-    for offset, out_ref in zip(OFFSETS, outs):
+    for offset, out_ref in zip(RELAY, outs):
         start = (place + offset + side) % side * size
         for n in range(chunks):
             source = pl.ds(pl.multiple_of(start + n * feats, feats), feats)
@@ -365,7 +366,7 @@
     gen_pot, target = kernel_call(
         at(merge_kernel, log_data),
         (shaped((gen_chunks, LANES), f32), shaped((feats, gen_rows), f32)),
-        [blocks[0]] + [hop(block, 1, back) for block, back in zip(blocks[1:], OFFSETS[1:])],
+        [blocks[0]] + [hop(block, 1, back) for block, back in zip(blocks[1:], RELAY[1:])],
     )
     return (gen_pot.reshape(gen_rows), potential.reshape(data_cols), target)
 

time: 102 us -> 102 us (level)
  no operation moved by 1% of the time
where the time goes in v9:
time: 102 us; the launch traced here: 101 us
  blocking collectives  46.8 us (46%)
  starting transfers between devices  28.5 us (28%)
  waiting for transfers between devices  16 us (16%)
  Pallas kernels  8.51 us (8%)
    all_to_all x2, blocking collectives, local(): got = lax.all_to_all(lines, 'row', 0, 0)  26.3 us
    all_to_all x2, blocking collectives, local(): got = lax.all_to_all(lines, 'col', 0, 0)  20.6 us
    ppermute x12, starting transfers between devices, hop(): return lax.ppermute(array, ('row', 'col'), pairs)  16.5 us
    ppermute x12, waiting for transfers between devices, hop(): return lax.ppermute(array, ('row', 'col'), pairs)  13.5 us
    all_to_all x1, starting transfers between devices, local(): own = lax.all_to_all(outgoing, 'row', 0, 0).reshape(features, half)  9.99 us
    pallas_call x13, Pallas kernels, kernel_call(): pl.pallas_call(body, out_shape=out_shape, in_specs=[whole] * len(args), o...  8.51 us
    ppermute x1, starting transfers between devices, local(): lax.ppermute(own, 'row', [(i, i ^ 1) for i in range(rows_n)])  2.06 us
  transfers between devices with their start and end apart: 14, of which 8 were waited for; matrix products, arithmetic and copies ran while one was open for 1% of the time, Pallas kernels for 2%

profile of v9, /device:TPU:1, one launch (start us, length us, event | category | flops | bytes accessed | tf_op | source)
XLA Modules:
  0.0 101.2 jit_solution(2273385153067073736)
XLA Ops:
  0.6 1.7 %shard_map.59 = bf16[16,32,512]{2,1,0:T(8,128)(2,1)} custom-call(bf16[32,1024]{1,0:T(8,128)(2,1)} %bitcast.9), custom_call_target="tpu_custom_call" | custom-call | tf_op jit(solution)/shard_map/pallas_call | solution.py:28
  2.4 0.0 copy-start
  2.4 10.0 %all-to-all-start = ((bf16[16,32,512]{2,1,0:T(8,128)(2,1)}), bf16[16,32,512]{2,1,0:T(8,128)(2,1)S(1)}, u32[]{:S(2)}, u32[]{:S(2)}) async-start(bf16[16,32,512]{2,1,0:T(8,128)(2,1)} %shard_map.59), calls=%async_computation | async-start | bytes 1048576 | tf_op jit(solution)/shard_map/all_to_all | solution.py:317
  12.4 0.0 copy-done
  12.4 2.8 %collective-permute-start.1 = (bf16[32,512]{1,0:T(8,128)(2,1)S(1)}, bf16[32,512]{1,0:T(8,128)(2,1)S(1)}, u32[]{:S(2)}, u32[]{:S(2)}) collective-permute-start(bf16[32,512]{1,0:T(8,128)(2,1)S(1)} %copy-done), channel_id=1, source_target_pairs={{0,1},{1,2},{2,3},{3,0},{4,5},{5,6},{6,7},{7,4},{8,9},{9,10},{10,1... | collective-permute-start | bytes 98312 | tf_op jit(solution)/shard_map/ppermute | solution.py:307
  15.2 0.0 collective-permute-start
  15.2 1.6 %collective-permute-start.2 = (bf16[32,512]{1,0:T(8,128)(2,1)S(1)}, bf16[32,512]{1,0:T(8,128)(2,1)S(1)}, u32[]{:S(2)}, u32[]{:S(2)}) collective-permute-start(bf16[32,512]{1,0:T(8,128)(2,1)S(1)} %copy-done), channel_id=1, source_target_pairs={{0,2},{1,3},{2,0},{3,1},{4,6},{5,7},{6,4},{7,5},{8,10},{9,11},{10,... | collective-permute-start | bytes 98312 | tf_op jit(solution)/shard_map/ppermute | solution.py:307
  16.8 0.0 collective-permute-done.1.refs_2_
  16.8 2.6 %collective-permute-done.refs_1_ = bf16[32,512]{1,0:T(8,128)(2,1)S(1)} collective-permute-done((bf16[32,512]{1,0:T(8,128)(2,1)S(1)}, bf16[32,512]{1,0:T(8,128)(2,1)S(1)}, u32[]{:S(2)}, u32[]{:S(2)}) %collective-permute-start) | collective-permute-done | bytes 32800 | tf_op jit(solution)/shard_map/ppermute | solution.py:307
  19.5 0.0 collective-permute-done.2.refs_3_
  19.5 2.8 %collective-permute-start.5 = (bf16[4,32,512]{2,1,0:T(8,128)(2,1)S(1)}, bf16[4,32,512]{2,1,0:T(8,128)(2,1)S(1)}, u32[]{:S(2)}, u32[]{:S(2)}) collective-permute-start(bf16[4,32,512]{2,1,0:T(8,128)(2,1)S(1)} %shard_map.58.g0), channel_id=1, source_target_pairs={{0,8},{1,9},{2,10},{3,11},{4,12},{5,13},{6,14},{7,15},{8,0},{9,1},... | collective-permute-start | bytes 393224 | tf_op jit(solution)/shard_map/ppermute | solution.py:307
  22.4 0.4 collective-permute-start.4
  22.8 2.3 %collective-permute-start.3 = (bf16[4,32,512]{2,1,0:T(8,128)(2,1)S(1)}, bf16[4,32,512]{2,1,0:T(8,128)(2,1)S(1)}, u32[]{:S(2)}, u32[]{:S(2)}) collective-permute-start(bf16[4,32,512]{2,1,0:T(8,128)(2,1)S(1)} %shard_map.58.g0), channel_id=1, source_target_pairs={{0,4},{1,5},{2,6},{3,7},{4,8},{5,9},{6,10},{7,11},{8,12},{9,13},{1... | collective-permute-start | bytes 393224 | tf_op jit(solution)/shard_map/ppermute | solution.py:307
  25.0 0.0 collective-permute-done.5.__3_.g3
  25.0 2.6 %collective-permute-done.4.__2_.g2 = bf16[4,32,512]{2,1,0:T(8,128)(2,1)S(1)} collective-permute-done((bf16[4,32,512]{2,1,0:T(8,128)(2,1)S(1)}, bf16[4,32,512]{2,1,0:T(8,128)(2,1)S(1)}, u32[]{:S(2)}, u32[]{:S(2)}) %collective-permute-start.4) | collective-permute-done | bytes 131104 | tf_op jit(solution)/shard_map/ppermute | solution.py:307
  27.7 0.0 collective-permute-done.3.__1_.g1
  27.7 2.0 %all-to-all-done = bf16[16,32,512]{2,1,0:T(8,128)(2,1)S(1)} async-done(((bf16[16,32,512]{2,1,0:T(8,128)(2,1)}), bf16[16,32,512]{2,1,0:T(8,128)(2,1)S(1)}, u32[]{:S(2)}, u32[]{:S(2)}) %all-to-all-start) | async-done | bytes 524320 | tf_op jit(solution)/shard_map/all_to_all | solution.py:317
  29.7 0.0 copy-start.1
  29.7 2.1 %collective-permute-start.6 = (bf16[512,512]{1,0:T(8,128)(2,1)S(1)}, bf16[512,512]{1,0:T(8,128)(2,1)S(1)}, u32[]{:S(2)}, u32[]{:S(2)}) collective-permute-start(bf16[512,512]{1,0:T(8,128)(2,1)S(1)} %shard_map.60.data_ref.refs_3_), channel_id=1, source_target_pairs={{0,16},{16,0},{32,48},{48,32},{64,80},{80,64},{96,112},{112,96},{1... | collective-permute-start | bytes 1572872 | tf_op jit(solution)/shard_map/ppermute | solution.py:324
  31.8 0.0 copy-done.1
  31.8 1.0 shard_map.61
  32.7 0.6 collective-permute-done.6.data_ref.refs_4_.more_ref
  33.3 0.5 shard_map.62.other_ref.refs_1_
  33.8 0.4 shard_map.63
  34.2 11.3 %all_to_all.25.refs_2_ = f32[16,4,128]{2,1,0:T(4,128)S(1)} all-to-all(f32[16,4,128]{2,1,0:T(4,128)S(1)} %shard_map.63), channel_id=1, replica_groups=mesh['row'=16,'col'=16] {'col'}, dimensions={0} | all-to-all | bytes 65536 | tf_op jit(solution)/shard_map/all_to_all | solution.py:342
  45.5 0.5 shard_map.64
  46.1 14.4 %all_to_all.26.refs_2_ = f32[16,8,128]{2,1,0:T(8,128)S(1)} all-to-all(f32[16,8,128]{2,1,0:T(8,128)S(1)} %shard_map.64), channel_id=1, replica_groups=mesh['row'=16,'col'=16] {'row'}, dimensions={0} | all-to-all | bytes 131072 | tf_op jit(solution)/shard_map/all_to_all | solution.py:349
  60.5 0.6 shard_map.65
  61.1 9.2 %all_to_all.27.refs_2_ = f32[16,4,128]{2,1,0:T(4,128)S(1)} all-to-all(f32[16,4,128]{2,1,0:T(4,128)S(1)} %shard_map.65), channel_id=1, replica_groups=mesh['row'=16,'col'=16] {'col'}, dimensions={0} | all-to-all | bytes 65536 | tf_op jit(solution)/shard_map/all_to_all | solution.py:342
  70.4 0.5 shard_map.66
  70.9 11.8 %all_to_all.28.refs_2_ = f32[16,8,128]{2,1,0:T(8,128)S(1)} all-to-all(f32[16,8,128]{2,1,0:T(8,128)S(1)} %shard_map.66), channel_id=1, replica_groups=mesh['row'=16,'col'=16] {'row'}, dimensions={0} | all-to-all | bytes 131072 | tf_op jit(solution)/shard_map/all_to_all | solution.py:349
  82.8 1.6 %shard_map.67 = (f32[8,128]{1,0:T(8,128)S(1)}, f32[8,128]{1,0:T(8,128)S(1)}, bf16[512,1024]{1,0:T(8,128)(2,1)S(1)}, bf16[512,1024]{1,0:T(8,128)(2,1)S(1)}, f32[5...) custom-call(f32[512,512]{1,0:T(8,128)S(1)} %get-tuple-element.19.refs_0_, ...), custom_call_target="tpu_custom_call" | custom-call | tf_op jit(solution)/shard_map/pallas_call | solution.py:28
  84.4 1.0 collective-permute-start.7
  85.4 0.6 collective-permute-start.8
  85.9 2.1 %collective-permute-start.9 = (f32[520,128]{1,0:T(8,128)S(1)}, f32[520,128]{1,0:T(8,128)S(1)}, u32[]{:S(2)}, u32[]{:S(2)}) collective-permute-start(f32[520,128]{1,0:T(8,128)S(1)} %get-tuple-element.27), channel_id=1, source_target_pairs={{0,3},{1,0},{2,1},{3,2},{4,7},{5,4},{6,5},{7,6},{8,11},{9,8},{10,9... | collective-permute-start | bytes 798728 | tf_op jit(solution)/shard_map/ppermute | solution.py:307
  88.0 0.8 shard_map.68.refs_0_
  88.9 2.7 %collective-permute-done.7.refs_1_ = f32[520,128]{1,0:T(8,128)S(1)} collective-permute-done((f32[520,128]{1,0:T(8,128)S(1)}, f32[520,128]{1,0:T(8,128)S(1)}, u32[]{:S(2)}, u32[]{:S(2)}) %collective-permute-start.7) | collective-permute-done | bytes 266272 | tf_op jit(solution)/shard_map/ppermute | solution.py:307
  91.6 2.8 %collective-permute-done.8.refs_2_ = f32[520,128]{1,0:T(8,128)S(1)} collective-permute-done((f32[520,128]{1,0:T(8,128)S(1)}, f32[520,128]{1,0:T(8,128)S(1)}, u32[]{:S(2)}, u32[]{:S(2)}) %collective-permute-start.8) | collective-permute-done | bytes 266272 | tf_op jit(solution)/shard_map/ppermute | solution.py:307
  94.4 0.0 collective-permute-done.9.refs_3_
  94.4 0.1 shard_map.69
  94.5 0.1 collective-permute-start.10
  94.6 2.1 %collective-permute-start.11 = (f32[136,128]{1,0:T(8,128)S(1)}, f32[136,128]{1,0:T(8,128)S(1)}, u32[]{:S(2)}, u32[]{:S(2)}) collective-permute-start(f32[136,128]{1,0:T(8,128)S(1)} %get-tuple-element.30), channel_id=1, source_target_pairs={{0,8},{1,9},{2,10},{3,11},{4,12},{5,13},{6,14},{7,15},{8,0},{9,1},... | collective-permute-start | bytes 208904 | tf_op jit(solution)/shard_map/ppermute | solution.py:307
  96.7 0.7 collective-permute-start.12
  97.3 0.6 copy.8
  97.9 2.1 %collective-permute-done.10.refs_1_ = f32[136,128]{1,0:T(8,128)S(1)} collective-permute-done((f32[136,128]{1,0:T(8,128)S(1)}, f32[136,128]{1,0:T(8,128)S(1)}, u32[]{:S(2)}, u32[]{:S(2)}) %collective-permute-start.10) | collective-permute-done | bytes 69664 | tf_op jit(solution)/shard_map/ppermute | solution.py:307
  100.0 0.0 collective-permute-done.11.refs_2_
  100.0 0.6 collective-permute-done.12.refs_3_
  100.6 0.7 shard_map.70
  (2 shorter events, 0.0 us)
Async XLA Ops:
  2.4 10.0 %copy-start = (bf16[32,512]{1,0:T(8,128)(2,1)S(1)}, bf16[32,512]{1,0:T(8,128)(2,1)}, u32[]{:S(2)}) copy-start(bf16[32,512]{1,0:T(8,128)(2,1)} %refs_0_.1) | copy-start | bytes 98308
  2.4 27.3 %all-to-all-start = ((bf16[16,32,512]{2,1,0:T(8,128)(2,1)}), bf16[16,32,512]{2,1,0:T(8,128)(2,1)S(1)}, u32[]{:S(2)}, u32[]{:S(2)}) async-start(bf16[16,32,512]{2,1,0:T(8,128)(2,1)} %shard_map.59), calls=%async_computation | async-start | bytes 1048576 | tf_op jit(solution)/shard_map/all_to_all | solution.py:317
  12.4 4.5 %collective-permute-start.1 = (bf16[32,512]{1,0:T(8,128)(2,1)S(1)}, bf16[32,512]{1,0:T(8,128)(2,1)S(1)}, u32[]{:S(2)}, u32[]{:S(2)}) collective-permute-start(bf16[32,512]{1,0:T(8,128)(2,1)S(1)} %copy-done), channel_id=1, source_target_pairs={{0,1},{1,2},{2,3},{3,0},{4,5},{5,6},{6,7},{7,4},{8,9},{9,10},{10,1... | collective-permute-start | bytes 98312 | tf_op jit(solution)/shard_map/ppermute | solution.py:307
  15.2 4.3 %collective-permute-start = (bf16[32,512]{1,0:T(8,128)(2,1)S(1)}, bf16[32,512]{1,0:T(8,128)(2,1)S(1)}, u32[]{:S(2)}, u32[]{:S(2)}) collective-permute-start(bf16[32,512]{1,0:T(8,128)(2,1)S(1)} %copy-done), channel_id=1, source_target_pairs={{0,3},{1,0},{2,1},{3,2},{4,7},{5,4},{6,5},{7,6},{8,11},{9,8},{10,9... | collective-permute-start | bytes 98312 | tf_op jit(solution)/shard_map/ppermute | solution.py:307
  15.2 4.3 %collective-permute-start.2 = (bf16[32,512]{1,0:T(8,128)(2,1)S(1)}, bf16[32,512]{1,0:T(8,128)(2,1)S(1)}, u32[]{:S(2)}, u32[]{:S(2)}) collective-permute-start(bf16[32,512]{1,0:T(8,128)(2,1)S(1)} %copy-done), channel_id=1, source_target_pairs={{0,2},{1,3},{2,0},{3,1},{4,6},{5,7},{6,4},{7,5},{8,10},{9,11},{10,... | collective-permute-start | bytes 98312 | tf_op jit(solution)/shard_map/ppermute | solution.py:307
  19.5 5.5 %collective-permute-start.5 = (bf16[4,32,512]{2,1,0:T(8,128)(2,1)S(1)}, bf16[4,32,512]{2,1,0:T(8,128)(2,1)S(1)}, u32[]{:S(2)}, u32[]{:S(2)}) collective-permute-start(bf16[4,32,512]{2,1,0:T(8,128)(2,1)S(1)} %shard_map.58.g0), channel_id=1, source_target_pairs={{0,8},{1,9},{2,10},{3,11},{4,12},{5,13},{6,14},{7,15},{8,0},{9,1},... | collective-permute-start | bytes 393224 | tf_op jit(solution)/shard_map/ppermute | solution.py:307
  22.4 5.3 %collective-permute-start.4 = (bf16[4,32,512]{2,1,0:T(8,128)(2,1)S(1)}, bf16[4,32,512]{2,1,0:T(8,128)(2,1)S(1)}, u32[]{:S(2)}, u32[]{:S(2)}) collective-permute-start(bf16[4,32,512]{2,1,0:T(8,128)(2,1)S(1)} %shard_map.58.g0), channel_id=1, source_target_pairs={{0,12},{1,13},{2,14},{3,15},{4,0},{5,1},{6,2},{7,3},{8,4},{9,5},{1... | collective-permute-start | bytes 393224 | tf_op jit(solution)/shard_map/ppermute | solution.py:307
  22.8 4.9 %collective-permute-start.3 = (bf16[4,32,512]{2,1,0:T(8,128)(2,1)S(1)}, bf16[4,32,512]{2,1,0:T(8,128)(2,1)S(1)}, u32[]{:S(2)}, u32[]{:S(2)}) collective-permute-start(bf16[4,32,512]{2,1,0:T(8,128)(2,1)S(1)} %shard_map.58.g0), channel_id=1, source_target_pairs={{0,4},{1,5},{2,6},{3,7},{4,8},{5,9},{6,10},{7,11},{8,12},{9,13},{1... | collective-permute-start | bytes 393224 | tf_op jit(solution)/shard_map/ppermute | solution.py:307
  29.7 2.1 %copy-start.1 = (f32[1024]{0:T(1024)S(1)}, f32[1024]{0:T(1024)}, u32[]{:S(2)}) copy-start(f32[1024]{0:T(1024)} %param.5) | copy-start | bytes 12292
  29.7 3.6 %collective-permute-start.6 = (bf16[512,512]{1,0:T(8,128)(2,1)S(1)}, bf16[512,512]{1,0:T(8,128)(2,1)S(1)}, u32[]{:S(2)}, u32[]{:S(2)}) collective-permute-start(bf16[512,512]{1,0:T(8,128)(2,1)S(1)} %shard_map.60.data_ref.refs_3_), channel_id=1, source_target_pairs={{0,16},{16,0},{32,48},{48,32},{64,80},{80,64},{96,112},{112,96},{1... | collective-permute-start | bytes 1572872 | tf_op jit(solution)/shard_map/ppermute | solution.py:324
  84.4 7.2 %collective-permute-start.7 = (f32[520,128]{1,0:T(8,128)S(1)}, f32[520,128]{1,0:T(8,128)S(1)}, u32[]{:S(2)}, u32[]{:S(2)}) collective-permute-start(f32[520,128]{1,0:T(8,128)S(1)} %get-tuple-element.25), channel_id=1, source_target_pairs={{0,2},{1,3},{2,0},{3,1},{4,6},{5,7},{6,4},{7,5},{8,10},{9,11},{10,... | collective-permute-start | bytes 798728 | tf_op jit(solution)/shard_map/ppermute | solution.py:307
  85.4 9.0 %collective-permute-start.8 = (f32[520,128]{1,0:T(8,128)S(1)}, f32[520,128]{1,0:T(8,128)S(1)}, u32[]{:S(2)}, u32[]{:S(2)}) collective-permute-start(f32[520,128]{1,0:T(8,128)S(1)} %get-tuple-element.26), channel_id=1, source_target_pairs={{0,1},{1,2},{2,3},{3,0},{4,5},{5,6},{6,7},{7,4},{8,9},{9,10},{10,1... | collective-permute-start | bytes 798728 | tf_op jit(solution)/shard_map/ppermute | solution.py:307
  85.9 8.5 %collective-permute-start.9 = (f32[520,128]{1,0:T(8,128)S(1)}, f32[520,128]{1,0:T(8,128)S(1)}, u32[]{:S(2)}, u32[]{:S(2)}) collective-permute-start(f32[520,128]{1,0:T(8,128)S(1)} %get-tuple-element.27), channel_id=1, source_target_pairs={{0,3},{1,0},{2,1},{3,2},{4,7},{5,4},{6,5},{7,6},{8,11},{9,8},{10,9... | collective-permute-start | bytes 798728 | tf_op jit(solution)/shard_map/ppermute | solution.py:307
  94.5 5.5 %collective-permute-start.10 = (f32[136,128]{1,0:T(8,128)S(1)}, f32[136,128]{1,0:T(8,128)S(1)}, u32[]{:S(2)}, u32[]{:S(2)}) collective-permute-start(f32[136,128]{1,0:T(8,128)S(1)} %get-tuple-element.29), channel_id=1, source_target_pairs={{0,4},{1,5},{2,6},{3,7},{4,8},{5,9},{6,10},{7,11},{8,12},{9,13},{1... | collective-permute-start | bytes 208904 | tf_op jit(solution)/shard_map/ppermute | solution.py:307
  94.6 5.4 %collective-permute-start.11 = (f32[136,128]{1,0:T(8,128)S(1)}, f32[136,128]{1,0:T(8,128)S(1)}, u32[]{:S(2)}, u32[]{:S(2)}) collective-permute-start(f32[136,128]{1,0:T(8,128)S(1)} %get-tuple-element.30), channel_id=1, source_target_pairs={{0,8},{1,9},{2,10},{3,11},{4,12},{5,13},{6,14},{7,15},{8,0},{9,1},... | collective-permute-start | bytes 208904 | tf_op jit(solution)/shard_map/ppermute | solution.py:307
  96.7 3.9 %collective-permute-start.12 = (f32[136,128]{1,0:T(8,128)S(1)}, f32[136,128]{1,0:T(8,128)S(1)}, u32[]{:S(2)}, u32[]{:S(2)}) collective-permute-start(f32[136,128]{1,0:T(8,128)S(1)} %get-tuple-element.31), channel_id=1, source_target_pairs={{0,12},{1,13},{2,14},{3,15},{4,0},{5,1},{6,2},{7,3},{8,4},{9,5},{1... | collective-permute-start | bytes 208904 | tf_op jit(solution)/shard_map/ppermute | solution.py:307
